TPU v7x, 256 devices: a whole 4x4x8 slice. The times are simulated.
256 devices in a mesh: cells: 64 (over y_lo, x, z), tracers: 4 (over y_hi, core).
Axes of the slice: x: 4, y: 4 (y_hi: 2, y_lo: 2; y = y_hi * 2 + y_lo), z: 8, core: 2. Of those that a mesh axis runs over, the one named last changes fastest.
Arguments:
- tracers: float32 [256, 6, 384, 128], P('tracers', None, 'cells'), may hold values from 0 to 18, as said below
- hour_fields: float32 [4, 10, 6, 384, 128], P('tracers', None, None, 'cells'), may hold values from -1 to 2, as said below
- reader_table: int32 [64], P('cells'), may hold values from 0 to 3
Outputs:
- transported: float32 [256, 6, 384, 128], P('tracers', None, 'cells')
Inputs may be any that keep to these rules, and one draw needn't show every extreme that they name: `reader_table`: tracers index of the device whose copy of hour_fields is valid for this block. `tracers`: positive mixing ratios. `hour_fields`: rows 0 and 1 are Courant numbers of magnitude below 1, rows 2 and 3 positive pressure thicknesses, rows from 4 on the given inverse of each column's implicit diffusion matrix.
All inputs are finite; a program needn't handle non-finite values.
Results may differ from a plain program's by a relative error of at most 0.0003.
Values sent between devices are 32-bit elements; how exact they have to be, the bound alone decides.
No kernel may reach another device: no remote copies, remote signals or barrier semaphores. Data moves between devices by JAX's collectives and lax.ppermute only.
A program may use at most 64 MiB of HBM per device.

v0:
```python
import jax
import jax.numpy as jnp
from jax import lax
from jax.sharding import PartitionSpec as P


def broadcast(block, axis, holder):
    block = jnp.where(lax.axis_index(axis) == holder, block, jnp.zeros_like(block))
    return lax.psum(block, axis)


def padded(value, sides, width):
    for axis, dim in sides:
        peers, length = (lax.axis_size(axis), value.shape[dim])
        up = [(i, (i + 1) % peers) for i in range(peers)]
        down = [(j, i) for i, j in up]
        last = lax.slice_in_dim(value, length - width, length, axis=dim)
        first = lax.slice_in_dim(value, 0, width, axis=dim)
        before = lax.ppermute(last, axis, up)
        after = lax.ppermute(first, axis, down)
        value = jnp.concatenate([before, value, after], axis=dim)
    return value


def window(array, start, count, along):
    return lax.slice_in_dim(array, start, start + count, axis=array.ndim + along)


def ppm_sweep(extended, courant, along):
    inner = extended.shape[extended.ndim + along] - 6
    edge_val = 7.0 / 12.0 * (
        window(extended, 1, inner + 3, along) + window(extended, 2, inner + 3, along)
    ) - 1.0 / 12.0 * (window(extended, 0, inner + 3, along) + window(extended, 3, inner + 3, along))
    left_edge = window(edge_val, 0, inner + 2, along)
    right_edge = window(edge_val, 1, inner + 2, along)
    centre = window(extended, 2, inner + 2, along)
    slope_part = right_edge - left_edge
    curvature = 6.0 * (centre - 0.5 * (left_edge + right_edge))
    upwind_pos = window(right_edge, 0, inner + 1, along) - 0.5 * courant * (
        window(slope_part, 0, inner + 1, along)
        - (1.0 - 2.0 / 3.0 * courant) * window(curvature, 0, inner + 1, along)
    )
    backward = -courant
    upwind_neg = window(left_edge, 1, inner + 1, along) + 0.5 * backward * (
        window(slope_part, 1, inner + 1, along)
        + (1.0 - 2.0 / 3.0 * backward) * window(curvature, 1, inner + 1, along)
    )
    fluxes = courant * jnp.where(courant >= 0, upwind_pos, upwind_neg)
    return window(extended, 3, inner, along) - (
        window(fluxes, 1, inner, along) - window(fluxes, 0, inner, along)
    )


def sweep_walls(field, courant_y):
    extended = jnp.concatenate([field[..., :1]] * 3 + [field] + [field[..., -1:]] * 3, axis=-1)
    zero_face = jnp.zeros_like(courant_y[..., :1])
    faces = jnp.concatenate([zero_face, courant_y[..., 1:], zero_face], axis=-1)
    return ppm_sweep(extended, faces, -1)


def per_device(tracers, hour_fields, reader_table):
    width = tracers.shape[2]
    fields = broadcast(hour_fields[0], "tracers", reader_table[0])
    courant_x = fields[0]
    courant_y = fields[1]
    dp_old = fields[2]
    dp_new = fields[3]
    inverse = fields[4:]
    mass_part = jnp.sum(tracers * dp_old[None], axis=(1, 2, 3))
    before = lax.psum(mass_part, "cells")
    stacked = jnp.concatenate([tracers, courant_x[None]], axis=0)
    widened = padded(stacked, (("cells", 2),), 3)
    x_faces = 0.5 * widened[-1][:, 3 : width + 4]
    first = ppm_sweep(widened[:-1], x_faces, -2)
    second = sweep_walls(first, courant_y)
    rimmed = padded(second, (("cells", 2),), 3)
    third = ppm_sweep(rimmed, x_faces, -2)
    diffused = jnp.einsum("lmxy,tmxy->tlxy", inverse, third, precision=lax.Precision.HIGHEST)
    after = lax.psum(jnp.sum(diffused * dp_new[None], axis=(1, 2, 3)), "cells")
    return diffused * (before / after)[:, None, None, None]


def solution(mesh):
    placed = (
        P("tracers", None, "cells", None),
        P("tracers", None, None, "cells", None),
        P("cells"),
    )
    return jax.shard_map(
        per_device,
        mesh=mesh,
        in_specs=placed,
        out_specs=P("tracers", None, "cells", None),
        check_vma=False,
    )
```

profile of v0, /device:TPU:16, one launch (start us, length us, event | category | flops | bytes accessed | tf_op | source)
XLA Modules:
  0.0 411.4 jit_solution(12450782397732067464)
XLA Ops:
  7.2 5.1 %copy.48 = f32[1,10,6,6,128]{2,1,4,3,0:T(8,128)} copy(f32[1,10,6,6,128]{4,0,3,2,1:T(1,128)} %param.4) | data formatting | bytes 368640 | tf_op args[1]
  12.3 6.1 %select_bitcast_fusion = f32[10,6,6,128]{1,0,3,2:T(8,128)} fusion(f32[1,10,6,6,128]{2,1,4,3,0:T(8,128)} %copy.48, pred[]{:T(512)S(6)} %eq.3), kind=kLoop, calls=%fused_computation | loop fusion | flops 46080 | bytes 368641 | tf_op jit(solution)/shard_map/jit(_where)/select_n | solution.py:8
  18.4 1.2 copy-done
  19.6 0.7 copy.57
  20.3 129.9 %all-reduce.3.cloned.1.call-done = f32[10,6,6,128]{1,0,3,2:T(8,128)} async-done(((f32[10,6,6,128]{1,0,3,2:T(8,128)}), f32[10,6,6,128]{1,0,3,2:T(8,128)}) %all-reduce.3.cloned.1.call-update) | async-done | bytes 184336 | tf_op jit(solution)/shard_map/psum | solution.py:9
  150.2 7.3 %fusion.48 = (f32[1,6,6,128]{1,0,3,2:T(1,128)S(1)}, f32[1,6,6,128]{1,0,3,2:T(1,128)S(1)}, f32[1,6,6,128]{1,0,3,2:T(1,128)}, f32[1,6,6,128]{1,0,3,2:T(1,128)}) fusion(f32[10,6,6,128]{1,0,3,2:T(8,128)} %all-reduce.3.cloned.1.call-done), kind=kLoop, calls=%fused_computation.99 | loop fusion | bytes 147456 | tf_op jit(solution)/shard_map/slice | solution.py:67
  157.5 1.8 copy.50
  159.3 1.1 fusion.47
  160.4 1.0 copy.52
  161.4 7.7 %collective-permute-start.1 = (f32[65,6,3,128]{3,0,2,1:T(8,128)}, f32[65,6,3,128]{3,0,2,1:T(8,128)}, u32[]{:S(2)}, u32[]{:S(2)}) collective-permute-start(f32[65,6,3,128]{3,0,2,1:T(8,128)} %copy.52), channel_id=1, source_target_pairs={{4,0},{8,4},{12,8},{16,12},{20,16},{24,20},{28,24},{32,28},{36,32}... | collective-permute-start | bytes 1797128 | tf_op jit(solution)/shard_map/ppermute | solution.py:20
  169.1 0.9 copy.51
  170.0 0.8 slice.247
  170.8 1.8 copy.58
  172.6 0.8 broadcast_compare_fusion
  173.4 0.8 pad_maximum_fusion.14
  174.3 9.8 %collective-permute-done.1 = f32[65,6,3,128]{3,0,2,1:T(8,128)} collective-permute-done((f32[65,6,3,128]{3,0,2,1:T(8,128)}, f32[65,6,3,128]{3,0,2,1:T(8,128)}, u32[]{:S(2)}, u32[]{:S(2)}) %collective-permute-start.1) | collective-permute-done | bytes 599072 | tf_op jit(solution)/shard_map/ppermute | solution.py:20
  184.0 1.3 copy.54
  185.3 6.1 %collective-permute-done = f32[65,6,3,128]{3,0,2,1:T(8,128)} collective-permute-done((f32[65,6,3,128]{3,0,2,1:T(8,128)}, f32[65,6,3,128]{3,0,2,1:T(8,128)}, u32[]{:S(2)}, u32[]{:S(2)}) %collective-permute-start) | collective-permute-done | bytes 599072 | tf_op jit(solution)/shard_map/ppermute | solution.py:19
  191.4 1.3 copy.53
  192.8 0.7 pad_maximum_fusion.7
  193.6 2.0 fusion.19
  195.6 0.5 slice_subtract_fusion.7
  196.2 0.8 fusion.41
  197.0 0.9 fusion.36
  197.8 0.5 fusion.50
  198.3 5.4 %fusion.2 = f32[64,6,6,131]{3,2,1,0:T(8,128)S(1)} fusion(f32[64,6,6,1]{3,2,1,0:T(8,128)S(1)} %get-tuple-element.22, f32[64,6,6,1]{3,2,1,0:T(8,128)S(1)} %get-tuple-element.21, f32[64,6,6,128]{3,2,1,0:T(8,128)S(1)} %fusion.36), kind=kLoop, calls=%fused_computation.11 | loop fusion | flops 4829184 | bytes 2405376 | tf_op jit(solution)/shard_map/sub | solution.py:31
  203.8 2.1 slice_subtract_fusion
  205.9 2.6 fusion.13
  208.5 0.5 fusion.35
  209.0 0.3 fusion.49
  209.4 0.7 collective-permute-start.3
  210.2 0.9 copy.59
  211.1 1.4 collective-permute-start.2
  212.5 0.8 copy.68
  213.4 10.5 %collective-permute-done.3 = f32[64,6,3,128]{3,0,2,1:T(8,128)S(1)} collective-permute-done((f32[64,6,3,128]{3,0,2,1:T(8,128)S(1)}, f32[64,6,3,128]{3,0,2,1:T(8,128)S(1)}, u32[]{:S(2)}, u32[]{:S(2)}) %collective-permute-start.3) | collective-permute-done | bytes 589856 | tf_op jit(solution)/shard_map/ppermute | solution.py:20
  224.0 0.4 copy.62
  224.4 5.7 %collective-permute-done.2 = f32[64,6,3,128]{3,0,2,1:T(8,128)} collective-permute-done((f32[64,6,3,128]{3,0,2,1:T(8,128)}, f32[64,6,3,128]{3,0,2,1:T(8,128)}, u32[]{:S(2)}, u32[]{:S(2)}) %collective-permute-start.2) | collective-permute-done | bytes 589856 | tf_op jit(solution)/shard_map/ppermute | solution.py:19
  230.1 1.5 copy.61
  231.6 0.7 pad_maximum_fusion.12
  232.3 1.7 fusion.8
  234.1 0.5 slice_subtract_fusion.6
  234.8 0.8 fusion.30
  235.7 1.4 fusion.25
  237.1 2.5 copy.65
  239.5 8.7 %fusion.5 = f32[6,128,64,6]{2,3,1,0:T(8,128)} fusion(f32[64,6,6,128]{0,1,3,2:T(8,128)S(1)} %copy.65, f32[10,6,6,128]{1,0,3,2:T(8,128)} %all-reduce.3.cloned.1.call-done), kind=kOutput, calls=%fused_computation.14 | convolution fusion | flops 21233664 | bytes 5505024 | tf_op jit(solution)/shard_map/lmxy,tmxy->tlxy/dot_general | solution.py:78
  248.3 2.3 copy.66
  250.9 152.3 %all-reduce = (f32[64]{0:T(128)S(1)}, f32[64]{0:T(128)S(1)}) all-reduce(f32[64]{0:T(128)S(1)} %get-tuple-element.34, f32[64]{0:T(128)S(1)} %get-tuple-element.33), channel_id=1, replica_groups=mesh['cells'=64,'tracers'=4] {'cells'}, use_global_device_ids=true, to_apply=%region_2.3 | all-reduce | flops 128 | bytes 1024 | tf_op jit(solution)/shard_map/psum | solution.py:70
  403.3 1.2 bitcast_multiply_fusion
  (40 shorter events, 1.0 us)
Async XLA Ops:
  6.5 143.7 %all-reduce.3.cloned.1.call-start = ((), (), s32[]{:S(2)}) async-start(), calls=%async_computation | async-start | bytes 12582912 | tf_op jit(solution)/shard_map/psum | solution.py:9
  18.4 1.3 copy-start
  159.3 10.7 %copy-start.2 = (f32[1,6,6,128]{1,0,3,2:T(1,128)S(1)}, f32[1,6,6,128]{1,0,3,2:T(1,128)}, u32[]{:S(2)}) copy-start(f32[1,6,6,128]{1,0,3,2:T(1,128)} %get-tuple-element.9) | copy-start | bytes 55300
  161.4 22.6 %collective-permute-start.1 = (f32[65,6,3,128]{3,0,2,1:T(8,128)}, f32[65,6,3,128]{3,0,2,1:T(8,128)}, u32[]{:S(2)}, u32[]{:S(2)}) collective-permute-start(f32[65,6,3,128]{3,0,2,1:T(8,128)} %copy.52), channel_id=1, source_target_pairs={{4,0},{8,4},{12,8},{16,12},{20,16},{24,20},{28,24},{32,28},{36,32}... | collective-permute-start | bytes 1797128 | tf_op jit(solution)/shard_map/ppermute | solution.py:20
  170.0 21.4 %collective-permute-start = (f32[65,6,3,128]{3,0,2,1:T(8,128)}, f32[65,6,3,128]{3,0,2,1:T(8,128)}, u32[]{:S(2)}, u32[]{:S(2)}) collective-permute-start(f32[65,6,3,128]{3,0,2,1:T(8,128)} %copy.51), channel_id=1, source_target_pairs={{0,4},{4,8},{8,12},{12,16},{16,20},{20,24},{24,28},{28,32},{32,36}... | collective-permute-start | bytes 1797128 | tf_op jit(solution)/shard_map/ppermute | solution.py:19
  172.6 20.1 %copy-start.3 = (f32[1,6,6,128]{3,2,1,0:T(8,128)S(1)}, f32[1,6,6,128]{3,2,1,0:T(8,128)}, u32[]{:S(2)}) copy-start(f32[1,6,6,128]{3,2,1,0:T(8,128)} %copy.50) | copy-start | bytes 55300
  192.8 3.3 copy-start.4
  192.8 3.3 copy-start.6
  192.8 3.3 copy-start.8
  192.8 3.3 copy-start.10
  192.8 3.3 copy-start.12
  209.4 14.5 %collective-permute-start.3 = (f32[64,6,3,128]{3,0,2,1:T(8,128)S(1)}, f32[64,6,3,128]{3,0,2,1:T(8,128)S(1)}, u32[]{:S(2)}, u32[]{:S(2)}) collective-permute-start(f32[64,6,3,128]{3,0,2,1:T(8,128)S(1)} %copy.60), channel_id=1, source_target_pairs={{4,0},{8,4},{12,8},{16,12},{20,16},{24,20},{28,24},{32,28},{36,32}... | collective-permute-start | bytes 1769480 | tf_op jit(solution)/shard_map/ppermute | solution.py:20
  211.1 19.0 %collective-permute-start.2 = (f32[64,6,3,128]{3,0,2,1:T(8,128)}, f32[64,6,3,128]{3,0,2,1:T(8,128)}, u32[]{:S(2)}, u32[]{:S(2)}) collective-permute-start(f32[64,6,3,128]{3,0,2,1:T(8,128)} %copy.59), channel_id=1, source_target_pairs={{0,4},{4,8},{8,12},{12,16},{16,20},{20,24},{24,28},{28,32},{32,36}... | collective-permute-start | bytes 1769480 | tf_op jit(solution)/shard_map/ppermute | solution.py:19
  234.0 0.7 copy-start.5
  234.0 0.7 copy-start.7
  234.0 0.8 copy-start.9
  234.1 0.8 copy-start.11
  234.1 0.8 copy-start.13
  248.3 2.4 copy-start.1
  248.3 2.4 copy-start.14
Sparse Core Ops, SparseCore 0:
  18.5 131.6 all-reduce.2
where the time goes:
time: 413 us; the launch traced here: 411 us
  waiting for transfers between devices  162 us (39%)
  blocking collectives  152 us (37%)
  local copies, waits for them, and re-layouts  33 us (8%)
  other arithmetic  31.1 us (8%)
  between operations  14.4 us (3%)
  starting transfers between devices  9.78 us (2%)
  matrix products  8.75 us (2%)
    psum x1, blocking collectives, per_device(): before = lax.psum(mass_part, 'cells')  152 us
    psum x1, waiting for transfers between devices, broadcast(): return lax.psum(block, axis)  130 us
    ppermute x2, waiting for transfers between devices, padded(): after = lax.ppermute(first, axis, down)  20.3 us
    ppermute x2, waiting for transfers between devices, padded(): before = lax.ppermute(last, axis, up)  11.8 us
    sub x3, other arithmetic, ppm_sweep(): 7.0 / 12.0  9.21 us
    dot_general x1, matrix products, per_device(): jnp.einsum('lmxy,tmxy->tlxy', inverse, third, precision=lax.Precision.HIG...  8.75 us
    ppermute x2, starting transfers between devices, padded(): after = lax.ppermute(first, axis, down)  8.39 us
  transfers between devices with their start and end apart: 5, of which 5 were waited for; matrix products, arithmetic and copies ran while one was open for 2% of the time, Pallas kernels for 0%

commit v1 on v0

v1 whole, which is shorter than its diff:
```python
import functools

import jax
import jax.numpy as jnp
from jax import lax
from jax.experimental import pallas as pl
from jax.experimental.pallas import tpu as pltpu
from jax.sharding import PartitionSpec as P

LEV, CX, NY = 6, 6, 128
ROWS = LEV * CX
NF = 10
HALO = 3
WIDE = CX + 2 * HALO
F32 = jnp.float32
VMEM_LIMIT = 48 * 1024 * 1024


def face_weights(c):
    a = jnp.abs(c)
    up = c >= 0
    zero = jnp.zeros_like(c)
    edge = c * (1.0 - a) * (1.0 - a)
    far = -c * a * (1.0 - a)
    mid = c * a * (3.0 - 2.0 * a)
    far_p, far_n = jnp.where(up, far, zero), jnp.where(up, zero, far)
    mid_p, mid_n = jnp.where(up, mid, zero), jnp.where(up, zero, mid)
    s, b = 1.0 / 12.0, 7.0 / 12.0
    return [
        -s * far_p,
        b * far_p - s * edge,
        b * (edge + far_p) - s * far_n + mid_p,
        b * (edge + far_n) - s * far_p + mid_n,
        b * far_n - s * edge,
        -s * far_n,
    ]


def cell_weights(west, east):
    out = []
    for k in range(-3, 4):
        total = None
        if k <= 2:
            total = west[k + 3]
        if k >= -2:
            total = -east[k + 2] if total is None else total - east[k + 2]
        out.append(total + 1.0 if k == 0 else total)
    return out


def wall_weights(c):
    lane = lax.broadcasted_iota(jnp.int32, c.shape, 1)
    last = NY - 1
    c = jnp.where(lane == 0, 0.0, c)
    west = face_weights(c)
    east = [pltpu.roll(a, NY - 1, 1) for a in west]
    b = cell_weights(west, east)
    zero = jnp.zeros_like(c)
    m1, m2, m3 = b[2], b[1], b[0]
    p1, p2, p3 = b[4], b[5], b[6]
    low, high = m2 + m3, p2 + p3
    return [
        jnp.where(lane <= 2, zero, m3),
        jnp.where(lane <= 1, zero, jnp.where(lane == 2, low, m2)),
        jnp.where(lane == 0, zero, jnp.where(lane == 1, m1 + low, m1)),
        b[3] + jnp.where(lane == 0, m1 + low, zero) + jnp.where(lane == last, p1 + high, zero),
        jnp.where(lane == last, zero, jnp.where(lane == last - 1, p1 + high, p1)),
        jnp.where(lane >= last - 1, zero, jnp.where(lane == last - 2, high, p2)),
        jnp.where(lane >= last - 2, zero, p3),
    ]


def merge_kernel(flag, own, other, fields, message):
    take = flag[0] == 1
    fields[...] = jnp.where(take, own[...], other[...])
    for x in range(CX):
        for f in range(2):
            message[pl.ds(f * ROWS + x * LEV, LEV), :] = fields[pl.ds(f * ROWS + x, LEV, stride=CX), :]
        total = None
        for l in range(LEV):
            thickness = fields[pl.ds(3 * ROWS + l * CX + x, 1), :]
            row = thickness * fields[pl.ds((4 + l) * ROWS + x, LEV, stride=CX), :]
            total = row if total is None else total + row
        message[pl.ds(2 * ROWS + x * LEV, LEV), :] = total


def weights_kernel(flag, own, first, second, fields, tracers, wx, wy, masses):
    left_first = flag[0] == 1

    def column(f, x):
        rows = pl.ds(f * ROWS + (x % CX) * LEV, LEV)
        if 0 <= x < CX:
            return own[rows, :]
        a, b = first[rows, :], second[rows, :]
        return jnp.where(left_first, a, b) if x < 0 else jnp.where(left_first, b, a)

    w = {x: column(2, x) for x in range(-6, 12)}
    face = {x: face_weights(0.5 * column(0, x)) for x in range(-5, 12)}
    stride = WIDE * 8

    def adjoint_x(v, lo, hi):
        jump = {f: v[f] - v[f - 1] for f in range(lo - 2, hi + 3)}
        out = {}
        for j in range(lo, hi):
            total = v[j]
            for k in range(-3, 3):
                total = total + face[j - k][k + 3] * jump[j - k]
            out[j] = total
        return out

    v = adjoint_x(w, -HALO, CX + HALO)
    for x in range(-HALO, CX + HALO):
        for k, b in enumerate(cell_weights(face[x], face[x + 1])):
            wx[pl.ds((x + HALO) * 8 + k, LEV, stride=stride), :] = b
        b = wall_weights(column(1, x))
        total = None
        for k in range(7):
            wy[pl.ds((x + HALO) * 8 + k, LEV, stride=stride), :] = b[k]
            part = b[k] * v[x]
            if k != 3:
                part = pltpu.roll(part, (k - 3) % NY, 1)
            total = part if total is None else total + part
        v[x] = total
    v = adjoint_x(v, 0, CX)

    before = after = None
    for l in range(LEV):
        for x in range(CX):
            q = tracers[l, x]
            b = q * fields[pl.ds(2 * ROWS + l * CX + x, 1), :]
            a = q * v[x][l : l + 1, :]
            before = b if before is None else before + b
            after = a if after is None else after + a
    both = jnp.concatenate([before, after], axis=0)
    sums = lax.dot_general(
        jnp.ones((8, NY), F32), both, (((1,), (1,)), ((), ())), precision=lax.Precision.HIGHEST, preferred_element_type=F32
    )
    for i in range(masses.shape[0] // 8):
        masses[pl.ds(8 * i, 8), :] = sums


def sweep_kernel(flag, tracers, first, second, wx, wy, fields, received, out, wide, middle, third, sems):
    count = tracers.shape[2]
    left_first = flag[0]
    first_at = (1 - left_first) * 2 * CX
    second_at = left_first * 2 * CX

    def copies(l):
        return [
            pltpu.make_async_copy(tracers.at[l], wide.at[l, pl.ds(CX, CX)], sems.at[l, 0]),
            pltpu.make_async_copy(first.at[l], wide.at[l, pl.ds(first_at, CX)], sems.at[l, 1]),
            pltpu.make_async_copy(second.at[l], wide.at[l, pl.ds(second_at, CX)], sems.at[l, 2]),
        ]

    for l in range(LEV):
        for copy in copies(l):
            copy.start()

    total = jnp.sum(received[...], axis=0, keepdims=True)
    ratio = total / pltpu.roll(jnp.broadcast_to(total, (8, NY)), NY // 2, 1)[:1]
    lane = lax.broadcasted_iota(jnp.int32, (count, NY), 1)
    row = lax.broadcasted_iota(jnp.int32, (count, NY), 0)
    scale = jnp.sum(jnp.where(lane == row, jnp.broadcast_to(ratio, (count, NY)), 0.0), axis=1, keepdims=True)

    block = 32

    def level(l, carry):
        for copy in copies(l):
            copy.wait()
        for t in range(0, count, block):
            ts = pl.ds(t, block)
            for x in range(WIDE):
                value = None
                for k in range(7):
                    part = wx[l, x, pl.ds(k, 1), :] * wide[l, x + k, ts, :]
                    value = part if value is None else value + part
                moved = None
                for k in range(7):
                    q = value if k == 3 else pltpu.roll(value, (3 - k) % NY, 1)
                    part = wy[l, x, pl.ds(k, 1), :] * q
                    moved = part if moved is None else moved + part
                middle[x, ts, :] = moved
            for x in range(CX):
                value = None
                for k in range(7):
                    part = wx[l, x + HALO, pl.ds(k, 1), :] * middle[x + k, ts, :]
                    value = part if value is None else value + part
                third[l, x, ts, :] = value
        return carry

    lax.fori_loop(0, LEV, level, 0)
    for x in range(CX):
        for t in range(0, count, block):
            ts = pl.ds(t, block)
            levels = [third[m, x, ts, :] for m in range(LEV)]
            factor = scale[t : t + block]
            for l in range(LEV):
                value = None
                for m in range(LEV):
                    part = fields[pl.ds((4 + l) * ROWS + m * CX + x, 1), :] * levels[m]
                    value = part if value is None else value + part
                out[l, x, ts, :] = value * factor


SMEM = pl.BlockSpec(memory_space=pltpu.SMEM)
VMEM = pl.BlockSpec(memory_space=pltpu.VMEM)
ANY = pl.BlockSpec(memory_space=pl.ANY)


def call(kernel, ins, outs, scratch=(), flops=0):
    many = isinstance(outs, list)
    shapes = [jax.ShapeDtypeStruct(s, F32) for s in outs] if many else jax.ShapeDtypeStruct(outs, F32)
    return pl.pallas_call(
        kernel,
        out_shape=shapes,
        in_specs=ins,
        out_specs=[VMEM] * len(outs) if many else VMEM,
        scratch_shapes=list(scratch),
        compiler_params=pltpu.CompilerParams(vmem_limit_bytes=VMEM_LIMIT),
    )


def swap(value, axis, partner):
    n = lax.axis_size(axis)
    return lax.ppermute(value, axis, [(i, partner(i, n)) for i in range(n)])


def even_pairs(i, n):
    return i ^ 1


def odd_pairs(i, n):
    return (i + 1) % n if i % 2 else (i - 1) % n


def per_device(tracers, hour_fields, reader_table):
    cells, mine = lax.axis_index("cells"), lax.axis_index("tracers")
    n = lax.axis_size("cells")
    reader = reader_table[0]
    odd = (cells % 2).astype(jnp.int32)[None]
    state = jnp.transpose(tracers, (1, 2, 0, 3))
    count = state.shape[2]
    raw = hour_fields.reshape(NF * ROWS, NY)

    far = swap(raw, "tracers", lambda i, n: i ^ 2)
    half = jnp.where(reader // 2 == mine // 2, raw, far)
    near = swap(half, "tracers", lambda i, n: i ^ 1)
    same = (reader % 2 == mine % 2).astype(jnp.int32)[None]
    fields, message = call(merge_kernel, [SMEM, VMEM, VMEM], [(NF * ROWS, NY), (3 * ROWS, NY)])(same, half, near)

    m1 = swap(message, "cells", even_pairs)
    m2 = swap(message, "cells", odd_pairs)
    h1 = swap(state, "cells", even_pairs)
    h2 = swap(state, "cells", odd_pairs)

    wx, wy, masses = call(
        weights_kernel,
        [SMEM, VMEM, VMEM, VMEM, VMEM, VMEM],
        [(LEV * WIDE * 8, NY), (LEV * WIDE * 8, NY), (n, 2 * count)],
    )(odd, message, m1, m2, fields, state)
    received = lax.all_to_all(masses, "cells", 0, 0, tiled=True)
    wx, wy = wx.reshape(LEV, WIDE, 8, NY), wy.reshape(LEV, WIDE, 8, NY)
    out = call(
        sweep_kernel,
        [SMEM, ANY, ANY, ANY, VMEM, VMEM, VMEM, VMEM],
        (LEV, CX, count, NY),
        [
            pltpu.VMEM((LEV, 3 * CX, count, NY), F32),
            pltpu.VMEM((WIDE, count, NY), F32),
            pltpu.VMEM((LEV, CX, count, NY), F32),
            pltpu.SemaphoreType.DMA((LEV, 3)),
        ],
    )(odd, state, h1, h2, wx, wy, fields, received)
    return jnp.transpose(out, (2, 0, 1, 3))


def solution(mesh):
    placed = (
        P("tracers", None, "cells", None),
        P("tracers", None, None, "cells", None),
        P("cells"),
    )
    return jax.shard_map(
        per_device,
        mesh=mesh,
        in_specs=placed,
        out_specs=P("tracers", None, "cells", None),
        check_vma=False,
    )
```

time: 413 us -> 79.6 us (0.19)
  blocking collectives: 152 us -> 16.8 us
  waiting for transfers between devices: 162 us -> 33.4 us
  local copies, waits for them, and re-layouts: 33 us -> 1.27 us
  other arithmetic: 31.1 us -> 0.94 us
  between operations: 14.4 us -> 0.72 us
  Pallas kernels: 0 us -> 11.4 us
  matrix products: 8.75 us -> 0 us
  starting transfers between devices: 9.78 us -> 14.3 us
    psum x1 -> x0, blocking collectives: 152 us -> none  [per_device(): before = lax.psum(mass_part, 'cells')]
    psum x1 -> x0, waiting for transfers between devices: 130 us -> none  [broadcast(): return lax.psum(block, axis)]
    all_to_all x0 -> x1, blocking collectives: none -> 16.8 us  [per_device(): received = lax.all_to_all(masses, 'cells', 0, 0, tiled=True)]
    slice x10 -> x0, local copies, waits for them, and re-layouts: 15.4 us -> none  [the longest x1 7.34 us: per_device(): dp_new = fields[3]]
    sub x9 -> x0, other arithmetic: 15 us -> none  [the longest x3 9.21 us: ppm_sweep(): 7.0 / 12.0]
    pallas_call x0 -> x3, Pallas kernels: none -> 11.4 us  [the longest x1 10.5 us: per_device(): call(sweep_kernel, [SMEM, ANY, ANY, ANY, VMEM, VMEM, VMEM, VMEM], (LEV, C...]
    dot_general x1 -> x0, matrix products: 8.75 us -> none  [per_device(): jnp.einsum('lmxy,tmxy->tlxy', inverse, third, precision=lax.Precision.HIG...]
    unnamed x32 -> x4, local copies, waits for them, and re-layouts: 7.37 us -> 1.27 us
  transfers between devices with their start and end apart: 5 -> 6, of which waited for: 5 -> 4; matrix products, arithmetic and copies ran while one was open for 2% -> 1% of each run, Pallas kernels for 0% -> 1%
where the time goes in v1:
time: 79.6 us; the launch traced here: 78.9 us
  waiting for transfers between devices  33.4 us (42%)
  blocking collectives  16.8 us (21%)
  starting transfers between devices  14.3 us (18%)
  Pallas kernels  11.4 us (14%)
  local copies, waits for them, and re-layouts  1.27 us (2%)
  other arithmetic  0.94 us (1%)
    ppermute x6, waiting for transfers between devices, swap(): return lax.ppermute(value, axis, [(i, partner(i, n)) for i in range(n)])  33.4 us
    all_to_all x1, blocking collectives, per_device(): received = lax.all_to_all(masses, 'cells', 0, 0, tiled=True)  16.8 us
    ppermute x6, starting transfers between devices, swap(): return lax.ppermute(value, axis, [(i, partner(i, n)) for i in range(n)])  14.3 us
    pallas_call x1, Pallas kernels, per_device(): call(sweep_kernel, [SMEM, ANY, ANY, ANY, VMEM, VMEM, VMEM, VMEM], (LEV, C...  10.5 us
  transfers between devices with their start and end apart: 6, of which 4 were waited for; matrix products, arithmetic and copies ran while one was open for 1% of the time, Pallas kernels for 1%

profile of v1, /device:TPU:16, one launch (start us, length us, event | category | flops | bytes accessed | tf_op | source)
XLA Modules:
  0.0 78.9 jit_solution(7973517524919056021)
XLA Ops:
  0.0 8.8 %collective-permute-start.1 = (f32[6,6,64,128]{3,2,1,0:T(8,128)}, f32[6,6,64,128]{3,2,1,0:T(8,128)S(1)}, u32[]{:S(2)}, u32[]{:S(2)}) collective-permute-start(f32[6,6,64,128]{3,2,1,0:T(8,128)} %bitcast.16), channel_id=1, source_target_pairs={{0,252},{4,8},{8,4},{12,16},{16,12},{20,24},{24,20},{28,32},{32,28... | collective-permute-start | bytes 3538952 | tf_op jit(solution)/shard_map/ppermute | solution.py:225
  8.8 0.0 collective-permute-start
  8.8 0.6 collective-permute-start.2
  10.1 27.9 %collective-permute-done.2 = f32[360,128]{1,0:T(8,128)S(1)} collective-permute-done((f32[360,128]{1,0:T(8,128)}, f32[360,128]{1,0:T(8,128)S(1)}, u32[]{:S(2)}, u32[]{:S(2)}) %collective-permute-start.2) | collective-permute-done | bytes 184352 | tf_op jit(solution)/shard_map/ppermute | solution.py:225
  37.9 0.9 %broadcast_select_fusion.own = f32[360,128]{1,0:T(8,128)S(1)} fusion(f32[360,128]{1,0:T(8,128)} %bitcast.25, f32[360,128]{1,0:T(8,128)S(1)} %collective-permute-done.2, pred[]{:T(512)S(6)} %eq.11), kind=kLoop, calls=%fused_computation | loop fusion | flops 46080 | bytes 552961 | tf_op jit(solution)/shard_map/jit(_where)/select_n | solution.py:246
  38.9 0.1 collective-permute-start.3
  39.0 1.4 %collective-permute-done.3.other = f32[360,128]{1,0:T(8,128)S(1)} collective-permute-done((f32[360,128]{1,0:T(8,128)S(1)}, f32[360,128]{1,0:T(8,128)S(1)}, u32[]{:S(2)}, u32[]{:S(2)}) %collective-permute-start.3) | collective-permute-done | bytes 184352 | tf_op jit(solution)/shard_map/ppermute | solution.py:225
  40.4 0.1 shard_map.37
  40.5 4.8 %collective-permute-start.5 = (f32[108,128]{1,0:T(8,128)S(1)}, f32[108,128]{1,0:T(8,128)S(1)}, u32[]{:S(2)}, u32[]{:S(2)}) collective-permute-start(f32[108,128]{1,0:T(8,128)S(1)} %get-tuple-element.10.own), channel_id=1, source_target_pairs={{0,252},{4,8},{8,4},{12,16},{16,12},{20,24},{24,20},{28,32},{32,28... | collective-permute-start | bytes 165896 | tf_op jit(solution)/shard_map/ppermute | solution.py:225
  45.3 0.0 collective-permute-start.4
  45.3 3.7 %collective-permute-done.5.second = f32[108,128]{1,0:T(8,128)S(1)} collective-permute-done((f32[108,128]{1,0:T(8,128)S(1)}, f32[108,128]{1,0:T(8,128)S(1)}, u32[]{:S(2)}, u32[]{:S(2)}) %collective-permute-start.5) | collective-permute-done | bytes 55328 | tf_op jit(solution)/shard_map/ppermute | solution.py:225
  48.9 0.5 collective-permute-done.4.first
  49.5 0.0 copy-start
  49.5 1.3 %copy-done = f32[64,6,6,128]{3,0,2,1:T(8,128)S(1)} copy-done((f32[64,6,6,128]{3,0,2,1:T(8,128)S(1)}, f32[64,6,6,128]{3,0,2,1:T(8,128)}, u32[]{:S(2)}) %copy-start) | copy-done | bytes 1179672
  50.7 0.0 copy-start.1
  50.7 0.8 %shard_map.38 = (f32[576,128]{1,0:T(8,128)S(1)}, f32[576,128]{1,0:T(8,128)S(1)}, f32[64,128]{1,0:T(8,128)S(1)}) custom-call(s32[1]{0:T(128)} %bitcast.flag, f32[108,128]{1,0:T(8,128)S(1)} %get-tuple-element.10.own, f32[108,128]{1,0:T(8,128)S(1)} %collective-permute-done.4.first, f32[108,128]{1,0:T(8,128)S(1)} %collective-permute-done.5.second, ...), custom_call_target="tpu_custom_call" | custom-call | tf_op jit(solution)/shard_map/pallas_call | solution.py:256
  51.6 16.8 %all_to_all.11 = f32[64,1,128]{2,1,0:T(1,128)S(1)} all-to-all(f32[64,1,128]{2,1,0:T(1,128)S(1)} %bitcast.23), channel_id=1, replica_groups=mesh['cells'=64,'tracers'=4] {'cells'}, dimensions={0} | all-to-all | bytes 65536 | tf_op jit(solution)/shard_map/all_to_all | solution.py:261
  68.4 0.0 collective-permute-done.1.second
  68.4 0.0 collective-permute-done.first
  68.4 0.0 copy-done.1
  68.4 10.5 %shard_map.39 = f32[6,6,64,128]{3,2,1,0:T(8,128)} custom-call(s32[1]{0:T(128)} %bitcast.flag, f32[6,6,64,128]{3,2,1,0:T(8,128)S(1)} %bitcast.19, f32[6,6,64,128]{3,2,1,0:T(8,128)S(1)} %collective-permute-done.first, f32[6,6,64,128]{3,2,1,0:T(8,128)S(1)} %collective-permute-done.1.second, f32[6,12,8,128]{3,2,1,0:T(8,128)S(1)} %bitcast.20, ...), custom_call_target="tpu_custom_call" | custom-call | tf_op jit(solution)/shard_map/pallas_call | solution.py:263
Async XLA Ops:
  0.0 68.4 %collective-permute-start.1 = (f32[6,6,64,128]{3,2,1,0:T(8,128)}, f32[6,6,64,128]{3,2,1,0:T(8,128)S(1)}, u32[]{:S(2)}, u32[]{:S(2)}) collective-permute-start(f32[6,6,64,128]{3,2,1,0:T(8,128)} %bitcast.16), channel_id=1, source_target_pairs={{0,252},{4,8},{8,4},{12,16},{16,12},{20,24},{24,20},{28,32},{32,28... | collective-permute-start | bytes 3538952 | tf_op jit(solution)/shard_map/ppermute | solution.py:225
  8.8 59.6 %collective-permute-start = (f32[6,6,64,128]{3,2,1,0:T(8,128)}, f32[6,6,64,128]{3,2,1,0:T(8,128)S(1)}, u32[]{:S(2)}, u32[]{:S(2)}) collective-permute-start(f32[6,6,64,128]{3,2,1,0:T(8,128)} %bitcast.17), channel_id=1, source_target_pairs={{0,4},{4,0},{8,12},{12,8},{16,20},{20,16},{24,28},{28,24},{32,36},... | collective-permute-start | bytes 3538952 | tf_op jit(solution)/shard_map/ppermute | solution.py:225
  8.8 29.2 %collective-permute-start.2 = (f32[360,128]{1,0:T(8,128)}, f32[360,128]{1,0:T(8,128)S(1)}, u32[]{:S(2)}, u32[]{:S(2)}) collective-permute-start(f32[360,128]{1,0:T(8,128)} %bitcast.24), channel_id=1, source_target_pairs={{0,2},{1,3},{2,0},{3,1},{4,6},{5,7},{6,4},{7,5},{8,10},{9,11},{10,... | collective-permute-start | bytes 552968 | tf_op jit(solution)/shard_map/ppermute | solution.py:225
  38.9 1.5 %collective-permute-start.3 = (f32[360,128]{1,0:T(8,128)S(1)}, f32[360,128]{1,0:T(8,128)S(1)}, u32[]{:S(2)}, u32[]{:S(2)}) collective-permute-start(f32[360,128]{1,0:T(8,128)S(1)} %broadcast_select_fusion.own), channel_id=1, source_target_pairs={{0,1},{1,0},{2,3},{3,2},{4,5},{5,4},{6,7},{7,6},{8,9},{9,8},{10,11... | collective-permute-start | bytes 552968 | tf_op jit(solution)/shard_map/ppermute | solution.py:225
  40.5 8.5 %collective-permute-start.5 = (f32[108,128]{1,0:T(8,128)S(1)}, f32[108,128]{1,0:T(8,128)S(1)}, u32[]{:S(2)}, u32[]{:S(2)}) collective-permute-start(f32[108,128]{1,0:T(8,128)S(1)} %get-tuple-element.10.own), channel_id=1, source_target_pairs={{0,252},{4,8},{8,4},{12,16},{16,12},{20,24},{24,20},{28,32},{32,28... | collective-permute-start | bytes 165896 | tf_op jit(solution)/shard_map/ppermute | solution.py:225
  45.3 4.2 %collective-permute-start.4 = (f32[108,128]{1,0:T(8,128)S(1)}, f32[108,128]{1,0:T(8,128)S(1)}, u32[]{:S(2)}, u32[]{:S(2)}) collective-permute-start(f32[108,128]{1,0:T(8,128)S(1)} %get-tuple-element.10.own), channel_id=1, source_target_pairs={{0,4},{4,0},{8,12},{12,8},{16,20},{20,16},{24,28},{28,24},{32,36},... | collective-permute-start | bytes 165896 | tf_op jit(solution)/shard_map/ppermute | solution.py:225
  49.5 1.3 %copy-start = (f32[64,6,6,128]{3,0,2,1:T(8,128)S(1)}, f32[64,6,6,128]{3,0,2,1:T(8,128)}, u32[]{:S(2)}) copy-start(f32[64,6,6,128]{3,0,2,1:T(8,128)} %param.3) | copy-start | bytes 3538948
  50.7 17.6 %copy-start.1 = (f32[64,6,6,128]{3,0,2,1:T(8,128)S(1)}, f32[64,6,6,128]{3,0,2,1:T(8,128)}, u32[]{:S(2)}) copy-start(f32[64,6,6,128]{3,0,2,1:T(8,128)} %param.3) | copy-start | bytes 3538948

commit v2 on v1

--- a/solution.py
+++ b/solution.py
@@ -12,8 +12,10 @@
 NF = 10
 HALO = 3
 WIDE = CX + 2 * HALO
+EARLY = 2
 F32 = jnp.float32
-VMEM_LIMIT = 48 * 1024 * 1024
+VMEM_LIMIT = 10 * 1024 * 1024
+WHOLE_VMEM = 60 * 1024 * 1024
 
 
 def face_weights(c):
@@ -70,9 +72,24 @@
     ]
 
 
-def merge_kernel(flag, own, other, fields, message):
-    take = flag[0] == 1
-    fields[...] = jnp.where(take, own[...], other[...])
+def split_kernel(start, tracers, *rest):
+    part, sems = rest[-2:]
+    moves = [pltpu.make_async_copy(tracers.at[start + l], part.at[l], sems.at[l]) for l in range(part.shape[0])]
+    for move in moves:
+        move.start()
+    for move in moves:
+        move.wait()
+
+
+def gate_kernel(*refs):
+    pass
+
+
+def merge_kernel(place, own, near, far, across, fields, message):
+    core, chip = place[0] == 1, place[1] == 1
+    here = jnp.where(core, own[...], near[...])
+    there = jnp.where(core, far[...], across[...])
+    fields[...] = jnp.where(chip, here, there)
     for x in range(CX):
         for f in range(2):
             message[pl.ds(f * ROWS + x * LEV, LEV), :] = fields[pl.ds(f * ROWS + x, LEV, stride=CX), :]
@@ -139,84 +156,112 @@
         masses[pl.ds(8 * i, 8), :] = sums
 
 
-def sweep_kernel(flag, tracers, first, second, wx, wy, fields, received, out, wide, middle, third, sems):
-    count = tracers.shape[2]
-    left_first = flag[0]
-    first_at = (1 - left_first) * 2 * CX
-    second_at = left_first * 2 * CX
+def start_wide(flag, start, tracers, first, second, wide, sems):
+    first_at = (1 - flag[0]) * 2 * CX
+    second_at = flag[0] * 2 * CX
 
     def copies(l):
         return [
-            pltpu.make_async_copy(tracers.at[l], wide.at[l, pl.ds(CX, CX)], sems.at[l, 0]),
+            pltpu.make_async_copy(tracers.at[start + l], wide.at[l, pl.ds(CX, CX)], sems.at[l, 0]),
             pltpu.make_async_copy(first.at[l], wide.at[l, pl.ds(first_at, CX)], sems.at[l, 1]),
             pltpu.make_async_copy(second.at[l], wide.at[l, pl.ds(second_at, CX)], sems.at[l, 2]),
         ]
 
-    for l in range(LEV):
+    for l in range(first.shape[0]):
         for copy in copies(l):
             copy.start()
-
+    return copies
+
+
+def sweep_levels(start, copies, wide, wx, wy, middle, third, third_at):
+    count, block = middle.shape[1], 32
+
+    def level(l, carry):
+        for copy in copies(l):
+            copy.wait()
+        row = (start + l) * WIDE
+
+        def weight(ref, x, k):
+            return ref[pl.ds((row + x) * 8 + k, 1), :]
+
+        for t in range(0, count, block):
+            ts = pl.ds(t, block)
+            for x in range(WIDE):
+                value = None
+                for k in range(7):
+                    part = weight(wx, x, k) * wide[l, x + k, ts, :]
+                    value = part if value is None else value + part
+                moved = None
+                for k in range(7):
+                    q = value if k == 3 else pltpu.roll(value, (3 - k) % NY, 1)
+                    part = weight(wy, x, k) * q
+                    moved = part if moved is None else moved + part
+                middle[x, ts, :] = moved
+            for x in range(CX):
+                value = None
+                for k in range(7):
+                    part = weight(wx, x + HALO, k) * middle[x + k, ts, :]
+                    value = part if value is None else value + part
+                third[third_at + l, x, ts, :] = value
+        return carry
+
+    lax.fori_loop(0, wide.shape[0], level, 0)
+
+
+def early_kernel(flag, tracers, h1, h2, wx, wy, third, wide, middle, sems):
+    copies = start_wide(flag, 0, tracers, h1, h2, wide, sems)
+    sweep_levels(0, copies, wide, wx, wy, middle, third, 0)
+
+
+def late_kernel(flag, tracers, h1, h2, wx, wy, fields, early, out, wide, middle, third, sems):
+    done = early.shape[0]
+    copies = start_wide(flag, done, tracers, h1, h2, wide, sems)
+    count, block = tracers.shape[2], 32
+    sweep_levels(done, copies, wide, wx, wy, middle, third, 0)
+    for x in range(CX):
+        for t in range(0, count, block):
+            ts = pl.ds(t, block)
+            levels = [early[m, x, ts, :] if m < done else third[m - done, x, ts, :] for m in range(LEV)]
+            for l in range(LEV):
+                value = None
+                for m in range(LEV):
+                    part = fields[pl.ds((4 + l) * ROWS + m * CX + x, 1), :] * levels[m]
+                    value = part if value is None else value + part
+                out[l, x, ts, :] = value
+
+
+def scale_kernel(received, diffused, out, scaled, sems):
+    count = diffused.shape[2]
     total = jnp.sum(received[...], axis=0, keepdims=True)
     ratio = total / pltpu.roll(jnp.broadcast_to(total, (8, NY)), NY // 2, 1)[:1]
     lane = lax.broadcasted_iota(jnp.int32, (count, NY), 1)
     row = lax.broadcasted_iota(jnp.int32, (count, NY), 0)
     scale = jnp.sum(jnp.where(lane == row, jnp.broadcast_to(ratio, (count, NY)), 0.0), axis=1, keepdims=True)
-
-    block = 32
-
-    def level(l, carry):
-        for copy in copies(l):
-            copy.wait()
-        for t in range(0, count, block):
-            ts = pl.ds(t, block)
-            for x in range(WIDE):
-                value = None
-                for k in range(7):
-                    part = wx[l, x, pl.ds(k, 1), :] * wide[l, x + k, ts, :]
-                    value = part if value is None else value + part
-                moved = None
-                for k in range(7):
-                    q = value if k == 3 else pltpu.roll(value, (3 - k) % NY, 1)
-                    part = wy[l, x, pl.ds(k, 1), :] * q
-                    moved = part if moved is None else moved + part
-                middle[x, ts, :] = moved
-            for x in range(CX):
-                value = None
-                for k in range(7):
-                    part = wx[l, x + HALO, pl.ds(k, 1), :] * middle[x + k, ts, :]
-                    value = part if value is None else value + part
-                third[l, x, ts, :] = value
-        return carry
-
-    lax.fori_loop(0, LEV, level, 0)
-    for x in range(CX):
-        for t in range(0, count, block):
-            ts = pl.ds(t, block)
-            levels = [third[m, x, ts, :] for m in range(LEV)]
-            factor = scale[t : t + block]
-            for l in range(LEV):
-                value = None
-                for m in range(LEV):
-                    part = fields[pl.ds((4 + l) * ROWS + m * CX + x, 1), :] * levels[m]
-                    value = part if value is None else value + part
-                out[l, x, ts, :] = value * factor
+    factor = jnp.broadcast_to(scale, (count, NY))
+    moves = [pltpu.make_async_copy(scaled.at[l], out.at[l], sems.at[l]) for l in range(LEV)]
+    for l in range(LEV):
+        for x in range(CX):
+            scaled[l, x] = diffused[l, x] * factor
+        moves[l].start()
+    for move in moves:
+        move.wait()
 
 
 SMEM = pl.BlockSpec(memory_space=pltpu.SMEM)
 VMEM = pl.BlockSpec(memory_space=pltpu.VMEM)
 ANY = pl.BlockSpec(memory_space=pl.ANY)
-
-
-def call(kernel, ins, outs, scratch=(), flops=0):
-    many = isinstance(outs, list)
-    shapes = [jax.ShapeDtypeStruct(s, F32) for s in outs] if many else jax.ShapeDtypeStruct(outs, F32)
+HBM = pl.BlockSpec(memory_space=pltpu.HBM)
+
+
+def call(kernel, ins, outs, places=None, scratch=(), limit=VMEM_LIMIT, aliases=()):
     return pl.pallas_call(
         kernel,
-        out_shape=shapes,
+        out_shape=[jax.ShapeDtypeStruct(s, F32) for s in outs],
         in_specs=ins,
-        out_specs=[VMEM] * len(outs) if many else VMEM,
+        out_specs=places or [VMEM] * len(outs),
         scratch_shapes=list(scratch),
-        compiler_params=pltpu.CompilerParams(vmem_limit_bytes=VMEM_LIMIT),
+        compiler_params=pltpu.CompilerParams(vmem_limit_bytes=limit),
+        input_output_aliases=dict(aliases),
     )
 
 
@@ -242,16 +287,33 @@
     count = state.shape[2]
     raw = hour_fields.reshape(NF * ROWS, NY)
 
+    early, late = EARLY, LEV - EARLY
+
+    def other_core(value):
+        return swap(value, "tracers", lambda i, n: i ^ 1)
+
     far = swap(raw, "tracers", lambda i, n: i ^ 2)
-    half = jnp.where(reader // 2 == mine // 2, raw, far)
-    near = swap(half, "tracers", lambda i, n: i ^ 1)
-    same = (reader % 2 == mine % 2).astype(jnp.int32)[None]
-    fields, message = call(merge_kernel, [SMEM, VMEM, VMEM], [(NF * ROWS, NY), (3 * ROWS, NY)])(same, half, near)
+    near = other_core(raw)
+    def split(start, levels, after, limit, place):
+        kernel = functools.partial(split_kernel, start)
+        ins, shape = [HBM] + [ANY] * len(after), (levels, CX, count, NY)
+        return call(kernel, ins, [shape], [place], [pltpu.SemaphoreType.DMA((levels,))], limit)(state, *after)[0]
+
+    chunk = split(0, early, [], VMEM_LIMIT, ANY)
+    a2 = swap(chunk, "cells", odd_pairs)
+    a1 = swap(chunk, "cells", even_pairs)
+    across = other_core(far)
+    place = jnp.stack([reader % 2 == mine % 2, reader // 2 == mine // 2]).astype(jnp.int32)
+    fields, message = call(
+        merge_kernel, [SMEM, VMEM, VMEM, VMEM, VMEM], [(NF * ROWS, NY), (3 * ROWS, NY)]
+    )(place, raw, near, far, across)
 
     m1 = swap(message, "cells", even_pairs)
     m2 = swap(message, "cells", odd_pairs)
-    h1 = swap(state, "cells", even_pairs)
-    h2 = swap(state, "cells", odd_pairs)
+    rest = split(early, late, [far], VMEM_LIMIT, ANY)
+    rest = call(gate_kernel, [ANY] * 5, [rest.shape], [ANY], aliases={0: 0})(rest, m1, m2, a1, a2)[0]
+    b1 = swap(rest, "cells", even_pairs)
+    b2 = swap(rest, "cells", odd_pairs)
 
     wx, wy, masses = call(
         weights_kernel,
@@ -259,18 +321,36 @@
         [(LEV * WIDE * 8, NY), (LEV * WIDE * 8, NY), (n, 2 * count)],
     )(odd, message, m1, m2, fields, state)
     received = lax.all_to_all(masses, "cells", 0, 0, tiled=True)
-    wx, wy = wx.reshape(LEV, WIDE, 8, NY), wy.reshape(LEV, WIDE, 8, NY)
+    third = call(
+        early_kernel,
+        [SMEM, ANY, ANY, ANY, VMEM, VMEM],
+        [(early, CX, count, NY)],
+        None,
+        [
+            pltpu.VMEM((early, 3 * CX, count, NY), F32),
+            pltpu.VMEM((WIDE, count, NY), F32),
+            pltpu.SemaphoreType.DMA((early, 3)),
+        ],
+    )(odd, state, a1, a2, wx, wy)[0]
+    diffused = call(
+        late_kernel,
+        [SMEM, ANY, ANY, ANY, VMEM, VMEM, VMEM, VMEM],
+        [(LEV, CX, count, NY)],
+        None,
+        [
+            pltpu.VMEM((late, 3 * CX, count, NY), F32),
+            pltpu.VMEM((WIDE, count, NY), F32),
+            pltpu.VMEM((late, CX, count, NY), F32),
+            pltpu.SemaphoreType.DMA((late, 3)),
+        ],
+    )(odd, state, b1, b2, wx, wy, fields, third)[0]
     out = call(
-        sweep_kernel,
-        [SMEM, ANY, ANY, ANY, VMEM, VMEM, VMEM, VMEM],
-        (LEV, CX, count, NY),
-        [
-            pltpu.VMEM((LEV, 3 * CX, count, NY), F32),
-            pltpu.VMEM((WIDE, count, NY), F32),
-            pltpu.VMEM((LEV, CX, count, NY), F32),
-            pltpu.SemaphoreType.DMA((LEV, 3)),
-        ],
-    )(odd, state, h1, h2, wx, wy, fields, received)
+        scale_kernel,
+        [VMEM, VMEM],
+        [(LEV, CX, count, NY)],
+        [HBM],
+        [pltpu.VMEM((LEV, CX, count, NY), F32), pltpu.SemaphoreType.DMA((LEV,))],
+    )(received, diffused)[0]
     return jnp.transpose(out, (2, 0, 1, 3))
 
 

time: 79.6 us -> 55.2 us (0.69)
  waiting for transfers between devices: 33.4 us -> 10.3 us
  blocking collectives: 16.8 us -> 0 us
  starting transfers between devices: 14.3 us -> 25.6 us
  local copies, waits for them, and re-layouts: 1.27 us -> 5.01 us
  Pallas kernels: 11.4 us -> 12.6 us
  other arithmetic: 0.94 us -> 0.08 us
    ppermute x6 -> x9, waiting for transfers between devices: 33.4 us -> 10.3 us  [swap(): return lax.ppermute(value, axis, [(i, partner(i, n)) for i in range(n)])]
    all_to_all x1 -> x0, blocking collectives: 16.8 us -> none  [per_device(): received = lax.all_to_all(masses, 'cells', 0, 0, tiled=True)]
    all_to_all x0 -> x1, starting transfers between devices: none -> 5.73 us  [per_device(): received = lax.all_to_all(masses, 'cells', 0, 0, tiled=True)]
    ppermute x6 -> x9, starting transfers between devices: 14.3 us -> 19.9 us  [swap(): return lax.ppermute(value, axis, [(i, partner(i, n)) for i in range(n)])]
    unnamed x4 -> x20, local copies, waits for them, and re-layouts: 1.27 us -> 5.01 us
    pallas_call x2 -> x7, Pallas kernels: 10.6 us -> 11.8 us  [the longest x1 4.56 us: per_device(): call(late_kernel, [SMEM, ANY, ANY, ANY, VMEM, VMEM, VMEM, VMEM], [(LEV, C...]
    select_n x1 -> x0, other arithmetic: 0.94 us -> none  [per_device(): half = jnp.where(reader // 2 == mine // 2, raw, far)]
  transfers between devices with their start and end apart: 6 -> 10, of which waited for: 4 -> 7; matrix products, arithmetic and copies ran while one was open for 1% -> 0% of each run, Pallas kernels for 1% -> 19%
where the time goes in v2:
time: 55.2 us; the launch traced here: 54.5 us
  starting transfers between devices  25.6 us (46%)
  Pallas kernels  12.6 us (23%)
  waiting for transfers between devices  10.3 us (19%)
  local copies, waits for them, and re-layouts  5.01 us (9%)
  between operations  0.78 us (1%)
    ppermute x9, starting transfers between devices, swap(): return lax.ppermute(value, axis, [(i, partner(i, n)) for i in range(n)])  19.9 us
    ppermute x9, waiting for transfers between devices, swap(): return lax.ppermute(value, axis, [(i, partner(i, n)) for i in range(n)])  10.3 us
    all_to_all x1, starting transfers between devices, per_device(): received = lax.all_to_all(masses, 'cells', 0, 0, tiled=True)  5.73 us
    unnamed x20, local copies, waits for them, and re-layouts  5.01 us
    pallas_call x1, Pallas kernels, per_device(): call(late_kernel, [SMEM, ANY, ANY, ANY, VMEM, VMEM, VMEM, VMEM], [(LEV, C...  4.56 us
    pallas_call x1, Pallas kernels, per_device(): call(early_kernel, [SMEM, ANY, ANY, ANY, VMEM, VMEM], [(early, CX, count,...  2.97 us
    pallas_call x1, Pallas kernels, per_device(): call(scale_kernel, [VMEM, VMEM], [(LEV, CX, count, NY)], [HBM], [pltpu.VM...  2.04 us
    pallas_call x2, Pallas kernels, split(): call(kernel, ins, [shape], [place], [pltpu.SemaphoreType.DMA((levels,))],...  1.55 us
  transfers between devices with their start and end apart: 10, of which 7 were waited for; matrix products, arithmetic and copies ran while one was open for 0% of the time, Pallas kernels for 19%

profile of v2, /device:TPU:16, one launch (start us, length us, event | category | flops | bytes accessed | tf_op | source)
XLA Modules:
  0.0 54.5 jit_solution(10337397675820168585)
XLA Ops:
  0.0 2.1 %collective-permute-start.1 = (f32[360,128]{1,0:T(8,128)}, f32[360,128]{1,0:T(8,128)S(1)}, u32[]{:S(2)}, u32[]{:S(2)}) collective-permute-start(f32[360,128]{1,0:T(8,128)} %bitcast.20), channel_id=1, source_target_pairs={{0,2},{1,3},{2,0},{3,1},{4,6},{5,7},{6,4},{7,5},{8,10},{9,11},{10,... | collective-permute-start | bytes 552968 | tf_op jit(solution)/shard_map/ppermute | solution.py:270
  2.1 0.0 copy-start
  2.1 1.3 %copy-done = f32[64,6,6,128]{3,0,2,1:T(8,128)S(1)} copy-done((f32[64,6,6,128]{3,0,2,1:T(8,128)S(1)}, f32[64,6,6,128]{3,0,2,1:T(8,128)}, u32[]{:S(2)}) %copy-start) | copy-done | bytes 1179672
  3.3 0.0 copy-start.6
  3.3 0.0 copy-start.1
  3.3 0.5 shard_map.40
  3.9 8.0 %collective-permute-start.6 = (f32[2,6,64,128]{3,2,1,0:T(8,128)S(1)}, f32[2,6,64,128]{3,2,1,0:T(8,128)S(1)}, u32[]{:S(2)}, u32[]{:S(2)}) collective-permute-start(f32[2,6,64,128]{3,2,1,0:T(8,128)S(1)} %shard_map.40), channel_id=1, source_target_pairs={{0,252},{4,8},{8,4},{12,16},{16,12},{20,24},{24,20},{28,32},{32,28... | collective-permute-start | bytes 1179656 | tf_op jit(solution)/shard_map/ppermute | solution.py:270
  11.9 0.0 collective-permute-start.5
  11.9 0.0 copy-done.6
  11.9 0.0 collective-permute-start
  11.9 0.0 collective-permute-done.1.far.rest_0_
  11.9 0.5 collective-permute-start.2
  13.1 0.1 add_convert_fusion.place
  13.2 0.1 collective-permute-done.near
  13.3 0.3 collective-permute-done.2.across
  13.6 0.6 %shard_map.37 = (f32[360,128]{1,0:T(8,128)S(1)}, f32[108,128]{1,0:T(8,128)S(1)}) custom-call(s32[2]{0:T(128)S(1)} %add_convert_fusion.place, f32[360,128]{1,0:T(8,128)S(1)} %bitcast.22, f32[360,128]{1,0:T(8,128)S(1)} %collective-permute-done.near, f32[360,128]{1,0:T(8,128)S(1)} %collective-permute-done.1.far.rest_0_, ...), custom_call_target="tpu_custom_call" | custom-call | tf_op jit(solution)/shard_map/pallas_call | solution.py:307
  14.2 0.0 copy-start.7
  14.2 4.8 %collective-permute-start.4 = (f32[108,128]{1,0:T(8,128)S(1)}, f32[108,128]{1,0:T(8,128)S(1)}, u32[]{:S(2)}, u32[]{:S(2)}) collective-permute-start(f32[108,128]{1,0:T(8,128)S(1)} %get-tuple-element.10.own), channel_id=1, source_target_pairs={{0,252},{4,8},{8,4},{12,16},{16,12},{20,24},{24,20},{28,32},{32,28... | collective-permute-start | bytes 165896 | tf_op jit(solution)/shard_map/ppermute | solution.py:270
  19.0 0.0 collective-permute-start.3
  19.0 0.0 copy-done.1
  19.0 1.0 %shard_map.39.refs_0_ = f32[4,6,64,128]{3,2,1,0:T(8,128)S(1)} custom-call(f32[6,6,64,128]{3,2,1,0:T(8,128)S(1)} %bitcast.16, f32[360,128]{1,0:T(8,128)S(1)} %collective-permute-done.1.far.rest_0_), custom_call_target="tpu_custom_call" | custom-call | tf_op jit(solution)/shard_map/pallas_call | solution.py:300
  20.1 0.6 %collective-permute-done.6.refs_4_.h2 = f32[2,6,64,128]{3,2,1,0:T(8,128)S(1)} collective-permute-done((f32[2,6,64,128]{3,2,1,0:T(8,128)S(1)}, f32[2,6,64,128]{3,2,1,0:T(8,128)S(1)}, u32[]{:S(2)}, u32[]{:S(2)}) %collective-permute-start.6) | collective-permute-done | bytes 393248 | tf_op jit(solution)/shard_map/ppermute | solution.py:270
  20.7 2.1 %collective-permute-done.5.refs_3_.h1 = f32[2,6,64,128]{3,2,1,0:T(8,128)S(1)} collective-permute-done((f32[2,6,64,128]{3,2,1,0:T(8,128)S(1)}, f32[2,6,64,128]{3,2,1,0:T(8,128)S(1)}, u32[]{:S(2)}, u32[]{:S(2)}) %collective-permute-start.5) | collective-permute-done | bytes 393248 | tf_op jit(solution)/shard_map/ppermute | solution.py:270
  22.8 0.0 collective-permute-done.4.second.refs_2_
  22.8 0.0 copy-start.2
  22.8 0.6 %collective-permute-done.3.first.refs_1_ = f32[108,128]{1,0:T(8,128)S(1)} collective-permute-done((f32[108,128]{1,0:T(8,128)S(1)}, f32[108,128]{1,0:T(8,128)S(1)}, u32[]{:S(2)}, u32[]{:S(2)}) %collective-permute-start.3) | collective-permute-done | bytes 55328 | tf_op jit(solution)/shard_map/ppermute | solution.py:270
  23.4 0.0 copy-start.4
  23.4 0.0 copy-done.7
  23.4 0.0 copy-done.2
  23.4 0.6 %copy-done.4 = f32[108,128]{1,0:T(8,128)} copy-done((f32[108,128]{1,0:T(8,128)}, f32[108,128]{1,0:T(8,128)S(1)}, u32[]{:S(2)}) %copy-start.4) | copy-done | bytes 55320
  24.0 4.5 %collective-permute-start.8 = (f32[4,6,64,128]{3,2,1,0:T(8,128)S(1)}, f32[4,6,64,128]{3,2,1,0:T(8,128)}, u32[]{:S(2)}, u32[]{:S(2)}) collective-permute-start(f32[4,6,64,128]{3,2,1,0:T(8,128)S(1)} %shard_map.41), channel_id=1, source_target_pairs={{0,252},{4,8},{8,4},{12,16},{16,12},{20,24},{24,20},{28,32},{32,28... | collective-permute-start | bytes 2359304 | tf_op jit(solution)/shard_map/ppermute | solution.py:270
  28.6 0.0 collective-permute-start.7
  28.6 0.0 copy-start.3
  28.6 0.8 %copy-done.3 = f32[108,128]{1,0:T(8,128)S(1)} copy-done((f32[108,128]{1,0:T(8,128)S(1)}, f32[108,128]{1,0:T(8,128)}, u32[]{:S(2)}) %copy-start.3) | copy-done | bytes 55320
  29.4 0.0 copy-start.5
  29.4 0.8 %copy-done.5 = f32[108,128]{1,0:T(8,128)S(1)} copy-done((f32[108,128]{1,0:T(8,128)S(1)}, f32[108,128]{1,0:T(8,128)}, u32[]{:S(2)}) %copy-start.5) | copy-done | bytes 55320
  30.2 0.0 copy-start.8
  30.2 0.8 %copy-done.8 = f32[108,128]{1,0:T(8,128)S(1)} copy-done((f32[108,128]{1,0:T(8,128)S(1)}, f32[108,128]{1,0:T(8,128)}, u32[]{:S(2)}) %copy-start.8) | copy-done | bytes 55320
  31.0 0.8 %shard_map.38 = (f32[576,128]{1,0:T(8,128)S(1)}, f32[576,128]{1,0:T(8,128)S(1)}, f32[64,128]{1,0:T(8,128)S(1)}) custom-call(s32[1]{0:T(128)} %bitcast.flag, f32[108,128]{1,0:T(8,128)S(1)} %copy-done.8, f32[108,128]{1,0:T(8,128)S(1)} %copy-done.5, f32[108,128]{1,0:T(8,128)S(1)} %copy-done.3, f32[360,128]{1,0:T(8,128)S(1)} %get-tuple-element.11.fields, ...), custom_call_target="tpu_custom_call" | custom-call | tf_op jit(solution)/shard_map/pallas_call | solution.py:318
  31.9 0.0 copy-start.9
  31.9 0.6 %copy-done.9 = f32[64,128]{1,0:T(8,128)} copy-done((f32[64,128]{1,0:T(8,128)}, f32[64,128]{1,0:T(8,128)S(1)}, u32[]{:S(2)}) %copy-start.9) | copy-done | bytes 32792
  32.5 5.7 %all-to-all-start = ((f32[64,1,128]{2,1,0:T(1,128)}), f32[64,1,128]{2,1,0:T(1,128)}, u32[]{:S(2)}, u32[]{:S(2)}) async-start(f32[64,1,128]{2,1,0:T(1,128)} %bitcast.23), calls=%async_computation | async-start | bytes 65536 | tf_op jit(solution)/shard_map/all_to_all | solution.py:323
  38.3 3.0 %shard_map.42.early = f32[2,6,64,128]{3,2,1,0:T(8,128)S(1)} custom-call(s32[1]{0:T(128)} %bitcast.flag, f32[6,6,64,128]{3,2,1,0:T(8,128)S(1)} %bitcast.18, f32[2,6,64,128]{3,2,1,0:T(8,128)S(1)} %collective-permute-done.5.refs_3_.h1, f32[2,6,64,128]{3,2,1,0:T(8,128)S(1)} %collective-permute-done.6.refs_4_.h2, f32[576,128]{1,0:T(8,128)S(1)} %get-tuple-element.13.wx, ...), custom_call_target="tpu_custom_call" | custom-call | tf_op jit(solution)/shard_map/pallas_call | solution.py:324
  41.2 6.4 %collective-permute-done.8.h2 = f32[4,6,64,128]{3,2,1,0:T(8,128)} collective-permute-done((f32[4,6,64,128]{3,2,1,0:T(8,128)S(1)}, f32[4,6,64,128]{3,2,1,0:T(8,128)}, u32[]{:S(2)}, u32[]{:S(2)}) %collective-permute-start.8) | collective-permute-done | bytes 786464 | tf_op jit(solution)/shard_map/ppermute | solution.py:270
  47.7 0.2 collective-permute-done.7.h1
  47.8 4.6 %shard_map.43.diffused = f32[6,6,64,128]{3,2,1,0:T(8,128)S(1)} custom-call(s32[1]{0:T(128)} %bitcast.flag, f32[6,6,64,128]{3,2,1,0:T(8,128)S(1)} %bitcast.19, f32[4,6,64,128]{3,2,1,0:T(8,128)} %collective-permute-done.7.h1, f32[4,6,64,128]{3,2,1,0:T(8,128)} %collective-permute-done.8.h2, f32[576,128]{1,0:T(8,128)S(1)} %get-tuple-element.13.wx, ...), custom_call_target="tpu_custom_call" | custom-call | tf_op jit(solution)/shard_map/pallas_call | solution.py:335
  52.4 0.0 all-to-all-done
  52.4 2.0 %shard_map.44 = f32[6,6,64,128]{3,2,1,0:T(8,128)} custom-call(f32[64,128]{1,0:T(8,128)} %bitcast.8.received, f32[6,6,64,128]{3,2,1,0:T(8,128)S(1)} %shard_map.43.diffused), custom_call_target="tpu_custom_call" | custom-call | tf_op jit(solution)/shard_map/pallas_call | solution.py:347
  (1 shorter events, 0.0 us)
Async XLA Ops:
  0.0 11.9 %collective-permute-start.1 = (f32[360,128]{1,0:T(8,128)}, f32[360,128]{1,0:T(8,128)S(1)}, u32[]{:S(2)}, u32[]{:S(2)}) collective-permute-start(f32[360,128]{1,0:T(8,128)} %bitcast.20), channel_id=1, source_target_pairs={{0,2},{1,3},{2,0},{3,1},{4,6},{5,7},{6,4},{7,5},{8,10},{9,11},{10,... | collective-permute-start | bytes 552968 | tf_op jit(solution)/shard_map/ppermute | solution.py:270
  2.1 1.3 %copy-start = (f32[64,6,6,128]{3,0,2,1:T(8,128)S(1)}, f32[64,6,6,128]{3,0,2,1:T(8,128)}, u32[]{:S(2)}) copy-start(f32[64,6,6,128]{3,0,2,1:T(8,128)} %param.3) | copy-start | bytes 3538948
  3.3 8.5 %copy-start.6 = (f32[1,10,6,6,128]{4,0,3,2,1:T(1,128)S(1)}, f32[1,10,6,6,128]{4,0,3,2,1:T(1,128)}, u32[]{:S(2)}) copy-start(f32[1,10,6,6,128]{4,0,3,2,1:T(1,128)} %param.4) | copy-start | bytes 552964
  3.3 15.7 %copy-start.1 = (f32[64,6,6,128]{3,0,2,1:T(8,128)S(1)}, f32[64,6,6,128]{3,0,2,1:T(8,128)}, u32[]{:S(2)}) copy-start(f32[64,6,6,128]{3,0,2,1:T(8,128)} %param.3) | copy-start | bytes 3538948
  3.9 16.9 %collective-permute-start.6 = (f32[2,6,64,128]{3,2,1,0:T(8,128)S(1)}, f32[2,6,64,128]{3,2,1,0:T(8,128)S(1)}, u32[]{:S(2)}, u32[]{:S(2)}) collective-permute-start(f32[2,6,64,128]{3,2,1,0:T(8,128)S(1)} %shard_map.40), channel_id=1, source_target_pairs={{0,252},{4,8},{8,4},{12,16},{16,12},{20,24},{24,20},{28,32},{32,28... | collective-permute-start | bytes 1179656 | tf_op jit(solution)/shard_map/ppermute | solution.py:270
  11.9 10.9 %collective-permute-start.5 = (f32[2,6,64,128]{3,2,1,0:T(8,128)S(1)}, f32[2,6,64,128]{3,2,1,0:T(8,128)S(1)}, u32[]{:S(2)}, u32[]{:S(2)}) collective-permute-start(f32[2,6,64,128]{3,2,1,0:T(8,128)S(1)} %shard_map.40), channel_id=1, source_target_pairs={{0,4},{4,0},{8,12},{12,8},{16,20},{20,16},{24,28},{28,24},{32,36},... | collective-permute-start | bytes 1179656 | tf_op jit(solution)/shard_map/ppermute | solution.py:270
  11.9 1.4 %collective-permute-start = (f32[360,128]{1,0:T(8,128)S(1)}, f32[360,128]{1,0:T(8,128)S(1)}, u32[]{:S(2)}, u32[]{:S(2)}) collective-permute-start(f32[360,128]{1,0:T(8,128)S(1)} %bitcast.21), channel_id=1, source_target_pairs={{0,1},{1,0},{2,3},{3,2},{4,5},{5,4},{6,7},{7,6},{8,9},{9,8},{10,11... | collective-permute-start | bytes 552968 | tf_op jit(solution)/shard_map/ppermute | solution.py:270
  11.9 1.7 %collective-permute-start.2 = (f32[360,128]{1,0:T(8,128)S(1)}, f32[360,128]{1,0:T(8,128)S(1)}, u32[]{:S(2)}, u32[]{:S(2)}) collective-permute-start(f32[360,128]{1,0:T(8,128)S(1)} %collective-permute-done.1.far.rest_0_), channel_id=1, source_target_pairs={{0,1},{1,0},{2,3},{3,2},{4,5},{5,4},{6,7},{7,6},{8,9},{9,8},{10,11... | collective-permute-start | bytes 552968 | tf_op jit(solution)/shard_map/ppermute | solution.py:270
  14.2 9.2 %copy-start.7 = (f32[108,128]{1,0:T(8,128)}, f32[108,128]{1,0:T(8,128)S(1)}, u32[]{:S(2)}) copy-start(f32[108,128]{1,0:T(8,128)S(1)} %get-tuple-element.10.own) | copy-start | bytes 165892
  14.2 8.6 %collective-permute-start.4 = (f32[108,128]{1,0:T(8,128)S(1)}, f32[108,128]{1,0:T(8,128)S(1)}, u32[]{:S(2)}, u32[]{:S(2)}) collective-permute-start(f32[108,128]{1,0:T(8,128)S(1)} %get-tuple-element.10.own), channel_id=1, source_target_pairs={{0,252},{4,8},{8,4},{12,16},{16,12},{20,24},{24,20},{28,32},{32,28... | collective-permute-start | bytes 165896 | tf_op jit(solution)/shard_map/ppermute | solution.py:270
  19.0 4.4 %collective-permute-start.3 = (f32[108,128]{1,0:T(8,128)S(1)}, f32[108,128]{1,0:T(8,128)S(1)}, u32[]{:S(2)}, u32[]{:S(2)}) collective-permute-start(f32[108,128]{1,0:T(8,128)S(1)} %get-tuple-element.10.own), channel_id=1, source_target_pairs={{0,4},{4,0},{8,12},{12,8},{16,20},{20,16},{24,28},{28,24},{32,36},... | collective-permute-start | bytes 165896 | tf_op jit(solution)/shard_map/ppermute | solution.py:270
  22.8 0.6 %copy-start.2 = (f32[108,128]{1,0:T(8,128)}, f32[108,128]{1,0:T(8,128)S(1)}, u32[]{:S(2)}) copy-start(f32[108,128]{1,0:T(8,128)S(1)} %collective-permute-done.4.second.refs_2_) | copy-start | bytes 165892
  23.4 0.6 %copy-start.4 = (f32[108,128]{1,0:T(8,128)}, f32[108,128]{1,0:T(8,128)S(1)}, u32[]{:S(2)}) copy-start(f32[108,128]{1,0:T(8,128)S(1)} %collective-permute-done.3.first.refs_1_) | copy-start | bytes 165892
  24.0 23.6 %collective-permute-start.8 = (f32[4,6,64,128]{3,2,1,0:T(8,128)S(1)}, f32[4,6,64,128]{3,2,1,0:T(8,128)}, u32[]{:S(2)}, u32[]{:S(2)}) collective-permute-start(f32[4,6,64,128]{3,2,1,0:T(8,128)S(1)} %shard_map.41), channel_id=1, source_target_pairs={{0,252},{4,8},{8,4},{12,16},{16,12},{20,24},{24,20},{28,32},{32,28... | collective-permute-start | bytes 2359304 | tf_op jit(solution)/shard_map/ppermute | solution.py:270
  28.6 19.3 %collective-permute-start.7 = (f32[4,6,64,128]{3,2,1,0:T(8,128)S(1)}, f32[4,6,64,128]{3,2,1,0:T(8,128)}, u32[]{:S(2)}, u32[]{:S(2)}) collective-permute-start(f32[4,6,64,128]{3,2,1,0:T(8,128)S(1)} %shard_map.41), channel_id=1, source_target_pairs={{0,4},{4,0},{8,12},{12,8},{16,20},{20,16},{24,28},{28,24},{32,36},... | collective-permute-start | bytes 2359304 | tf_op jit(solution)/shard_map/ppermute | solution.py:270
  28.6 0.8 %copy-start.3 = (f32[108,128]{1,0:T(8,128)S(1)}, f32[108,128]{1,0:T(8,128)}, u32[]{:S(2)}) copy-start(f32[108,128]{1,0:T(8,128)} %copy-done.2) | copy-start | bytes 165892
  29.4 0.8 %copy-start.5 = (f32[108,128]{1,0:T(8,128)S(1)}, f32[108,128]{1,0:T(8,128)}, u32[]{:S(2)}) copy-start(f32[108,128]{1,0:T(8,128)} %copy-done.4) | copy-start | bytes 165892
  30.2 0.8 %copy-start.8 = (f32[108,128]{1,0:T(8,128)S(1)}, f32[108,128]{1,0:T(8,128)}, u32[]{:S(2)}) copy-start(f32[108,128]{1,0:T(8,128)} %copy-done.7) | copy-start | bytes 165892
  31.9 0.6 %copy-start.9 = (f32[64,128]{1,0:T(8,128)}, f32[64,128]{1,0:T(8,128)S(1)}, u32[]{:S(2)}) copy-start(f32[64,128]{1,0:T(8,128)S(1)} %get-tuple-element.12) | copy-start | bytes 98308
  32.5 19.9 %all-to-all-start = ((f32[64,1,128]{2,1,0:T(1,128)}), f32[64,1,128]{2,1,0:T(1,128)}, u32[]{:S(2)}, u32[]{:S(2)}) async-start(f32[64,1,128]{2,1,0:T(1,128)} %bitcast.23), calls=%async_computation | async-start | bytes 65536 | tf_op jit(solution)/shard_map/all_to_all | solution.py:323

commit v3 on v2

--- a/solution.py
+++ b/solution.py
@@ -12,10 +12,13 @@
 NF = 10
 HALO = 3
 WIDE = CX + 2 * HALO
-EARLY = 2
+CHUNKS = (2, 0)
+KA_FLOPS = 10000000000
+KB_FLOPS = 0
+MERGE_FLOPS = 0
+HEAD = 112
 F32 = jnp.float32
 VMEM_LIMIT = 10 * 1024 * 1024
-WHOLE_VMEM = 60 * 1024 * 1024
 
 
 def face_weights(c):
@@ -81,12 +84,8 @@
         move.wait()
 
 
-def gate_kernel(*refs):
-    pass
-
-
-def merge_kernel(place, own, near, far, across, fields, message):
-    core, chip = place[0] == 1, place[1] == 1
+def merge_kernel(same_core, same_chip, own, near, far, across, after, fields, message):
+    core, chip = same_core[0] == 1, same_chip[0] == 1
     here = jnp.where(core, own[...], near[...])
     there = jnp.where(core, far[...], across[...])
     fields[...] = jnp.where(chip, here, there)
@@ -101,7 +100,7 @@
         message[pl.ds(2 * ROWS + x * LEV, LEV), :] = total
 
 
-def weights_kernel(flag, own, first, second, fields, tracers, wx, wy, masses):
+def weights_kernel(flag, own, first, second, fields, tracers, after, wx, wy, masses):
     left_first = flag[0] == 1
 
     def column(f, x):
@@ -157,17 +156,21 @@
 
 
 def start_wide(flag, start, tracers, first, second, wide, sems):
-    first_at = (1 - flag[0]) * 2 * CX
-    second_at = flag[0] * 2 * CX
+    size = tracers.shape[1]
+    first_at = (1 - flag[0]) * 2 * size
+    second_at = flag[0] * 2 * size
+
+    def level(ref, l):
+        return ref.at[l] if ref.ndim == 3 else ref.at[pl.ds(pl.multiple_of(HEAD + l * size, 8), size)]
 
     def copies(l):
         return [
-            pltpu.make_async_copy(tracers.at[start + l], wide.at[l, pl.ds(CX, CX)], sems.at[l, 0]),
-            pltpu.make_async_copy(first.at[l], wide.at[l, pl.ds(first_at, CX)], sems.at[l, 1]),
-            pltpu.make_async_copy(second.at[l], wide.at[l, pl.ds(second_at, CX)], sems.at[l, 2]),
+            pltpu.make_async_copy(tracers.at[start + l], wide.at[l, pl.ds(size, size)], sems.at[l, 0]),
+            pltpu.make_async_copy(level(first, l), wide.at[l, pl.ds(first_at, size)], sems.at[l, 1]),
+            pltpu.make_async_copy(level(second, l), wide.at[l, pl.ds(second_at, size)], sems.at[l, 2]),
         ]
 
-    for l in range(first.shape[0]):
+    for l in range(wide.shape[0]):
         for copy in copies(l):
             copy.start()
     return copies
@@ -176,8 +179,13 @@
 def sweep_levels(start, copies, wide, wx, wy, middle, third, third_at):
     count, block = middle.shape[1], 32
 
+    def column(l, x, t):
+        if not isinstance(wide, tuple):
+            return wide[l, pl.ds(x * count + t, block), :]
+        return wide[x // CX][l + (start if x // CX == 1 else 0), pl.ds(x % CX * count + t, block), :]
+
     def level(l, carry):
-        for copy in copies(l):
+        for copy in copies(l) if copies else ():
             copy.wait()
         row = (start + l) * WIDE
 
@@ -189,7 +197,7 @@
             for x in range(WIDE):
                 value = None
                 for k in range(7):
-                    part = weight(wx, x, k) * wide[l, x + k, ts, :]
+                    part = weight(wx, x, k) * column(l, x + k, t)
                     value = part if value is None else value + part
                 moved = None
                 for k in range(7):
@@ -205,7 +213,15 @@
                 third[third_at + l, x, ts, :] = value
         return carry
 
-    lax.fori_loop(0, wide.shape[0], level, 0)
+    lax.fori_loop(0, wide[0].shape[0] if isinstance(wide, tuple) else wide.shape[0], level, 0)
+
+
+def token_kernel(first, second, token):
+    token[...] = jnp.zeros_like(token)
+
+
+def gate_kernel(*refs):
+    pass
 
 
 def early_kernel(flag, tracers, h1, h2, wx, wy, third, wide, middle, sems):
@@ -213,11 +229,17 @@
     sweep_levels(0, copies, wide, wx, wy, middle, third, 0)
 
 
-def late_kernel(flag, tracers, h1, h2, wx, wy, fields, early, out, wide, middle, third, sems):
-    done = early.shape[0]
-    copies = start_wide(flag, done, tracers, h1, h2, wide, sems)
-    count, block = tracers.shape[2], 32
-    sweep_levels(done, copies, wide, wx, wy, middle, third, 0)
+def late_kernel(flag, tracers, h1, h2, wx, wy, fields, early, out, middle, third):
+    done, count, block = early.shape[0], early.shape[2], 32
+
+    @pl.when(flag[0] == 1)
+    def _():
+        sweep_levels(done, None, (h1, tracers, h2), wx, wy, middle, third, 0)
+
+    @pl.when(flag[0] == 0)
+    def _():
+        sweep_levels(done, None, (h2, tracers, h1), wx, wy, middle, third, 0)
+
     for x in range(CX):
         for t in range(0, count, block):
             ts = pl.ds(t, block)
@@ -253,16 +275,30 @@
 HBM = pl.BlockSpec(memory_space=pltpu.HBM)
 
 
-def call(kernel, ins, outs, places=None, scratch=(), limit=VMEM_LIMIT, aliases=()):
+def work(flops):
+    return pl.CostEstimate(flops=flops, bytes_accessed=0, transcendentals=0)
+
+
+def call(kernel, ins, outs, places=None, scratch=(), limit=VMEM_LIMIT, aliases=(), cost=None):
+    places = places or [VMEM] * len(outs)
     return pl.pallas_call(
         kernel,
-        out_shape=[jax.ShapeDtypeStruct(s, F32) for s in outs],
+        out_shape=[s if not isinstance(s, tuple) else pltpu.VMEM(s, F32) if p is VMEM else jax.ShapeDtypeStruct(s, F32) for s, p in zip(outs, places)],
         in_specs=ins,
-        out_specs=places or [VMEM] * len(outs),
+        out_specs=places,
         scratch_shapes=list(scratch),
         compiler_params=pltpu.CompilerParams(vmem_limit_bytes=limit),
         input_output_aliases=dict(aliases),
+        cost_estimate=cost,
     )
+
+
+def in_hbm(value):
+    return pltpu.with_memory_space_constraint(value, pltpu.HBM)
+
+
+def in_vmem(value):
+    return pltpu.with_memory_space_constraint(value, pltpu.VMEM)
 
 
 def swap(value, axis, partner):
@@ -287,39 +323,42 @@
     count = state.shape[2]
     raw = hour_fields.reshape(NF * ROWS, NY)
 
-    early, late = EARLY, LEV - EARLY
+    a_levels, c_levels = CHUNKS
+    early, late = a_levels + c_levels, LEV - a_levels - c_levels
+    flat = state.reshape(LEV, CX * count, NY)
 
     def other_core(value):
         return swap(value, "tracers", lambda i, n: i ^ 1)
 
     far = swap(raw, "tracers", lambda i, n: i ^ 2)
     near = other_core(raw)
-    def split(start, levels, after, limit, place):
+    def split(start, levels, *after):
         kernel = functools.partial(split_kernel, start)
-        ins, shape = [HBM] + [ANY] * len(after), (levels, CX, count, NY)
-        return call(kernel, ins, [shape], [place], [pltpu.SemaphoreType.DMA((levels,))], limit)(state, *after)[0]
-
-    chunk = split(0, early, [], VMEM_LIMIT, ANY)
+        shape = (levels, CX * count, NY)
+        return call(kernel, [ANY] * (1 + len(after)), [shape], [ANY], [pltpu.SemaphoreType.DMA((levels,))])(in_hbm(flat), *after)[0]
+
+    chunk = split(0, a_levels)
+    a1 = swap(chunk, "cells", even_pairs)
     a2 = swap(chunk, "cells", odd_pairs)
-    a1 = swap(chunk, "cells", even_pairs)
     across = other_core(far)
-    place = jnp.stack([reader % 2 == mine % 2, reader // 2 == mine // 2]).astype(jnp.int32)
-    fields, message = call(
-        merge_kernel, [SMEM, VMEM, VMEM, VMEM, VMEM], [(NF * ROWS, NY), (3 * ROWS, NY)]
-    )(place, raw, near, far, across)
-
-    m1 = swap(message, "cells", even_pairs)
-    m2 = swap(message, "cells", odd_pairs)
-    rest = split(early, late, [far], VMEM_LIMIT, ANY)
-    rest = call(gate_kernel, [ANY] * 5, [rest.shape], [ANY], aliases={0: 0})(rest, m1, m2, a1, a2)[0]
+    same_core = (reader % 2 == mine % 2).astype(jnp.int32)[None]
+    same_chip = (reader // 2 == mine // 2).astype(jnp.int32)[None]
+    rest = split(early, late, far)
+    fields, message = call(merge_kernel, [SMEM, SMEM, VMEM, VMEM, VMEM, VMEM, ANY], [(NF * ROWS, NY), (3 * ROWS, NY)], cost=work(MERGE_FLOPS))(
+        same_core, same_chip, raw, near, far, across, rest
+    )
+    c1 = swap(message, "cells", even_pairs)
+    c2 = swap(message, "cells", odd_pairs)
+    rest = call(gate_kernel, [ANY, ANY], [rest.shape], [ANY], aliases={0: 0})(rest, message)[0]
     b1 = swap(rest, "cells", even_pairs)
     b2 = swap(rest, "cells", odd_pairs)
 
+    token = call(token_kernel, [ANY, ANY], [(8, NY)])(in_hbm(a1), in_hbm(a2))[0]
     wx, wy, masses = call(
         weights_kernel,
-        [SMEM, VMEM, VMEM, VMEM, VMEM, VMEM],
-        [(LEV * WIDE * 8, NY), (LEV * WIDE * 8, NY), (n, 2 * count)],
-    )(odd, message, m1, m2, fields, state)
+        [SMEM, VMEM, VMEM, VMEM, VMEM, VMEM, ANY],
+        [pltpu.HBM((LEV * WIDE * 8, NY), F32), pltpu.HBM((LEV * WIDE * 8, NY), F32), (n, 2 * count)],
+    )(odd, message, c1, c2, fields, state, token)
     received = lax.all_to_all(masses, "cells", 0, 0, tiled=True)
     third = call(
         early_kernel,
@@ -327,23 +366,23 @@
         [(early, CX, count, NY)],
         None,
         [
-            pltpu.VMEM((early, 3 * CX, count, NY), F32),
+            pltpu.VMEM((early, 3 * CX * count, NY), F32),
             pltpu.VMEM((WIDE, count, NY), F32),
             pltpu.SemaphoreType.DMA((early, 3)),
         ],
-    )(odd, state, a1, a2, wx, wy)[0]
+        cost=work(KA_FLOPS),
+    )(odd, flat, in_hbm(a1), in_hbm(a2), wx, wy)[0]
     diffused = call(
         late_kernel,
-        [SMEM, ANY, ANY, ANY, VMEM, VMEM, VMEM, VMEM],
+        [SMEM] + [VMEM] * 7,
         [(LEV, CX, count, NY)],
         None,
         [
-            pltpu.VMEM((late, 3 * CX, count, NY), F32),
             pltpu.VMEM((WIDE, count, NY), F32),
             pltpu.VMEM((late, CX, count, NY), F32),
-            pltpu.SemaphoreType.DMA((late, 3)),
         ],
-    )(odd, state, b1, b2, wx, wy, fields, third)[0]
+        cost=work(KB_FLOPS),
+    )(odd, flat, in_vmem(b1), in_vmem(b2), wx, wy, fields, third)[0]
     out = call(
         scale_kernel,
         [VMEM, VMEM],

time: 55.2 us -> 49.9 us (0.904)
  local copies, waits for them, and re-layouts: 5.01 us -> 1.93 us
  waiting for transfers between devices: 10.3 us -> 9.38 us
  starting transfers between devices: 25.6 us -> 24.7 us
    unnamed x20 -> x12, local copies, waits for them, and re-layouts: 5.01 us -> 1.93 us
    ppermute x9, starting transfers between devices: 19.9 us -> 18 us  [swap(): return lax.ppermute(value, axis, [(i, partner(i, n)) for i in range(n)])]
    ppermute x9, waiting for transfers between devices: 10.3 us -> 9.38 us  [swap(): return lax.ppermute(value, axis, [(i, partner(i, n)) for i in range(n)])]
    all_to_all x1, starting transfers between devices: 5.73 us -> 6.66 us  [per_device(): received = lax.all_to_all(masses, 'cells', 0, 0, tiled=True)]
    pallas_call x1, Pallas kernels: 2.04 us -> 1.29 us  [per_device(): call(scale_kernel, [VMEM, VMEM], [(LEV, CX, count, NY)], [HBM], [pltpu.VM...]
    pallas_call x6 -> x7, Pallas kernels: 7.6 us -> 8.26 us  [the longest x1 4.36 us: per_device(): call(late_kernel, [SMEM] + [VMEM] * 7, [(LEV, CX, count, NY)], None, [plt...]
  transfers between devices with their start and end apart: 10 -> 10, of which waited for: 7 -> 4; matrix products, arithmetic and copies ran while one was open for 0% -> 0% of each run, Pallas kernels for 19% -> 22%
where the time goes in v3:
time: 49.9 us; the launch traced here: 49.1 us
  starting transfers between devices  24.7 us (49%)
  Pallas kernels  12.3 us (25%)
  waiting for transfers between devices  9.38 us (19%)
  local copies, waits for them, and re-layouts  1.93 us (4%)
  between operations  0.79 us (2%)
    ppermute x9, starting transfers between devices, swap(): return lax.ppermute(value, axis, [(i, partner(i, n)) for i in range(n)])  18 us
    ppermute x9, waiting for transfers between devices, swap(): return lax.ppermute(value, axis, [(i, partner(i, n)) for i in range(n)])  9.38 us
    all_to_all x1, starting transfers between devices, per_device(): received = lax.all_to_all(masses, 'cells', 0, 0, tiled=True)  6.66 us
    pallas_call x1, Pallas kernels, per_device(): call(late_kernel, [SMEM] + [VMEM] * 7, [(LEV, CX, count, NY)], None, [plt...  4.36 us
    pallas_call x1, Pallas kernels, per_device(): call(early_kernel, [SMEM, ANY, ANY, ANY, VMEM, VMEM], [(early, CX, count,...  2.74 us
    pallas_call x2, Pallas kernels, split(): call(kernel, [ANY] * (1 + len(after)), [shape], [ANY], [pltpu.SemaphoreTy...  2.29 us
    unnamed x12, local copies, waits for them, and re-layouts  1.93 us
    pallas_call x1, Pallas kernels, per_device(): call(weights_kernel, [SMEM, VMEM, VMEM, VMEM, VMEM, VMEM, ANY], [pltpu.HB...  1.5 us
  transfers between devices with their start and end apart: 10, of which 4 were waited for; matrix products, arithmetic and copies ran while one was open for 0% of the time, Pallas kernels for 22%

profile of v3, /device:TPU:16, one launch (start us, length us, event | category | flops | bytes accessed | tf_op | source)
XLA Modules:
  0.0 49.1 jit_solution(7060632741403268687)
XLA Ops:
  0.0 0.0 copy-start.5
  0.0 2.1 %collective-permute-start.1 = (f32[360,128]{1,0:T(8,128)}, f32[360,128]{1,0:T(8,128)S(1)}, u32[]{:S(2)}, u32[]{:S(2)}) collective-permute-start(f32[360,128]{1,0:T(8,128)} %bitcast.22), channel_id=1, source_target_pairs={{0,2},{1,3},{2,0},{3,1},{4,6},{5,7},{6,4},{7,5},{8,10},{9,11},{10,... | collective-permute-start | bytes 552968 | tf_op jit(solution)/shard_map/ppermute | solution.py:306
  2.1 1.0 %shard_map.39 = f32[2,384,128]{2,1,0:T(8,128)S(1)} custom-call(f32[6,384,128]{2,1,0:T(8,128)} %bitcast.17), custom_call_target="tpu_custom_call" | custom-call | tf_op jit(solution)/shard_map/pallas_call | solution.py:338
  3.1 8.0 %collective-permute-start.6 = (f32[2,384,128]{2,1,0:T(8,128)S(1)}, f32[2,384,128]{2,1,0:T(8,128)}, u32[]{:S(2)}, u32[]{:S(2)}) collective-permute-start(f32[2,384,128]{2,1,0:T(8,128)S(1)} %shard_map.39), channel_id=1, source_target_pairs={{0,252},{4,8},{8,4},{12,16},{16,12},{20,24},{24,20},{28,32},{32,28... | collective-permute-start | bytes 1179656 | tf_op jit(solution)/shard_map/ppermute | solution.py:306
  11.1 0.0 collective-permute-start.5
  11.1 0.0 copy-done.5
  11.1 0.0 collective-permute-start
  11.2 0.0 collective-permute-done.1.rest_0_.far
  11.2 0.5 %collective-permute-start.2 = (f32[360,128]{1,0:T(8,128)S(1)}, f32[360,128]{1,0:T(8,128)S(1)}, u32[]{:S(2)}, u32[]{:S(2)}) collective-permute-start(f32[360,128]{1,0:T(8,128)S(1)} %collective-permute-done.1.rest_0_.far), channel_id=1, source_target_pairs={{0,1},{1,0},{2,3},{3,2},{4,5},{5,4},{6,7},{7,6},{8,9},{9,8},{10,11... | collective-permute-start | bytes 552968 | tf_op jit(solution)/shard_map/ppermute | solution.py:306
  12.4 1.3 %shard_map.37.after.refs_0_ = f32[4,384,128]{2,1,0:T(8,128)S(1)} custom-call(f32[6,384,128]{2,1,0:T(8,128)} %bitcast.18, f32[360,128]{1,0:T(8,128)S(1)} %collective-permute-done.1.rest_0_.far), custom_call_target="tpu_custom_call" | custom-call | tf_op jit(solution)/shard_map/pallas_call | solution.py:338
  13.6 0.0 collective-permute-done.near
  13.6 0.0 collective-permute-done.2.across
  13.6 0.1 shard_map.38
  13.7 5.3 %collective-permute-start.4 = (f32[108,128]{1,0:T(8,128)S(1)}, f32[108,128]{1,0:T(8,128)S(1)}, u32[]{:S(2)}, u32[]{:S(2)}) collective-permute-start(f32[108,128]{1,0:T(8,128)S(1)} %get-tuple-element.10.own.refs_1_), channel_id=1, source_target_pairs={{0,252},{4,8},{8,4},{12,16},{16,12},{20,24},{24,20},{28,32},{32,28... | collective-permute-start | bytes 165896 | tf_op jit(solution)/shard_map/ppermute | solution.py:306
  19.0 0.0 collective-permute-start.3
  19.0 0.0 copy-start
  19.0 2.0 %collective-permute-start.8 = (f32[4,384,128]{2,1,0:T(8,128)S(1)}, f32[4,384,128]{2,1,0:T(8,128)S(1)}, u32[]{:S(2)}, u32[]{:S(2)}) collective-permute-start(f32[4,384,128]{2,1,0:T(8,128)S(1)} %shard_map.42), channel_id=1, source_target_pairs={{0,252},{4,8},{8,4},{12,16},{16,12},{20,24},{24,20},{28,32},{32,28... | collective-permute-start | bytes 2359304 | tf_op jit(solution)/shard_map/ppermute | solution.py:306
  21.1 0.0 collective-permute-done.6.second.h2
  21.1 0.1 collective-permute-start.7
  21.2 0.4 collective-permute-done.5.first.h1
  21.5 0.7 %collective-permute-done.4.second = f32[108,128]{1,0:T(8,128)S(1)} collective-permute-done((f32[108,128]{1,0:T(8,128)S(1)}, f32[108,128]{1,0:T(8,128)S(1)}, u32[]{:S(2)}, u32[]{:S(2)}) %collective-permute-start.4) | collective-permute-done | bytes 55328 | tf_op jit(solution)/shard_map/ppermute | solution.py:306
  22.2 1.0 %collective-permute-done.3.first = f32[108,128]{1,0:T(8,128)S(1)} collective-permute-done((f32[108,128]{1,0:T(8,128)S(1)}, f32[108,128]{1,0:T(8,128)S(1)}, u32[]{:S(2)}, u32[]{:S(2)}) %collective-permute-start.3) | collective-permute-done | bytes 55328 | tf_op jit(solution)/shard_map/ppermute | solution.py:306
  23.2 0.0 copy-done
  23.2 1.5 %shard_map.41 = (f32[576,128]{1,0:T(8,128)}, f32[576,128]{1,0:T(8,128)}, f32[64,128]{1,0:T(8,128)}) custom-call(s32[1]{0:T(128)} %bitcast.flag, f32[108,128]{1,0:T(8,128)S(1)} %get-tuple-element.10.own.refs_1_, f32[108,128]{1,0:T(8,128)S(1)} %collective-permute-done.3.first, f32[108,128]{1,0:T(8,128)S(1)} %collective-permute-done.4.second, ...), custom_call_target="tpu_custom_call" | custom-call | tf_op jit(solution)/shard_map/pallas_call | solution.py:357
  24.7 6.7 %all-to-all-start = ((f32[64,1,128]{2,1,0:T(1,128)}), f32[64,1,128]{2,1,0:T(1,128)S(1)}, u32[]{:S(2)}, u32[]{:S(2)}) async-start(f32[64,1,128]{2,1,0:T(1,128)} %bitcast.9), calls=%async_computation | async-start | bytes 65536 | tf_op jit(solution)/shard_map/all_to_all | solution.py:362
  31.4 0.0 copy-start.1
  31.4 1.0 %copy-done.1 = f32[576,128]{1,0:T(8,128)S(1)} copy-done((f32[576,128]{1,0:T(8,128)S(1)}, f32[576,128]{1,0:T(8,128)}, u32[]{:S(2)}) %copy-start.1) | copy-done | bytes 294936
  32.3 0.0 copy-start.3
  32.3 1.0 %copy-done.3 = f32[576,128]{1,0:T(8,128)S(1)} copy-done((f32[576,128]{1,0:T(8,128)S(1)}, f32[576,128]{1,0:T(8,128)}, u32[]{:S(2)}) %copy-start.3) | copy-done | bytes 294936
  33.3 0.0 copy-start.2
  33.3 0.0 copy-start.4
  33.3 2.7 %shard_map.43.early = f32[2,6,64,128]{3,2,1,0:T(8,128)S(1)} custom-call(s32[1]{0:T(128)} %bitcast.flag, f32[6,384,128]{2,1,0:T(8,128)S(1)} %bitcast.20, f32[2,384,128]{2,1,0:T(8,128)} %collective-permute-done.5.first.h1, f32[2,384,128]{2,1,0:T(8,128)} %collective-permute-done.6.second.h2, f32[576,128]{1,0:T(8,128)S(1)} %copy-done.1, f32[576,128]{1,0:T(8,128)S(1)} %copy-done.3), custom_call_target="tpu_custom_call" | custom-call | flops 10000000000 | tf_op jit(solution)/shard_map/pallas_call | solution.py:363
  36.1 7.3 %collective-permute-done.8.h2 = f32[4,384,128]{2,1,0:T(8,128)S(1)} collective-permute-done((f32[4,384,128]{2,1,0:T(8,128)S(1)}, f32[4,384,128]{2,1,0:T(8,128)S(1)}, u32[]{:S(2)}, u32[]{:S(2)}) %collective-permute-start.8) | collective-permute-done | bytes 786464 | tf_op jit(solution)/shard_map/ppermute | solution.py:306
  43.4 0.0 collective-permute-done.7.h1
  43.4 0.0 copy-done.2
  43.4 0.0 copy-done.4
  43.4 4.4 %shard_map.44.diffused = f32[6,6,64,128]{3,2,1,0:T(8,128)S(1)} custom-call(s32[1]{0:T(128)} %bitcast.flag, f32[6,384,128]{2,1,0:T(8,128)S(1)} %bitcast.21, f32[4,384,128]{2,1,0:T(8,128)} %collective-permute-done.7.h1, f32[4,384,128]{2,1,0:T(8,128)S(1)} %collective-permute-done.8.h2, f32[576,128]{1,0:T(8,128)S(1)} %copy-done.2, f32[576,128]{1,0:T(8,128)S(1)} %copy-done.4, ...), custom_call_target="tpu_custom_call" | custom-call | tf_op jit(solution)/shard_map/pallas_call | solution.py:375
  47.8 0.0 all-to-all-done
  47.8 1.3 %shard_map.45 = f32[6,6,64,128]{3,2,1,0:T(8,128)} custom-call(f32[64,128]{1,0:T(8,128)S(1)} %bitcast.25, f32[6,6,64,128]{3,2,1,0:T(8,128)S(1)} %shard_map.44.diffused), custom_call_target="tpu_custom_call" | custom-call | tf_op jit(solution)/shard_map/pallas_call | solution.py:386
  (2 shorter events, 0.0 us)
Async XLA Ops:
  0.0 11.1 %copy-start.5 = (f32[1,10,6,6,128]{4,0,3,2,1:T(1,128)S(1)}, f32[1,10,6,6,128]{4,0,3,2,1:T(1,128)}, u32[]{:S(2)}) copy-start(f32[1,10,6,6,128]{4,0,3,2,1:T(1,128)} %param.4) | copy-start | bytes 552964
  0.0 11.2 %collective-permute-start.1 = (f32[360,128]{1,0:T(8,128)}, f32[360,128]{1,0:T(8,128)S(1)}, u32[]{:S(2)}, u32[]{:S(2)}) collective-permute-start(f32[360,128]{1,0:T(8,128)} %bitcast.22), channel_id=1, source_target_pairs={{0,2},{1,3},{2,0},{3,1},{4,6},{5,7},{6,4},{7,5},{8,10},{9,11},{10,... | collective-permute-start | bytes 552968 | tf_op jit(solution)/shard_map/ppermute | solution.py:306
  3.1 17.9 %collective-permute-start.6 = (f32[2,384,128]{2,1,0:T(8,128)S(1)}, f32[2,384,128]{2,1,0:T(8,128)}, u32[]{:S(2)}, u32[]{:S(2)}) collective-permute-start(f32[2,384,128]{2,1,0:T(8,128)S(1)} %shard_map.39), channel_id=1, source_target_pairs={{0,252},{4,8},{8,4},{12,16},{16,12},{20,24},{24,20},{28,32},{32,28... | collective-permute-start | bytes 1179656 | tf_op jit(solution)/shard_map/ppermute | solution.py:306
  11.1 10.4 %collective-permute-start.5 = (f32[2,384,128]{2,1,0:T(8,128)S(1)}, f32[2,384,128]{2,1,0:T(8,128)}, u32[]{:S(2)}, u32[]{:S(2)}) collective-permute-start(f32[2,384,128]{2,1,0:T(8,128)S(1)} %shard_map.39), channel_id=1, source_target_pairs={{0,4},{4,0},{8,12},{12,8},{16,20},{20,16},{24,28},{28,24},{32,36},... | collective-permute-start | bytes 1179656 | tf_op jit(solution)/shard_map/ppermute | solution.py:306
  11.1 2.5 %collective-permute-start = (f32[360,128]{1,0:T(8,128)S(1)}, f32[360,128]{1,0:T(8,128)S(1)}, u32[]{:S(2)}, u32[]{:S(2)}) collective-permute-start(f32[360,128]{1,0:T(8,128)S(1)} %bitcast.23), channel_id=1, source_target_pairs={{0,1},{1,0},{2,3},{3,2},{4,5},{5,4},{6,7},{7,6},{8,9},{9,8},{10,11... | collective-permute-start | bytes 552968 | tf_op jit(solution)/shard_map/ppermute | solution.py:306
  11.2 2.5 %collective-permute-start.2 = (f32[360,128]{1,0:T(8,128)S(1)}, f32[360,128]{1,0:T(8,128)S(1)}, u32[]{:S(2)}, u32[]{:S(2)}) collective-permute-start(f32[360,128]{1,0:T(8,128)S(1)} %collective-permute-done.1.rest_0_.far), channel_id=1, source_target_pairs={{0,1},{1,0},{2,3},{3,2},{4,5},{5,4},{6,7},{7,6},{8,9},{9,8},{10,11... | collective-permute-start | bytes 552968 | tf_op jit(solution)/shard_map/ppermute | solution.py:306
  13.7 8.5 %collective-permute-start.4 = (f32[108,128]{1,0:T(8,128)S(1)}, f32[108,128]{1,0:T(8,128)S(1)}, u32[]{:S(2)}, u32[]{:S(2)}) collective-permute-start(f32[108,128]{1,0:T(8,128)S(1)} %get-tuple-element.10.own.refs_1_), channel_id=1, source_target_pairs={{0,252},{4,8},{8,4},{12,16},{16,12},{20,24},{24,20},{28,32},{32,28... | collective-permute-start | bytes 165896 | tf_op jit(solution)/shard_map/ppermute | solution.py:306
  19.0 4.2 %collective-permute-start.3 = (f32[108,128]{1,0:T(8,128)S(1)}, f32[108,128]{1,0:T(8,128)S(1)}, u32[]{:S(2)}, u32[]{:S(2)}) collective-permute-start(f32[108,128]{1,0:T(8,128)S(1)} %get-tuple-element.10.own.refs_1_), channel_id=1, source_target_pairs={{0,4},{4,0},{8,12},{12,8},{16,20},{20,16},{24,28},{28,24},{32,36},... | collective-permute-start | bytes 165896 | tf_op jit(solution)/shard_map/ppermute | solution.py:306
  19.0 4.2 %copy-start = (f32[64,6,6,128]{3,0,2,1:T(8,128)S(1)}, f32[64,6,6,128]{3,0,2,1:T(8,128)}, u32[]{:S(2)}) copy-start(f32[64,6,6,128]{3,0,2,1:T(8,128)} %param.3) | copy-start | bytes 3538948
  19.0 24.3 %collective-permute-start.8 = (f32[4,384,128]{2,1,0:T(8,128)S(1)}, f32[4,384,128]{2,1,0:T(8,128)S(1)}, u32[]{:S(2)}, u32[]{:S(2)}) collective-permute-start(f32[4,384,128]{2,1,0:T(8,128)S(1)} %shard_map.42), channel_id=1, source_target_pairs={{0,252},{4,8},{8,4},{12,16},{16,12},{20,24},{24,20},{28,32},{32,28... | collective-permute-start | bytes 2359304 | tf_op jit(solution)/shard_map/ppermute | solution.py:306
  21.1 22.3 %collective-permute-start.7 = (f32[4,384,128]{2,1,0:T(8,128)S(1)}, f32[4,384,128]{2,1,0:T(8,128)}, u32[]{:S(2)}, u32[]{:S(2)}) collective-permute-start(f32[4,384,128]{2,1,0:T(8,128)S(1)} %shard_map.42), channel_id=1, source_target_pairs={{0,4},{4,0},{8,12},{12,8},{16,20},{20,16},{24,28},{28,24},{32,36},... | collective-permute-start | bytes 2359304 | tf_op jit(solution)/shard_map/ppermute | solution.py:306
  24.7 23.0 %all-to-all-start = ((f32[64,1,128]{2,1,0:T(1,128)}), f32[64,1,128]{2,1,0:T(1,128)S(1)}, u32[]{:S(2)}, u32[]{:S(2)}) async-start(f32[64,1,128]{2,1,0:T(1,128)} %bitcast.9), calls=%async_computation | async-start | bytes 65536 | tf_op jit(solution)/shard_map/all_to_all | solution.py:362
  31.4 1.0 %copy-start.1 = (f32[576,128]{1,0:T(8,128)S(1)}, f32[576,128]{1,0:T(8,128)}, u32[]{:S(2)}) copy-start(f32[576,128]{1,0:T(8,128)} %get-tuple-element.13.wx) | copy-start | bytes 884740
  32.3 1.0 %copy-start.3 = (f32[576,128]{1,0:T(8,128)S(1)}, f32[576,128]{1,0:T(8,128)}, u32[]{:S(2)}) copy-start(f32[576,128]{1,0:T(8,128)} %get-tuple-element.14.wy) | copy-start | bytes 884740
  33.3 10.1 %copy-start.2 = (f32[576,128]{1,0:T(8,128)S(1)}, f32[576,128]{1,0:T(8,128)}, u32[]{:S(2)}) copy-start(f32[576,128]{1,0:T(8,128)} %get-tuple-element.13.wx) | copy-start | bytes 884740
  33.3 10.1 %copy-start.4 = (f32[576,128]{1,0:T(8,128)S(1)}, f32[576,128]{1,0:T(8,128)}, u32[]{:S(2)}) copy-start(f32[576,128]{1,0:T(8,128)} %get-tuple-element.14.wy) | copy-start | bytes 884740

commit v4 on v3

--- a/solution.py
+++ b/solution.py
@@ -75,8 +75,7 @@
     ]
 
 
-def split_kernel(start, tracers, *rest):
-    part, sems = rest[-2:]
+def split_kernel(start, tracers, part, sems):
     moves = [pltpu.make_async_copy(tracers.at[start + l], part.at[l], sems.at[l]) for l in range(part.shape[0])]
     for move in moves:
         move.start()
@@ -84,8 +83,15 @@
         move.wait()
 
 
-def merge_kernel(same_core, same_chip, own, near, far, across, after, fields, message):
-    core, chip = same_core[0] == 1, same_chip[0] == 1
+def split_mask_kernel(start, reader, mine, tracers, part, mask, sems):
+    differ = reader[0] ^ mine[0]
+    mask[pl.ds(0, 8), :] = jnp.full((8, NY), differ & 1, jnp.int32)
+    mask[pl.ds(8, 8), :] = jnp.full((8, NY), differ >> 1, jnp.int32)
+    split_kernel(start, tracers, part, sems)
+
+
+def merge_kernel(mask, own, near, far, across, fields, message):
+    core, chip = mask[pl.ds(0, 1), :] == 0, mask[pl.ds(8, 1), :] == 0
     here = jnp.where(core, own[...], near[...])
     there = jnp.where(core, far[...], across[...])
     fields[...] = jnp.where(chip, here, there)
@@ -155,90 +161,84 @@
         masses[pl.ds(8 * i, 8), :] = sums
 
 
-def start_wide(flag, start, tracers, first, second, wide, sems):
-    size = tracers.shape[1]
-    first_at = (1 - flag[0]) * 2 * size
-    second_at = flag[0] * 2 * size
-
-    def level(ref, l):
-        return ref.at[l] if ref.ndim == 3 else ref.at[pl.ds(pl.multiple_of(HEAD + l * size, 8), size)]
-
+def stencil(weight, q):
+    value = weight(0) * q(0)
+    for k in range(1, 7):
+        value = value + weight(k) * q(k)
+    return value
+
+
+def sweeps(level, columns, first, last, wx, wy, middle, third):
+    count, block = middle.shape[1], 32
+
+    def weights(ref, x):
+        return lambda k: ref[pl.ds((level * WIDE + x) * 8 + k, 1), :]
+
+    for t in range(0, count, block):
+        ts = pl.ds(t, block)
+        for x in range(first, last):
+            value = stencil(weights(wx, x), lambda k: columns[(x + k) // CX][pl.ds((x + k) % CX * count + t, block), :])
+            middle[x, ts, :] = stencil(weights(wy, x), lambda k: value if k == 3 else pltpu.roll(value, (3 - k) % NY, 1))
+        for x in range(CX if third is not None else 0):
+            third[x, ts, :] = stencil(weights(wx, x + HALO), lambda k: middle[x + k, ts, :])
+
+
+def token_kernel(first, second, token):
+    token[...] = jnp.zeros_like(token)
+
+
+def gate_kernel(*refs):
+    pass
+
+
+def early_kernel(flag, tracers, h1, h2, wx, wy, third, s1, s2, middle, sems):
     def copies(l):
-        return [
-            pltpu.make_async_copy(tracers.at[start + l], wide.at[l, pl.ds(size, size)], sems.at[l, 0]),
-            pltpu.make_async_copy(level(first, l), wide.at[l, pl.ds(first_at, size)], sems.at[l, 1]),
-            pltpu.make_async_copy(level(second, l), wide.at[l, pl.ds(second_at, size)], sems.at[l, 2]),
-        ]
-
-    for l in range(wide.shape[0]):
+        return [pltpu.make_async_copy(h.at[l], s.at[l], sems.at[l, i]) for i, (h, s) in enumerate(((h1, s1), (h2, s2)))]
+
+    for l in range(s1.shape[0]):
         for copy in copies(l):
             copy.start()
-    return copies
-
-
-def sweep_levels(start, copies, wide, wx, wy, middle, third, third_at):
-    count, block = middle.shape[1], 32
-
-    def column(l, x, t):
-        if not isinstance(wide, tuple):
-            return wide[l, pl.ds(x * count + t, block), :]
-        return wide[x // CX][l + (start if x // CX == 1 else 0), pl.ds(x % CX * count + t, block), :]
-
-    def level(l, carry):
-        for copy in copies(l) if copies else ():
+
+    def level(left, right, l):
+        for copy in copies(l):
             copy.wait()
-        row = (start + l) * WIDE
-
-        def weight(ref, x, k):
-            return ref[pl.ds((row + x) * 8 + k, 1), :]
-
-        for t in range(0, count, block):
-            ts = pl.ds(t, block)
-            for x in range(WIDE):
-                value = None
-                for k in range(7):
-                    part = weight(wx, x, k) * column(l, x + k, t)
-                    value = part if value is None else value + part
-                moved = None
-                for k in range(7):
-                    q = value if k == 3 else pltpu.roll(value, (3 - k) % NY, 1)
-                    part = weight(wy, x, k) * q
-                    moved = part if moved is None else moved + part
-                middle[x, ts, :] = moved
-            for x in range(CX):
-                value = None
-                for k in range(7):
-                    part = weight(wx, x + HALO, k) * middle[x + k, ts, :]
-                    value = part if value is None else value + part
-                third[third_at + l, x, ts, :] = value
-        return carry
-
-    lax.fori_loop(0, wide[0].shape[0] if isinstance(wide, tuple) else wide.shape[0], level, 0)
-
-
-def token_kernel(first, second, token):
-    token[...] = jnp.zeros_like(token)
-
-
-def gate_kernel(*refs):
-    pass
-
-
-def early_kernel(flag, tracers, h1, h2, wx, wy, third, wide, middle, sems):
-    copies = start_wide(flag, 0, tracers, h1, h2, wide, sems)
-    sweep_levels(0, copies, wide, wx, wy, middle, third, 0)
-
-
-def late_kernel(flag, tracers, h1, h2, wx, wy, fields, early, out, middle, third):
-    done, count, block = early.shape[0], early.shape[2], 32
+        sweeps(l, (left.at[l], tracers.at[l], right.at[l]), 0, WIDE, wx, wy, middle, third.at[l])
 
     @pl.when(flag[0] == 1)
     def _():
-        sweep_levels(done, None, (h1, tracers, h2), wx, wy, middle, third, 0)
+        pl.loop(0, s1.shape[0])(functools.partial(level, s1, s2))
 
     @pl.when(flag[0] == 0)
     def _():
-        sweep_levels(done, None, (h2, tracers, h1), wx, wy, middle, third, 0)
+        pl.loop(0, s1.shape[0])(functools.partial(level, s2, s1))
+
+
+def late_kernel(flag, tracers, h1, h2, wx, wy, fields, early, out, s1, middle, third, sems):
+    done, count, block = early.shape[0], early.shape[2], 32
+    late = s1.shape[0]
+
+    def copy(l):
+        return pltpu.make_async_copy(h1.at[l], s1.at[l], sems.at[l])
+
+    for l in range(late):
+        copy(l).start()
+
+    def ready_side(left, right, first, last, l):
+        sweeps(done + l, (left.at[l], tracers.at[done + l], right.at[l]), first, last, wx, wy, middle.at[l], None)
+
+    def other_side(left, right, first, last, l):
+        copy(l).wait()
+        sweeps(done + l, (left.at[l], tracers.at[done + l], right.at[l]), first, last, wx, wy, middle.at[l], third.at[l])
+
+    @pl.when(flag[0] == 1)
+    def _():
+        pl.loop(0, late)(functools.partial(ready_side, s1, h2, CX, WIDE))
+        pl.loop(0, late)(functools.partial(other_side, s1, h2, 0, CX))
+
+    @pl.when(flag[0] == 0)
+    def _():
+        pl.loop(0, late)(functools.partial(ready_side, h2, s1, 0, CX))
+        pl.loop(0, late)(functools.partial(other_side, h2, s1, CX, WIDE))
 
     for x in range(CX):
         for t in range(0, count, block):
@@ -317,8 +317,7 @@
 def per_device(tracers, hour_fields, reader_table):
     cells, mine = lax.axis_index("cells"), lax.axis_index("tracers")
     n = lax.axis_size("cells")
-    reader = reader_table[0]
-    odd = (cells % 2).astype(jnp.int32)[None]
+    odd = (cells & 1).astype(jnp.int32)[None]
     state = jnp.transpose(tracers, (1, 2, 0, 3))
     count = state.shape[2]
     raw = hour_fields.reshape(NF * ROWS, NY)
@@ -327,6 +326,11 @@
     early, late = a_levels + c_levels, LEV - a_levels - c_levels
     flat = state.reshape(LEV, CX * count, NY)
 
+    def other_core(value):
+        return swap(value, "tracers", lambda i, n: i ^ 1)
+
+    far = swap(raw, "tracers", lambda i, n: i ^ 2)
+    near = other_core(raw)
     def other_core(value):
         return swap(value, "tracers", lambda i, n: i ^ 1)
 
@@ -337,15 +341,26 @@
         shape = (levels, CX * count, NY)
         return call(kernel, [ANY] * (1 + len(after)), [shape], [ANY], [pltpu.SemaphoreType.DMA((levels,))])(in_hbm(flat), *after)[0]
 
-    chunk = split(0, a_levels)
+    chunk = call(
+        functools.partial(split_kernel, 0),
+        [ANY],
+        [(a_levels, CX * count, NY)],
+        [ANY],
+        [pltpu.SemaphoreType.DMA((a_levels,))],
+    )(in_hbm(flat))[0]
     a1 = swap(chunk, "cells", even_pairs)
     a2 = swap(chunk, "cells", odd_pairs)
+    rest, mask = call(
+        functools.partial(split_mask_kernel, early),
+        [SMEM, SMEM, ANY],
+        [(late, CX * count, NY), jax.ShapeDtypeStruct((16, NY), jnp.int32)],
+        [ANY, VMEM],
+        [pltpu.SemaphoreType.DMA((late,))],
+    )(reader_table, mine.astype(jnp.int32)[None], in_hbm(flat))
+    far = call(gate_kernel, [ANY, ANY], [far.shape], [ANY], aliases={0: 0})(far, rest)[0]
     across = other_core(far)
-    same_core = (reader % 2 == mine % 2).astype(jnp.int32)[None]
-    same_chip = (reader // 2 == mine // 2).astype(jnp.int32)[None]
-    rest = split(early, late, far)
-    fields, message = call(merge_kernel, [SMEM, SMEM, VMEM, VMEM, VMEM, VMEM, ANY], [(NF * ROWS, NY), (3 * ROWS, NY)], cost=work(MERGE_FLOPS))(
-        same_core, same_chip, raw, near, far, across, rest
+    fields, message = call(merge_kernel, [VMEM] * 5, [(NF * ROWS, NY), (3 * ROWS, NY)], cost=work(MERGE_FLOPS))(
+        mask, raw, near, far, across
     )
     c1 = swap(message, "cells", even_pairs)
     c2 = swap(message, "cells", odd_pairs)
@@ -362,27 +377,30 @@
     received = lax.all_to_all(masses, "cells", 0, 0, tiled=True)
     third = call(
         early_kernel,
-        [SMEM, ANY, ANY, ANY, VMEM, VMEM],
+        [SMEM, VMEM, ANY, ANY, VMEM, VMEM],
         [(early, CX, count, NY)],
         None,
         [
-            pltpu.VMEM((early, 3 * CX * count, NY), F32),
+            pltpu.VMEM((early, CX * count, NY), F32),
+            pltpu.VMEM((early, CX * count, NY), F32),
             pltpu.VMEM((WIDE, count, NY), F32),
-            pltpu.SemaphoreType.DMA((early, 3)),
+            pltpu.SemaphoreType.DMA((early, 2)),
         ],
         cost=work(KA_FLOPS),
     )(odd, flat, in_hbm(a1), in_hbm(a2), wx, wy)[0]
     diffused = call(
         late_kernel,
-        [SMEM] + [VMEM] * 7,
+        [SMEM, VMEM, ANY] + [VMEM] * 5,
         [(LEV, CX, count, NY)],
         None,
         [
-            pltpu.VMEM((WIDE, count, NY), F32),
+            pltpu.VMEM((late, CX * count, NY), F32),
+            pltpu.VMEM((late, WIDE, count, NY), F32),
             pltpu.VMEM((late, CX, count, NY), F32),
+            pltpu.SemaphoreType.DMA((late,)),
         ],
         cost=work(KB_FLOPS),
-    )(odd, flat, in_vmem(b1), in_vmem(b2), wx, wy, fields, third)[0]
+    )(odd, flat, in_hbm(b1), in_vmem(b2), wx, wy, fields, third)[0]
     out = call(
         scale_kernel,
         [VMEM, VMEM],

time: 49.9 us -> 47.6 us (0.954); the launches traced: 49.1 us -> 47.3 us
  Pallas kernels: 12.3 us -> 11.3 us
  starting transfers between devices: 24.7 us -> 24 us
    pallas_call x5 -> x6, Pallas kernels: 9.5 us -> 8.48 us  [the longest x1 3.56 us: per_device(): call(late_kernel, [SMEM, VMEM, ANY] + [VMEM] * 5, [(LEV, CX, count, NY)],...]
    ppermute x9, starting transfers between devices: 18 us -> 17 us  [swap(): return lax.ppermute(value, axis, [(i, partner(i, n)) for i in range(n)])]
  transfers between devices with their start and end apart: 10 -> 10, of which waited for: 4 -> 4; matrix products, arithmetic and copies ran while one was open for 0% -> 0% of each run, Pallas kernels for 22% -> 21%
where the time goes in v4:
time: 47.6 us; the launch traced here: 47.3 us
  starting transfers between devices  24 us (50%)
  Pallas kernels  11.3 us (24%)
  waiting for transfers between devices  9.42 us (20%)
  local copies, waits for them, and re-layouts  1.93 us (4%)
  between operations  0.75 us (2%)
    ppermute x9, starting transfers between devices, swap(): return lax.ppermute(value, axis, [(i, partner(i, n)) for i in range(n)])  17 us
    ppermute x9, waiting for transfers between devices, swap(): return lax.ppermute(value, axis, [(i, partner(i, n)) for i in range(n)])  9.42 us
    all_to_all x1, starting transfers between devices, per_device(): received = lax.all_to_all(masses, 'cells', 0, 0, tiled=True)  6.92 us
    pallas_call x1, Pallas kernels, per_device(): call(late_kernel, [SMEM, VMEM, ANY] + [VMEM] * 5, [(LEV, CX, count, NY)],...  3.56 us
    pallas_call x1, Pallas kernels, per_device(): call(early_kernel, [SMEM, VMEM, ANY, ANY, VMEM, VMEM], [(early, CX, count...  2.52 us
    unnamed x12, local copies, waits for them, and re-layouts  1.93 us
    pallas_call x1, Pallas kernels, per_device(): call(weights_kernel, [SMEM, VMEM, VMEM, VMEM, VMEM, VMEM, ANY], [pltpu.HB...  1.48 us
    pallas_call x1, Pallas kernels, per_device(): call(scale_kernel, [VMEM, VMEM], [(LEV, CX, count, NY)], [HBM], [pltpu.VM...  1.29 us
  transfers between devices with their start and end apart: 10, of which 4 were waited for; matrix products, arithmetic and copies ran while one was open for 0% of the time, Pallas kernels for 21%

profile of v4, /device:TPU:16, one launch (start us, length us, event | category | flops | bytes accessed | tf_op | source)
XLA Modules:
  0.0 47.3 jit_solution(4656292313717562637)
XLA Ops:
  0.0 0.0 copy-start.5
  0.0 2.1 %collective-permute-start.1 = (f32[360,128]{1,0:T(8,128)}, f32[360,128]{1,0:T(8,128)S(1)}, u32[]{:S(2)}, u32[]{:S(2)}) collective-permute-start(f32[360,128]{1,0:T(8,128)} %bitcast.16), channel_id=1, source_target_pairs={{0,2},{1,3},{2,0},{3,1},{4,6},{5,7},{6,4},{7,5},{8,10},{9,11},{10,... | collective-permute-start | bytes 552968 | tf_op jit(solution)/shard_map/ppermute | solution.py:306
  2.1 1.0 %shard_map.40 = f32[2,384,128]{2,1,0:T(8,128)S(1)} custom-call(f32[6,384,128]{2,1,0:T(8,128)} %bitcast.11), custom_call_target="tpu_custom_call" | custom-call | tf_op jit(solution)/shard_map/pallas_call | solution.py:344
  3.1 8.0 %collective-permute-start.6 = (f32[2,384,128]{2,1,0:T(8,128)S(1)}, f32[2,384,128]{2,1,0:T(8,128)}, u32[]{:S(2)}, u32[]{:S(2)}) collective-permute-start(f32[2,384,128]{2,1,0:T(8,128)S(1)} %shard_map.40), channel_id=1, source_target_pairs={{0,252},{4,8},{8,4},{12,16},{16,12},{20,24},{24,20},{28,32},{32,28... | collective-permute-start | bytes 1179656 | tf_op jit(solution)/shard_map/ppermute | solution.py:306
  11.1 0.0 collective-permute-start.5
  11.1 0.0 copy-done.5
  11.1 0.0 collective-permute-start
  11.8 1.3 %shard_map.37 = (f32[4,384,128]{2,1,0:T(8,128)S(1)}, s32[16,128]{1,0:T(8,128)S(1)}) custom-call(s32[1]{0:T(128)S(6)} %copy.9.reader, s32[1]{0:T(128)} %bitcast.1.mine, f32[6,384,128]{2,1,0:T(8,128)} %bitcast.12), custom_call_target="tpu_custom_call" | custom-call | tf_op jit(solution)/shard_map/pallas_call | solution.py:353
  13.1 0.0 collective-permute-done.1.refs_0_
  13.1 0.6 %collective-permute-start.2 = (f32[360,128]{1,0:T(8,128)S(1)}, f32[360,128]{1,0:T(8,128)S(1)}, u32[]{:S(2)}, u32[]{:S(2)}) collective-permute-start(f32[360,128]{1,0:T(8,128)S(1)} %shard_map.38.far), channel_id=1, source_target_pairs={{0,1},{1,0},{2,3},{3,2},{4,5},{5,4},{6,7},{7,6},{8,9},{9,8},{10,11... | collective-permute-start | bytes 552968 | tf_op jit(solution)/shard_map/ppermute | solution.py:306
  13.7 0.0 collective-permute-done.near
  13.7 1.1 %collective-permute-done.2.across = f32[360,128]{1,0:T(8,128)S(1)} collective-permute-done((f32[360,128]{1,0:T(8,128)S(1)}, f32[360,128]{1,0:T(8,128)S(1)}, u32[]{:S(2)}, u32[]{:S(2)}) %collective-permute-start.2) | collective-permute-done | bytes 184352 | tf_op jit(solution)/shard_map/ppermute | solution.py:306
  14.7 0.1 shard_map.39
  14.8 3.6 %collective-permute-start.4 = (f32[108,128]{1,0:T(8,128)S(1)}, f32[108,128]{1,0:T(8,128)S(1)}, u32[]{:S(2)}, u32[]{:S(2)}) collective-permute-start(f32[108,128]{1,0:T(8,128)S(1)} %get-tuple-element.14.own.refs_1_), channel_id=1, source_target_pairs={{0,252},{4,8},{8,4},{12,16},{16,12},{20,24},{24,20},{28,32},{32,28... | collective-permute-start | bytes 165896 | tf_op jit(solution)/shard_map/ppermute | solution.py:306
  18.5 0.0 collective-permute-start.3
  18.5 0.0 copy-start
  18.5 2.7 %collective-permute-start.8 = (f32[4,384,128]{2,1,0:T(8,128)S(1)}, f32[4,384,128]{2,1,0:T(8,128)S(1)}, u32[]{:S(2)}, u32[]{:S(2)}) collective-permute-start(f32[4,384,128]{2,1,0:T(8,128)S(1)} %shard_map.43), channel_id=1, source_target_pairs={{0,252},{4,8},{8,4},{12,16},{16,12},{20,24},{24,20},{28,32},{32,28... | collective-permute-start | bytes 2359304 | tf_op jit(solution)/shard_map/ppermute | solution.py:306
  21.2 0.0 collective-permute-done.6.second.h2
  21.2 0.0 collective-permute-start.7
  21.2 0.8 %collective-permute-done.5.first.h1 = f32[2,384,128]{2,1,0:T(8,128)} collective-permute-done((f32[2,384,128]{2,1,0:T(8,128)S(1)}, f32[2,384,128]{2,1,0:T(8,128)}, u32[]{:S(2)}, u32[]{:S(2)}) %collective-permute-start.5) | collective-permute-done | bytes 393248 | tf_op jit(solution)/shard_map/ppermute | solution.py:306
  22.0 1.4 %collective-permute-done.4.second = f32[108,128]{1,0:T(8,128)S(1)} collective-permute-done((f32[108,128]{1,0:T(8,128)S(1)}, f32[108,128]{1,0:T(8,128)S(1)}, u32[]{:S(2)}, u32[]{:S(2)}) %collective-permute-start.4) | collective-permute-done | bytes 55328 | tf_op jit(solution)/shard_map/ppermute | solution.py:306
  23.3 0.0 collective-permute-done.3.first
  23.3 0.0 copy-done
  23.3 1.5 %shard_map.42 = (f32[576,128]{1,0:T(8,128)}, f32[576,128]{1,0:T(8,128)}, f32[64,128]{1,0:T(8,128)}) custom-call(s32[1]{0:T(128)} %bitcast.flag, f32[108,128]{1,0:T(8,128)S(1)} %get-tuple-element.14.own.refs_1_, f32[108,128]{1,0:T(8,128)S(1)} %collective-permute-done.3.first, f32[108,128]{1,0:T(8,128)S(1)} %collective-permute-done.4.second, ...), custom_call_target="tpu_custom_call" | custom-call | tf_op jit(solution)/shard_map/pallas_call | solution.py:372
  24.8 6.9 %all-to-all-start = ((f32[64,1,128]{2,1,0:T(1,128)}), f32[64,1,128]{2,1,0:T(1,128)S(1)}, u32[]{:S(2)}, u32[]{:S(2)}) async-start(f32[64,1,128]{2,1,0:T(1,128)} %bitcast.7), calls=%async_computation | async-start | bytes 65536 | tf_op jit(solution)/shard_map/all_to_all | solution.py:377
  31.7 0.0 copy-start.1
  31.8 1.0 %copy-done.1 = f32[576,128]{1,0:T(8,128)S(1)} copy-done((f32[576,128]{1,0:T(8,128)S(1)}, f32[576,128]{1,0:T(8,128)}, u32[]{:S(2)}) %copy-start.1) | copy-done | bytes 294936
  32.7 0.0 copy-start.3
  32.7 1.0 %copy-done.3 = f32[576,128]{1,0:T(8,128)S(1)} copy-done((f32[576,128]{1,0:T(8,128)S(1)}, f32[576,128]{1,0:T(8,128)}, u32[]{:S(2)}) %copy-start.3) | copy-done | bytes 294936
  33.7 0.0 copy-start.2
  33.7 0.0 copy-start.4
  33.7 2.5 %shard_map.44.early = f32[2,6,64,128]{3,2,1,0:T(8,128)S(1)} custom-call(s32[1]{0:T(128)} %bitcast.flag, f32[6,384,128]{2,1,0:T(8,128)S(1)} %bitcast.14, f32[2,384,128]{2,1,0:T(8,128)} %collective-permute-done.5.first.h1, f32[2,384,128]{2,1,0:T(8,128)} %collective-permute-done.6.second.h2, f32[576,128]{1,0:T(8,128)S(1)} %copy-done.1, f32[576,128]{1,0:T(8,128)S(1)} %copy-done.3), custom_call_target="tpu_custom_call" | custom-call | flops 10000000000 | tf_op jit(solution)/shard_map/pallas_call | solution.py:378
  36.2 6.2 %collective-permute-done.8.h2 = f32[4,384,128]{2,1,0:T(8,128)S(1)} collective-permute-done((f32[4,384,128]{2,1,0:T(8,128)S(1)}, f32[4,384,128]{2,1,0:T(8,128)S(1)}, u32[]{:S(2)}, u32[]{:S(2)}) %collective-permute-start.8) | collective-permute-done | bytes 786464 | tf_op jit(solution)/shard_map/ppermute | solution.py:306
  42.4 0.0 collective-permute-done.7.h1
  42.4 0.0 copy-done.2
  42.4 0.0 copy-done.4
  42.4 3.6 %shard_map.45.diffused = f32[6,6,64,128]{3,2,1,0:T(8,128)S(1)} custom-call(s32[1]{0:T(128)} %bitcast.flag, f32[6,384,128]{2,1,0:T(8,128)S(1)} %bitcast.15, f32[4,384,128]{2,1,0:T(8,128)} %collective-permute-done.7.h1, f32[4,384,128]{2,1,0:T(8,128)S(1)} %collective-permute-done.8.h2, f32[576,128]{1,0:T(8,128)S(1)} %copy-done.2, f32[576,128]{1,0:T(8,128)S(1)} %copy-done.4, ...), custom_call_target="tpu_custom_call" | custom-call | tf_op jit(solution)/shard_map/pallas_call | solution.py:391
  46.0 0.0 all-to-all-done
  46.0 1.3 %shard_map.46 = f32[6,6,64,128]{3,2,1,0:T(8,128)} custom-call(f32[64,128]{1,0:T(8,128)S(1)} %bitcast.19, f32[6,6,64,128]{3,2,1,0:T(8,128)S(1)} %shard_map.45.diffused), custom_call_target="tpu_custom_call" | custom-call | tf_op jit(solution)/shard_map/pallas_call | solution.py:404
  (3 shorter events, 0.0 us)
Async XLA Ops:
  0.0 11.1 %copy-start.5 = (f32[1,10,6,6,128]{4,0,3,2,1:T(1,128)S(1)}, f32[1,10,6,6,128]{4,0,3,2,1:T(1,128)}, u32[]{:S(2)}) copy-start(f32[1,10,6,6,128]{4,0,3,2,1:T(1,128)} %param.4) | copy-start | bytes 552964
  0.0 13.1 %collective-permute-start.1 = (f32[360,128]{1,0:T(8,128)}, f32[360,128]{1,0:T(8,128)S(1)}, u32[]{:S(2)}, u32[]{:S(2)}) collective-permute-start(f32[360,128]{1,0:T(8,128)} %bitcast.16), channel_id=1, source_target_pairs={{0,2},{1,3},{2,0},{3,1},{4,6},{5,7},{6,4},{7,5},{8,10},{9,11},{10,... | collective-permute-start | bytes 552968 | tf_op jit(solution)/shard_map/ppermute | solution.py:306
  3.1 18.1 %collective-permute-start.6 = (f32[2,384,128]{2,1,0:T(8,128)S(1)}, f32[2,384,128]{2,1,0:T(8,128)}, u32[]{:S(2)}, u32[]{:S(2)}) collective-permute-start(f32[2,384,128]{2,1,0:T(8,128)S(1)} %shard_map.40), channel_id=1, source_target_pairs={{0,252},{4,8},{8,4},{12,16},{16,12},{20,24},{24,20},{28,32},{32,28... | collective-permute-start | bytes 1179656 | tf_op jit(solution)/shard_map/ppermute | solution.py:306
  11.1 10.8 %collective-permute-start.5 = (f32[2,384,128]{2,1,0:T(8,128)S(1)}, f32[2,384,128]{2,1,0:T(8,128)}, u32[]{:S(2)}, u32[]{:S(2)}) collective-permute-start(f32[2,384,128]{2,1,0:T(8,128)S(1)} %shard_map.40), channel_id=1, source_target_pairs={{0,4},{4,0},{8,12},{12,8},{16,20},{20,16},{24,28},{28,24},{32,36},... | collective-permute-start | bytes 1179656 | tf_op jit(solution)/shard_map/ppermute | solution.py:306
  11.1 2.5 %collective-permute-start = (f32[360,128]{1,0:T(8,128)S(1)}, f32[360,128]{1,0:T(8,128)S(1)}, u32[]{:S(2)}, u32[]{:S(2)}) collective-permute-start(f32[360,128]{1,0:T(8,128)S(1)} %bitcast.17), channel_id=1, source_target_pairs={{0,1},{1,0},{2,3},{3,2},{4,5},{5,4},{6,7},{7,6},{8,9},{9,8},{10,11... | collective-permute-start | bytes 552968 | tf_op jit(solution)/shard_map/ppermute | solution.py:306
  13.1 1.6 %collective-permute-start.2 = (f32[360,128]{1,0:T(8,128)S(1)}, f32[360,128]{1,0:T(8,128)S(1)}, u32[]{:S(2)}, u32[]{:S(2)}) collective-permute-start(f32[360,128]{1,0:T(8,128)S(1)} %shard_map.38.far), channel_id=1, source_target_pairs={{0,1},{1,0},{2,3},{3,2},{4,5},{5,4},{6,7},{7,6},{8,9},{9,8},{10,11... | collective-permute-start | bytes 552968 | tf_op jit(solution)/shard_map/ppermute | solution.py:306
  14.8 8.5 %collective-permute-start.4 = (f32[108,128]{1,0:T(8,128)S(1)}, f32[108,128]{1,0:T(8,128)S(1)}, u32[]{:S(2)}, u32[]{:S(2)}) collective-permute-start(f32[108,128]{1,0:T(8,128)S(1)} %get-tuple-element.14.own.refs_1_), channel_id=1, source_target_pairs={{0,252},{4,8},{8,4},{12,16},{16,12},{20,24},{24,20},{28,32},{32,28... | collective-permute-start | bytes 165896 | tf_op jit(solution)/shard_map/ppermute | solution.py:306
  18.5 4.9 %collective-permute-start.3 = (f32[108,128]{1,0:T(8,128)S(1)}, f32[108,128]{1,0:T(8,128)S(1)}, u32[]{:S(2)}, u32[]{:S(2)}) collective-permute-start(f32[108,128]{1,0:T(8,128)S(1)} %get-tuple-element.14.own.refs_1_), channel_id=1, source_target_pairs={{0,4},{4,0},{8,12},{12,8},{16,20},{20,16},{24,28},{28,24},{32,36},... | collective-permute-start | bytes 165896 | tf_op jit(solution)/shard_map/ppermute | solution.py:306
  18.5 4.9 %copy-start = (f32[64,6,6,128]{3,0,2,1:T(8,128)S(1)}, f32[64,6,6,128]{3,0,2,1:T(8,128)}, u32[]{:S(2)}) copy-start(f32[64,6,6,128]{3,0,2,1:T(8,128)} %param.3) | copy-start | bytes 3538948
  18.5 23.9 %collective-permute-start.8 = (f32[4,384,128]{2,1,0:T(8,128)S(1)}, f32[4,384,128]{2,1,0:T(8,128)S(1)}, u32[]{:S(2)}, u32[]{:S(2)}) collective-permute-start(f32[4,384,128]{2,1,0:T(8,128)S(1)} %shard_map.43), channel_id=1, source_target_pairs={{0,252},{4,8},{8,4},{12,16},{16,12},{20,24},{24,20},{28,32},{32,28... | collective-permute-start | bytes 2359304 | tf_op jit(solution)/shard_map/ppermute | solution.py:306
  21.2 21.2 %collective-permute-start.7 = (f32[4,384,128]{2,1,0:T(8,128)S(1)}, f32[4,384,128]{2,1,0:T(8,128)}, u32[]{:S(2)}, u32[]{:S(2)}) collective-permute-start(f32[4,384,128]{2,1,0:T(8,128)S(1)} %shard_map.43), channel_id=1, source_target_pairs={{0,4},{4,0},{8,12},{12,8},{16,20},{20,16},{24,28},{28,24},{32,36},... | collective-permute-start | bytes 2359304 | tf_op jit(solution)/shard_map/ppermute | solution.py:306
  24.8 21.2 %all-to-all-start = ((f32[64,1,128]{2,1,0:T(1,128)}), f32[64,1,128]{2,1,0:T(1,128)S(1)}, u32[]{:S(2)}, u32[]{:S(2)}) async-start(f32[64,1,128]{2,1,0:T(1,128)} %bitcast.7), calls=%async_computation | async-start | bytes 65536 | tf_op jit(solution)/shard_map/all_to_all | solution.py:377
  31.7 1.0 %copy-start.1 = (f32[576,128]{1,0:T(8,128)S(1)}, f32[576,128]{1,0:T(8,128)}, u32[]{:S(2)}) copy-start(f32[576,128]{1,0:T(8,128)} %get-tuple-element.17.wx) | copy-start | bytes 884740
  32.7 1.0 %copy-start.3 = (f32[576,128]{1,0:T(8,128)S(1)}, f32[576,128]{1,0:T(8,128)}, u32[]{:S(2)}) copy-start(f32[576,128]{1,0:T(8,128)} %get-tuple-element.18.wy) | copy-start | bytes 884740
  33.7 8.8 %copy-start.2 = (f32[576,128]{1,0:T(8,128)S(1)}, f32[576,128]{1,0:T(8,128)}, u32[]{:S(2)}) copy-start(f32[576,128]{1,0:T(8,128)} %get-tuple-element.17.wx) | copy-start | bytes 884740
  33.7 8.8 %copy-start.4 = (f32[576,128]{1,0:T(8,128)S(1)}, f32[576,128]{1,0:T(8,128)}, u32[]{:S(2)}) copy-start(f32[576,128]{1,0:T(8,128)} %get-tuple-element.18.wy) | copy-start | bytes 884740

commit v5 on v4

--- a/solution.py
+++ b/solution.py
@@ -83,15 +83,8 @@
         move.wait()
 
 
-def split_mask_kernel(start, reader, mine, tracers, part, mask, sems):
-    differ = reader[0] ^ mine[0]
-    mask[pl.ds(0, 8), :] = jnp.full((8, NY), differ & 1, jnp.int32)
-    mask[pl.ds(8, 8), :] = jnp.full((8, NY), differ >> 1, jnp.int32)
-    split_kernel(start, tracers, part, sems)
-
-
-def merge_kernel(mask, own, near, far, across, fields, message):
-    core, chip = mask[pl.ds(0, 1), :] == 0, mask[pl.ds(8, 1), :] == 0
+def merge_kernel(core_differs, chip_differs, own, near, far, across, fields, message):
+    core, chip = core_differs[0] == 0, chip_differs[0] == 0
     here = jnp.where(core, own[...], near[...])
     there = jnp.where(core, far[...], across[...])
     fields[...] = jnp.where(chip, here, there)
@@ -213,8 +206,7 @@
         pl.loop(0, s1.shape[0])(functools.partial(level, s2, s1))
 
 
-def late_kernel(flag, tracers, h1, h2, wx, wy, fields, early, out, s1, middle, third, sems):
-    done, count, block = early.shape[0], early.shape[2], 32
+def late_kernel(done, flag, tracers, h1, h2, wx, wy, third, s1, middle, sems):
     late = s1.shape[0]
 
     def copy(l):
@@ -240,31 +232,27 @@
         pl.loop(0, late)(functools.partial(ready_side, h2, s1, 0, CX))
         pl.loop(0, late)(functools.partial(other_side, h2, s1, CX, WIDE))
 
-    for x in range(CX):
-        for t in range(0, count, block):
-            ts = pl.ds(t, block)
-            levels = [early[m, x, ts, :] if m < done else third[m - done, x, ts, :] for m in range(LEV)]
-            for l in range(LEV):
-                value = None
-                for m in range(LEV):
-                    part = fields[pl.ds((4 + l) * ROWS + m * CX + x, 1), :] * levels[m]
-                    value = part if value is None else value + part
-                out[l, x, ts, :] = value
-
-
-def scale_kernel(received, diffused, out, scaled, sems):
-    count = diffused.shape[2]
+
+def mix_kernel(received, fields, early, late, out, scaled, sems):
+    done, count, block = early.shape[0], early.shape[2], 32
     total = jnp.sum(received[...], axis=0, keepdims=True)
     ratio = total / pltpu.roll(jnp.broadcast_to(total, (8, NY)), NY // 2, 1)[:1]
     lane = lax.broadcasted_iota(jnp.int32, (count, NY), 1)
     row = lax.broadcasted_iota(jnp.int32, (count, NY), 0)
     scale = jnp.sum(jnp.where(lane == row, jnp.broadcast_to(ratio, (count, NY)), 0.0), axis=1, keepdims=True)
     factor = jnp.broadcast_to(scale, (count, NY))
-    moves = [pltpu.make_async_copy(scaled.at[l], out.at[l], sems.at[l]) for l in range(LEV)]
-    for l in range(LEV):
-        for x in range(CX):
-            scaled[l, x] = diffused[l, x] * factor
-        moves[l].start()
+    moves = [pltpu.make_async_copy(scaled.at[x], out.at[:, x], sems.at[x]) for x in range(CX)]
+    for x in range(CX):
+        for t in range(0, count, block):
+            ts = pl.ds(t, block)
+            levels = [early[m, x, ts, :] if m < done else late[m - done, x, ts, :] for m in range(LEV)]
+            for l in range(LEV):
+                value = None
+                for m in range(LEV):
+                    part = fields[pl.ds((4 + l) * ROWS + m * CX + x, 1), :] * levels[m]
+                    value = part if value is None else value + part
+                scaled[x, l, ts, :] = value * factor[t : t + block]
+        moves[x].start()
     for move in moves:
         move.wait()
 
@@ -350,17 +338,19 @@
     )(in_hbm(flat))[0]
     a1 = swap(chunk, "cells", even_pairs)
     a2 = swap(chunk, "cells", odd_pairs)
-    rest, mask = call(
-        functools.partial(split_mask_kernel, early),
-        [SMEM, SMEM, ANY],
-        [(late, CX * count, NY), jax.ShapeDtypeStruct((16, NY), jnp.int32)],
-        [ANY, VMEM],
+    rest = call(
+        functools.partial(split_kernel, early),
+        [ANY],
+        [(late, CX * count, NY)],
+        [ANY],
         [pltpu.SemaphoreType.DMA((late,))],
-    )(reader_table, mine.astype(jnp.int32)[None], in_hbm(flat))
+    )(in_hbm(flat))[0]
     far = call(gate_kernel, [ANY, ANY], [far.shape], [ANY], aliases={0: 0})(far, rest)[0]
     across = other_core(far)
-    fields, message = call(merge_kernel, [VMEM] * 5, [(NF * ROWS, NY), (3 * ROWS, NY)], cost=work(MERGE_FLOPS))(
-        mask, raw, near, far, across
+    differ = reader_table ^ mine.astype(jnp.int32)
+    core_differs, chip_differs = differ & 1, differ >> 1
+    fields, message = call(merge_kernel, [SMEM] * 2 + [VMEM] * 4, [(NF * ROWS, NY), (3 * ROWS, NY)], cost=work(MERGE_FLOPS))(
+        core_differs, chip_differs, raw, near, far, across
     )
     c1 = swap(message, "cells", even_pairs)
     c2 = swap(message, "cells", odd_pairs)
@@ -388,26 +378,25 @@
         ],
         cost=work(KA_FLOPS),
     )(odd, flat, in_hbm(a1), in_hbm(a2), wx, wy)[0]
-    diffused = call(
-        late_kernel,
-        [SMEM, VMEM, ANY] + [VMEM] * 5,
-        [(LEV, CX, count, NY)],
+    rest_third = call(
+        functools.partial(late_kernel, early),
+        [SMEM, VMEM, ANY, VMEM, VMEM, VMEM],
+        [(late, CX, count, NY)],
         None,
         [
             pltpu.VMEM((late, CX * count, NY), F32),
             pltpu.VMEM((late, WIDE, count, NY), F32),
-            pltpu.VMEM((late, CX, count, NY), F32),
             pltpu.SemaphoreType.DMA((late,)),
         ],
         cost=work(KB_FLOPS),
-    )(odd, flat, in_hbm(b1), in_vmem(b2), wx, wy, fields, third)[0]
+    )(odd, flat, in_hbm(b1), in_vmem(b2), wx, wy)[0]
     out = call(
-        scale_kernel,
-        [VMEM, VMEM],
+        mix_kernel,
+        [VMEM] * 4,
         [(LEV, CX, count, NY)],
         [HBM],
-        [pltpu.VMEM((LEV, CX, count, NY), F32), pltpu.SemaphoreType.DMA((LEV,))],
-    )(received, diffused)[0]
+        [pltpu.VMEM((CX, LEV, count, NY), F32), pltpu.SemaphoreType.DMA((CX,))],
+    )(received, fields, third, rest_third)[0]
     return jnp.transpose(out, (2, 0, 1, 3))
 
 

time: 47.6 us -> 47.2 us (level)
  starting transfers between devices: 24 us -> 24.7 us
  waiting for transfers between devices: 9.42 us -> 8.74 us
  Pallas kernels: 11.3 us -> 10.8 us
    ppermute x9, waiting for transfers between devices: 9.42 us -> 8.73 us  [swap(): return lax.ppermute(value, axis, [(i, partner(i, n)) for i in range(n)])]
    all_to_all x1, starting transfers between devices: 6.92 us -> 7.58 us  [per_device(): received = lax.all_to_all(masses, 'cells', 0, 0, tiled=True)]
    unnamed x12 -> x8, local copies, waits for them, and re-layouts: 1.93 us -> 1.93 us
  transfers between devices with their start and end apart: 10 -> 10, of which waited for: 4 -> 4; matrix products, arithmetic and copies ran while one was open for 0% -> 0% of each run, Pallas kernels for 21% -> 20%
where the time goes in v5:
time: 47.2 us; the launch traced here: 46.9 us
  starting transfers between devices  24.7 us (52%)
  Pallas kernels  10.8 us (23%)
  waiting for transfers between devices  8.74 us (19%)
  local copies, waits for them, and re-layouts  1.93 us (4%)
  between operations  0.75 us (2%)
    ppermute x9, starting transfers between devices, swap(): return lax.ppermute(value, axis, [(i, partner(i, n)) for i in range(n)])  17.1 us
    ppermute x9, waiting for transfers between devices, swap(): return lax.ppermute(value, axis, [(i, partner(i, n)) for i in range(n)])  8.73 us
    all_to_all x1, starting transfers between devices, per_device(): received = lax.all_to_all(masses, 'cells', 0, 0, tiled=True)  7.58 us
    pallas_call x1, Pallas kernels, per_device(): call(functools.partial(late_kernel, early), [SMEM, VMEM, ANY, VMEM, VMEM,...  3.18 us
    pallas_call x1, Pallas kernels, per_device(): call(early_kernel, [SMEM, VMEM, ANY, ANY, VMEM, VMEM], [(early, CX, count...  2.46 us
    unnamed x8, local copies, waits for them, and re-layouts  1.93 us
    pallas_call x1, Pallas kernels, per_device(): call(weights_kernel, [SMEM, VMEM, VMEM, VMEM, VMEM, VMEM, ANY], [pltpu.HB...  1.5 us
    pallas_call x1, Pallas kernels, per_device(): call(mix_kernel, [VMEM] * 4, [(LEV, CX, count, NY)], [HBM], [pltpu.VMEM((...  1.31 us
  transfers between devices with their start and end apart: 10, of which 4 were waited for; matrix products, arithmetic and copies ran while one was open for 0% of the time, Pallas kernels for 20%

profile of v5, /device:TPU:16, one launch (start us, length us, event | category | flops | bytes accessed | tf_op | source)
XLA Modules:
  0.0 46.9 jit_solution(14695248297965539636)
XLA Ops:
  0.0 0.0 copy-start.3
  0.0 2.1 %collective-permute-start.1 = (f32[360,128]{1,0:T(8,128)}, f32[360,128]{1,0:T(8,128)S(1)}, u32[]{:S(2)}, u32[]{:S(2)}) collective-permute-start(f32[360,128]{1,0:T(8,128)} %bitcast.16), channel_id=1, source_target_pairs={{0,2},{1,3},{2,0},{3,1},{4,6},{5,7},{6,4},{7,5},{8,10},{9,11},{10,... | collective-permute-start | bytes 552968 | tf_op jit(solution)/shard_map/ppermute | solution.py:294
  2.1 1.0 %shard_map.40 = f32[2,384,128]{2,1,0:T(8,128)S(1)} custom-call(f32[6,384,128]{2,1,0:T(8,128)} %bitcast.11), custom_call_target="tpu_custom_call" | custom-call | tf_op jit(solution)/shard_map/pallas_call | solution.py:332
  3.1 8.0 %collective-permute-start.6 = (f32[2,384,128]{2,1,0:T(8,128)S(1)}, f32[2,384,128]{2,1,0:T(8,128)}, u32[]{:S(2)}, u32[]{:S(2)}) collective-permute-start(f32[2,384,128]{2,1,0:T(8,128)S(1)} %shard_map.40), channel_id=1, source_target_pairs={{0,252},{4,8},{8,4},{12,16},{16,12},{20,24},{24,20},{28,32},{32,28... | collective-permute-start | bytes 1179656 | tf_op jit(solution)/shard_map/ppermute | solution.py:294
  11.1 0.0 collective-permute-start.5
  11.1 0.0 copy-done.3
  11.1 0.0 collective-permute-start
  11.2 1.3 %shard_map.37.refs_1_.refs_0_ = f32[4,384,128]{2,1,0:T(8,128)S(1)} custom-call(f32[6,384,128]{2,1,0:T(8,128)} %bitcast.12), custom_call_target="tpu_custom_call" | custom-call | tf_op jit(solution)/shard_map/pallas_call | solution.py:341
  12.4 0.0 collective-permute-done.1.refs_0_
  12.4 0.6 %collective-permute-start.2 = (f32[360,128]{1,0:T(8,128)S(1)}, f32[360,128]{1,0:T(8,128)S(1)}, u32[]{:S(2)}, u32[]{:S(2)}) collective-permute-start(f32[360,128]{1,0:T(8,128)S(1)} %shard_map.38.far), channel_id=1, source_target_pairs={{0,1},{1,0},{2,3},{3,2},{4,5},{5,4},{6,7},{7,6},{8,9},{9,8},{10,11... | collective-permute-start | bytes 552968 | tf_op jit(solution)/shard_map/ppermute | solution.py:294
  13.7 0.0 collective-permute-done.near
  13.7 0.4 collective-permute-done.2.across
  14.1 0.1 shard_map.39
  14.2 4.3 %collective-permute-start.4 = (f32[108,128]{1,0:T(8,128)S(1)}, f32[108,128]{1,0:T(8,128)S(1)}, u32[]{:S(2)}, u32[]{:S(2)}) collective-permute-start(f32[108,128]{1,0:T(8,128)S(1)} %get-tuple-element.10.own.refs_1_), channel_id=1, source_target_pairs={{0,252},{4,8},{8,4},{12,16},{16,12},{20,24},{24,20},{28,32},{32,28... | collective-permute-start | bytes 165896 | tf_op jit(solution)/shard_map/ppermute | solution.py:294
  18.5 0.0 collective-permute-start.3
  18.5 0.0 copy-start
  18.5 2.0 %collective-permute-start.8 = (f32[4,384,128]{2,1,0:T(8,128)S(1)}, f32[4,384,128]{2,1,0:T(8,128)S(1)}, u32[]{:S(2)}, u32[]{:S(2)}) collective-permute-start(f32[4,384,128]{2,1,0:T(8,128)S(1)} %shard_map.44), channel_id=1, source_target_pairs={{0,252},{4,8},{8,4},{12,16},{16,12},{20,24},{24,20},{28,32},{32,28... | collective-permute-start | bytes 2359304 | tf_op jit(solution)/shard_map/ppermute | solution.py:294
  20.5 0.0 collective-permute-done.6.second.h2
  20.5 0.1 collective-permute-start.7
  20.6 1.4 %collective-permute-done.5.first.h1 = f32[2,384,128]{2,1,0:T(8,128)} collective-permute-done((f32[2,384,128]{2,1,0:T(8,128)S(1)}, f32[2,384,128]{2,1,0:T(8,128)}, u32[]{:S(2)}, u32[]{:S(2)}) %collective-permute-start.5) | collective-permute-done | bytes 393248 | tf_op jit(solution)/shard_map/ppermute | solution.py:294
  22.0 0.7 %collective-permute-done.4.second = f32[108,128]{1,0:T(8,128)S(1)} collective-permute-done((f32[108,128]{1,0:T(8,128)S(1)}, f32[108,128]{1,0:T(8,128)S(1)}, u32[]{:S(2)}, u32[]{:S(2)}) %collective-permute-start.4) | collective-permute-done | bytes 55328 | tf_op jit(solution)/shard_map/ppermute | solution.py:294
  22.7 0.0 collective-permute-done.3.first
  22.7 0.0 copy-done
  22.7 1.5 %shard_map.42 = (f32[576,128]{1,0:T(8,128)}, f32[576,128]{1,0:T(8,128)}, f32[64,128]{1,0:T(8,128)}) custom-call(s32[1]{0:T(128)} %bitcast.flag, f32[108,128]{1,0:T(8,128)S(1)} %get-tuple-element.10.own.refs_1_, f32[108,128]{1,0:T(8,128)S(1)} %collective-permute-done.3.first, f32[108,128]{1,0:T(8,128)S(1)} %collective-permute-done.4.second, ...), custom_call_target="tpu_custom_call" | custom-call | tf_op jit(solution)/shard_map/pallas_call | solution.py:362
  24.2 7.6 %all-to-all-start = ((f32[64,1,128]{2,1,0:T(1,128)}), f32[64,1,128]{2,1,0:T(1,128)S(1)}, u32[]{:S(2)}, u32[]{:S(2)}) async-start(f32[64,1,128]{2,1,0:T(1,128)} %bitcast.7), calls=%async_computation | async-start | bytes 65536 | tf_op jit(solution)/shard_map/all_to_all | solution.py:367
  31.8 0.0 copy-start.1
  31.8 1.0 %copy-done.1 = f32[576,128]{1,0:T(8,128)S(1)} copy-done((f32[576,128]{1,0:T(8,128)S(1)}, f32[576,128]{1,0:T(8,128)}, u32[]{:S(2)}) %copy-start.1) | copy-done | bytes 294936
  32.7 0.0 copy-start.2
  32.7 1.0 %copy-done.2 = f32[576,128]{1,0:T(8,128)S(1)} copy-done((f32[576,128]{1,0:T(8,128)S(1)}, f32[576,128]{1,0:T(8,128)}, u32[]{:S(2)}) %copy-start.2) | copy-done | bytes 294936
  33.7 2.5 %shard_map.43.early = f32[2,6,64,128]{3,2,1,0:T(8,128)S(1)} custom-call(s32[1]{0:T(128)} %bitcast.flag, f32[6,384,128]{2,1,0:T(8,128)S(1)} %bitcast.14, f32[2,384,128]{2,1,0:T(8,128)} %collective-permute-done.5.first.h1, f32[2,384,128]{2,1,0:T(8,128)} %collective-permute-done.6.second.h2, f32[576,128]{1,0:T(8,128)S(1)} %copy-done.1, f32[576,128]{1,0:T(8,128)S(1)} %copy-done.2), custom_call_target="tpu_custom_call" | custom-call | flops 10000000000 | tf_op jit(solution)/shard_map/pallas_call | solution.py:368
  36.2 6.3 %collective-permute-done.8.h2 = f32[4,384,128]{2,1,0:T(8,128)S(1)} collective-permute-done((f32[4,384,128]{2,1,0:T(8,128)S(1)}, f32[4,384,128]{2,1,0:T(8,128)S(1)}, u32[]{:S(2)}, u32[]{:S(2)}) %collective-permute-start.8) | collective-permute-done | bytes 786464 | tf_op jit(solution)/shard_map/ppermute | solution.py:294
  42.4 0.0 collective-permute-done.7.h1
  42.4 3.2 %shard_map.45.late = f32[4,6,64,128]{3,2,1,0:T(8,128)S(1)} custom-call(s32[1]{0:T(128)} %bitcast.flag, f32[6,384,128]{2,1,0:T(8,128)S(1)} %bitcast.15, f32[4,384,128]{2,1,0:T(8,128)} %collective-permute-done.7.h1, f32[4,384,128]{2,1,0:T(8,128)S(1)} %collective-permute-done.8.h2, f32[576,128]{1,0:T(8,128)S(1)} %copy-done.1, f32[576,128]{1,0:T(8,128)S(1)} %copy-done.2), custom_call_target="tpu_custom_call" | custom-call | tf_op jit(solution)/shard_map/pallas_call | solution.py:381
  45.6 0.0 all-to-all-done
  45.6 1.3 %shard_map.46 = f32[6,6,64,128]{3,2,1,0:T(8,128)} custom-call(f32[64,128]{1,0:T(8,128)S(1)} %bitcast.19, f32[360,128]{1,0:T(8,128)S(1)} %get-tuple-element.11.fields, f32[2,6,64,128]{3,2,1,0:T(8,128)S(1)} %shard_map.43.early, f32[4,6,64,128]{3,2,1,0:T(8,128)S(1)} %shard_map.45.late), custom_call_target="tpu_custom_call" | custom-call | tf_op jit(solution)/shard_map/pallas_call | solution.py:393
  (3 shorter events, 0.0 us)
Async XLA Ops:
  0.0 11.1 %copy-start.3 = (f32[1,10,6,6,128]{4,0,3,2,1:T(1,128)S(1)}, f32[1,10,6,6,128]{4,0,3,2,1:T(1,128)}, u32[]{:S(2)}) copy-start(f32[1,10,6,6,128]{4,0,3,2,1:T(1,128)} %param.4) | copy-start | bytes 552964
  0.0 12.4 %collective-permute-start.1 = (f32[360,128]{1,0:T(8,128)}, f32[360,128]{1,0:T(8,128)S(1)}, u32[]{:S(2)}, u32[]{:S(2)}) collective-permute-start(f32[360,128]{1,0:T(8,128)} %bitcast.16), channel_id=1, source_target_pairs={{0,2},{1,3},{2,0},{3,1},{4,6},{5,7},{6,4},{7,5},{8,10},{9,11},{10,... | collective-permute-start | bytes 552968 | tf_op jit(solution)/shard_map/ppermute | solution.py:294
  3.1 17.4 %collective-permute-start.6 = (f32[2,384,128]{2,1,0:T(8,128)S(1)}, f32[2,384,128]{2,1,0:T(8,128)}, u32[]{:S(2)}, u32[]{:S(2)}) collective-permute-start(f32[2,384,128]{2,1,0:T(8,128)S(1)} %shard_map.40), channel_id=1, source_target_pairs={{0,252},{4,8},{8,4},{12,16},{16,12},{20,24},{24,20},{28,32},{32,28... | collective-permute-start | bytes 1179656 | tf_op jit(solution)/shard_map/ppermute | solution.py:294
  11.1 10.8 %collective-permute-start.5 = (f32[2,384,128]{2,1,0:T(8,128)S(1)}, f32[2,384,128]{2,1,0:T(8,128)}, u32[]{:S(2)}, u32[]{:S(2)}) collective-permute-start(f32[2,384,128]{2,1,0:T(8,128)S(1)} %shard_map.40), channel_id=1, source_target_pairs={{0,4},{4,0},{8,12},{12,8},{16,20},{20,16},{24,28},{28,24},{32,36},... | collective-permute-start | bytes 1179656 | tf_op jit(solution)/shard_map/ppermute | solution.py:294
  11.1 2.5 %collective-permute-start = (f32[360,128]{1,0:T(8,128)S(1)}, f32[360,128]{1,0:T(8,128)S(1)}, u32[]{:S(2)}, u32[]{:S(2)}) collective-permute-start(f32[360,128]{1,0:T(8,128)S(1)} %bitcast.17), channel_id=1, source_target_pairs={{0,1},{1,0},{2,3},{3,2},{4,5},{5,4},{6,7},{7,6},{8,9},{9,8},{10,11... | collective-permute-start | bytes 552968 | tf_op jit(solution)/shard_map/ppermute | solution.py:294
  12.4 1.6 %collective-permute-start.2 = (f32[360,128]{1,0:T(8,128)S(1)}, f32[360,128]{1,0:T(8,128)S(1)}, u32[]{:S(2)}, u32[]{:S(2)}) collective-permute-start(f32[360,128]{1,0:T(8,128)S(1)} %shard_map.38.far), channel_id=1, source_target_pairs={{0,1},{1,0},{2,3},{3,2},{4,5},{5,4},{6,7},{7,6},{8,9},{9,8},{10,11... | collective-permute-start | bytes 552968 | tf_op jit(solution)/shard_map/ppermute | solution.py:294
  14.2 8.5 %collective-permute-start.4 = (f32[108,128]{1,0:T(8,128)S(1)}, f32[108,128]{1,0:T(8,128)S(1)}, u32[]{:S(2)}, u32[]{:S(2)}) collective-permute-start(f32[108,128]{1,0:T(8,128)S(1)} %get-tuple-element.10.own.refs_1_), channel_id=1, source_target_pairs={{0,252},{4,8},{8,4},{12,16},{16,12},{20,24},{24,20},{28,32},{32,28... | collective-permute-start | bytes 165896 | tf_op jit(solution)/shard_map/ppermute | solution.py:294
  18.5 4.2 %collective-permute-start.3 = (f32[108,128]{1,0:T(8,128)S(1)}, f32[108,128]{1,0:T(8,128)S(1)}, u32[]{:S(2)}, u32[]{:S(2)}) collective-permute-start(f32[108,128]{1,0:T(8,128)S(1)} %get-tuple-element.10.own.refs_1_), channel_id=1, source_target_pairs={{0,4},{4,0},{8,12},{12,8},{16,20},{20,16},{24,28},{28,24},{32,36},... | collective-permute-start | bytes 165896 | tf_op jit(solution)/shard_map/ppermute | solution.py:294
  18.5 4.2 %copy-start = (f32[64,6,6,128]{3,0,2,1:T(8,128)S(1)}, f32[64,6,6,128]{3,0,2,1:T(8,128)}, u32[]{:S(2)}) copy-start(f32[64,6,6,128]{3,0,2,1:T(8,128)} %param.3) | copy-start | bytes 3538948
  18.5 23.9 %collective-permute-start.8 = (f32[4,384,128]{2,1,0:T(8,128)S(1)}, f32[4,384,128]{2,1,0:T(8,128)S(1)}, u32[]{:S(2)}, u32[]{:S(2)}) collective-permute-start(f32[4,384,128]{2,1,0:T(8,128)S(1)} %shard_map.44), channel_id=1, source_target_pairs={{0,252},{4,8},{8,4},{12,16},{16,12},{20,24},{24,20},{28,32},{32,28... | collective-permute-start | bytes 2359304 | tf_op jit(solution)/shard_map/ppermute | solution.py:294
  20.5 21.9 %collective-permute-start.7 = (f32[4,384,128]{2,1,0:T(8,128)S(1)}, f32[4,384,128]{2,1,0:T(8,128)}, u32[]{:S(2)}, u32[]{:S(2)}) collective-permute-start(f32[4,384,128]{2,1,0:T(8,128)S(1)} %shard_map.44), channel_id=1, source_target_pairs={{0,4},{4,0},{8,12},{12,8},{16,20},{20,16},{24,28},{28,24},{32,36},... | collective-permute-start | bytes 2359304 | tf_op jit(solution)/shard_map/ppermute | solution.py:294
  24.2 21.4 %all-to-all-start = ((f32[64,1,128]{2,1,0:T(1,128)}), f32[64,1,128]{2,1,0:T(1,128)S(1)}, u32[]{:S(2)}, u32[]{:S(2)}) async-start(f32[64,1,128]{2,1,0:T(1,128)} %bitcast.7), calls=%async_computation | async-start | bytes 65536 | tf_op jit(solution)/shard_map/all_to_all | solution.py:367
  31.8 1.0 %copy-start.1 = (f32[576,128]{1,0:T(8,128)S(1)}, f32[576,128]{1,0:T(8,128)}, u32[]{:S(2)}) copy-start(f32[576,128]{1,0:T(8,128)} %get-tuple-element.13.wx) | copy-start | bytes 884740
  32.7 1.0 %copy-start.2 = (f32[576,128]{1,0:T(8,128)S(1)}, f32[576,128]{1,0:T(8,128)}, u32[]{:S(2)}) copy-start(f32[576,128]{1,0:T(8,128)} %get-tuple-element.14.wy) | copy-start | bytes 884740

commit v6 on v5

--- a/solution.py
+++ b/solution.py
@@ -12,11 +12,8 @@
 NF = 10
 HALO = 3
 WIDE = CX + 2 * HALO
-CHUNKS = (2, 0)
-KA_FLOPS = 10000000000
-KB_FLOPS = 0
-MERGE_FLOPS = 0
-HEAD = 112
+EARLY = 2
+EARLY_WORK = 10_000_000_000
 F32 = jnp.float32
 VMEM_LIMIT = 10 * 1024 * 1024
 
@@ -215,22 +212,27 @@
     for l in range(late):
         copy(l).start()
 
-    def ready_side(left, right, first, last, l):
-        sweeps(done + l, (left.at[l], tracers.at[done + l], right.at[l]), first, last, wx, wy, middle.at[l], None)
-
-    def other_side(left, right, first, last, l):
-        copy(l).wait()
-        sweeps(done + l, (left.at[l], tracers.at[done + l], right.at[l]), first, last, wx, wy, middle.at[l], third.at[l])
+    def both_sides(left, right, ready, other):
+        def level(l, first, last_sweep):
+            columns = (left.at[l], tracers.at[done + l], right.at[l])
+            sweeps(done + l, columns, first, first + CX, wx, wy, middle.at[l], last_sweep)
+
+        @pl.loop(0, late)
+        def _(l):
+            level(l, ready, None)
+
+        @pl.loop(0, late)
+        def _(l):
+            copy(l).wait()
+            level(l, other, third.at[l])
 
     @pl.when(flag[0] == 1)
     def _():
-        pl.loop(0, late)(functools.partial(ready_side, s1, h2, CX, WIDE))
-        pl.loop(0, late)(functools.partial(other_side, s1, h2, 0, CX))
+        both_sides(s1, h2, CX, 0)
 
     @pl.when(flag[0] == 0)
     def _():
-        pl.loop(0, late)(functools.partial(ready_side, h2, s1, 0, CX))
-        pl.loop(0, late)(functools.partial(other_side, h2, s1, CX, WIDE))
+        both_sides(h2, s1, 0, CX)
 
 
 def mix_kernel(received, fields, early, late, out, scaled, sems):
@@ -310,8 +312,7 @@
     count = state.shape[2]
     raw = hour_fields.reshape(NF * ROWS, NY)
 
-    a_levels, c_levels = CHUNKS
-    early, late = a_levels + c_levels, LEV - a_levels - c_levels
+    early, late = EARLY, LEV - EARLY
     flat = state.reshape(LEV, CX * count, NY)
 
     def other_core(value):
@@ -319,22 +320,12 @@
 
     far = swap(raw, "tracers", lambda i, n: i ^ 2)
     near = other_core(raw)
-    def other_core(value):
-        return swap(value, "tracers", lambda i, n: i ^ 1)
-
-    far = swap(raw, "tracers", lambda i, n: i ^ 2)
-    near = other_core(raw)
-    def split(start, levels, *after):
-        kernel = functools.partial(split_kernel, start)
-        shape = (levels, CX * count, NY)
-        return call(kernel, [ANY] * (1 + len(after)), [shape], [ANY], [pltpu.SemaphoreType.DMA((levels,))])(in_hbm(flat), *after)[0]
-
     chunk = call(
         functools.partial(split_kernel, 0),
         [ANY],
-        [(a_levels, CX * count, NY)],
+        [(early, CX * count, NY)],
         [ANY],
-        [pltpu.SemaphoreType.DMA((a_levels,))],
+        [pltpu.SemaphoreType.DMA((early,))],
     )(in_hbm(flat))[0]
     a1 = swap(chunk, "cells", even_pairs)
     a2 = swap(chunk, "cells", odd_pairs)
@@ -349,7 +340,7 @@
     across = other_core(far)
     differ = reader_table ^ mine.astype(jnp.int32)
     core_differs, chip_differs = differ & 1, differ >> 1
-    fields, message = call(merge_kernel, [SMEM] * 2 + [VMEM] * 4, [(NF * ROWS, NY), (3 * ROWS, NY)], cost=work(MERGE_FLOPS))(
+    fields, message = call(merge_kernel, [SMEM] * 2 + [VMEM] * 4, [(NF * ROWS, NY), (3 * ROWS, NY)])(
         core_differs, chip_differs, raw, near, far, across
     )
     c1 = swap(message, "cells", even_pairs)
@@ -376,7 +367,7 @@
             pltpu.VMEM((WIDE, count, NY), F32),
             pltpu.SemaphoreType.DMA((early, 2)),
         ],
-        cost=work(KA_FLOPS),
+        cost=work(EARLY_WORK),
     )(odd, flat, in_hbm(a1), in_hbm(a2), wx, wy)[0]
     rest_third = call(
         functools.partial(late_kernel, early),
@@ -388,7 +379,6 @@
             pltpu.VMEM((late, WIDE, count, NY), F32),
             pltpu.SemaphoreType.DMA((late,)),
         ],
-        cost=work(KB_FLOPS),
     )(odd, flat, in_hbm(b1), in_vmem(b2), wx, wy)[0]
     out = call(
         mix_kernel,

time: 47.2 us -> 47.2 us (level)
  no operation moved by 1% of the time
where the time goes in v6:
time: 47.2 us; the launch traced here: 46.9 us
  starting transfers between devices  24.7 us (52%)
  Pallas kernels  10.8 us (23%)
  waiting for transfers between devices  8.74 us (19%)
  local copies, waits for them, and re-layouts  1.93 us (4%)
  between operations  0.75 us (2%)
    ppermute x9, starting transfers between devices, swap(): return lax.ppermute(value, axis, [(i, partner(i, n)) for i in range(n)])  17.1 us
    ppermute x9, waiting for transfers between devices, swap(): return lax.ppermute(value, axis, [(i, partner(i, n)) for i in range(n)])  8.73 us
    all_to_all x1, starting transfers between devices, per_device(): received = lax.all_to_all(masses, 'cells', 0, 0, tiled=True)  7.58 us
    pallas_call x1, Pallas kernels, per_device(): call(functools.partial(late_kernel, early), [SMEM, VMEM, ANY, VMEM, VMEM,...  3.18 us
    pallas_call x1, Pallas kernels, per_device(): call(early_kernel, [SMEM, VMEM, ANY, ANY, VMEM, VMEM], [(early, CX, count...  2.46 us
    unnamed x8, local copies, waits for them, and re-layouts  1.93 us
    pallas_call x1, Pallas kernels, per_device(): call(weights_kernel, [SMEM, VMEM, VMEM, VMEM, VMEM, VMEM, ANY], [pltpu.HB...  1.5 us
    pallas_call x1, Pallas kernels, per_device(): call(mix_kernel, [VMEM] * 4, [(LEV, CX, count, NY)], [HBM], [pltpu.VMEM((...  1.31 us
  transfers between devices with their start and end apart: 10, of which 4 were waited for; matrix products, arithmetic and copies ran while one was open for 0% of the time, Pallas kernels for 20%

profile of v6, /device:TPU:16, one launch (start us, length us, event | category | flops | bytes accessed | tf_op | source)
XLA Modules:
  0.0 46.9 jit_solution(14695248297965539636)
XLA Ops:
  0.0 0.0 copy-start.3
  0.0 2.1 %collective-permute-start.1 = (f32[360,128]{1,0:T(8,128)}, f32[360,128]{1,0:T(8,128)S(1)}, u32[]{:S(2)}, u32[]{:S(2)}) collective-permute-start(f32[360,128]{1,0:T(8,128)} %bitcast.16), channel_id=1, source_target_pairs={{0,2},{1,3},{2,0},{3,1},{4,6},{5,7},{6,4},{7,5},{8,10},{9,11},{10,... | collective-permute-start | bytes 552968 | tf_op jit(solution)/shard_map/ppermute | solution.py:296
  2.1 1.0 %shard_map.40 = f32[2,384,128]{2,1,0:T(8,128)S(1)} custom-call(f32[6,384,128]{2,1,0:T(8,128)} %bitcast.11), custom_call_target="tpu_custom_call" | custom-call | tf_op jit(solution)/shard_map/pallas_call | solution.py:323
  3.1 8.0 %collective-permute-start.6 = (f32[2,384,128]{2,1,0:T(8,128)S(1)}, f32[2,384,128]{2,1,0:T(8,128)}, u32[]{:S(2)}, u32[]{:S(2)}) collective-permute-start(f32[2,384,128]{2,1,0:T(8,128)S(1)} %shard_map.40), channel_id=1, source_target_pairs={{0,252},{4,8},{8,4},{12,16},{16,12},{20,24},{24,20},{28,32},{32,28... | collective-permute-start | bytes 1179656 | tf_op jit(solution)/shard_map/ppermute | solution.py:296
  11.1 0.0 collective-permute-start.5
  11.1 0.0 copy-done.3
  11.1 0.0 collective-permute-start
  11.2 1.3 %shard_map.37.refs_1_.refs_0_ = f32[4,384,128]{2,1,0:T(8,128)S(1)} custom-call(f32[6,384,128]{2,1,0:T(8,128)} %bitcast.12), custom_call_target="tpu_custom_call" | custom-call | tf_op jit(solution)/shard_map/pallas_call | solution.py:332
  12.4 0.0 collective-permute-done.1.refs_0_
  12.4 0.6 %collective-permute-start.2 = (f32[360,128]{1,0:T(8,128)S(1)}, f32[360,128]{1,0:T(8,128)S(1)}, u32[]{:S(2)}, u32[]{:S(2)}) collective-permute-start(f32[360,128]{1,0:T(8,128)S(1)} %shard_map.38.far), channel_id=1, source_target_pairs={{0,1},{1,0},{2,3},{3,2},{4,5},{5,4},{6,7},{7,6},{8,9},{9,8},{10,11... | collective-permute-start | bytes 552968 | tf_op jit(solution)/shard_map/ppermute | solution.py:296
  13.7 0.0 collective-permute-done.near
  13.7 0.4 collective-permute-done.2.across
  14.1 0.1 shard_map.39
  14.2 4.3 %collective-permute-start.4 = (f32[108,128]{1,0:T(8,128)S(1)}, f32[108,128]{1,0:T(8,128)S(1)}, u32[]{:S(2)}, u32[]{:S(2)}) collective-permute-start(f32[108,128]{1,0:T(8,128)S(1)} %get-tuple-element.10.own.refs_1_), channel_id=1, source_target_pairs={{0,252},{4,8},{8,4},{12,16},{16,12},{20,24},{24,20},{28,32},{32,28... | collective-permute-start | bytes 165896 | tf_op jit(solution)/shard_map/ppermute | solution.py:296
  18.5 0.0 collective-permute-start.3
  18.5 0.0 copy-start
  18.5 2.0 %collective-permute-start.8 = (f32[4,384,128]{2,1,0:T(8,128)S(1)}, f32[4,384,128]{2,1,0:T(8,128)S(1)}, u32[]{:S(2)}, u32[]{:S(2)}) collective-permute-start(f32[4,384,128]{2,1,0:T(8,128)S(1)} %shard_map.44), channel_id=1, source_target_pairs={{0,252},{4,8},{8,4},{12,16},{16,12},{20,24},{24,20},{28,32},{32,28... | collective-permute-start | bytes 2359304 | tf_op jit(solution)/shard_map/ppermute | solution.py:296
  20.5 0.0 collective-permute-done.6.second.h2
  20.5 0.1 collective-permute-start.7
  20.6 1.4 %collective-permute-done.5.first.h1 = f32[2,384,128]{2,1,0:T(8,128)} collective-permute-done((f32[2,384,128]{2,1,0:T(8,128)S(1)}, f32[2,384,128]{2,1,0:T(8,128)}, u32[]{:S(2)}, u32[]{:S(2)}) %collective-permute-start.5) | collective-permute-done | bytes 393248 | tf_op jit(solution)/shard_map/ppermute | solution.py:296
  22.0 0.7 %collective-permute-done.4.second = f32[108,128]{1,0:T(8,128)S(1)} collective-permute-done((f32[108,128]{1,0:T(8,128)S(1)}, f32[108,128]{1,0:T(8,128)S(1)}, u32[]{:S(2)}, u32[]{:S(2)}) %collective-permute-start.4) | collective-permute-done | bytes 55328 | tf_op jit(solution)/shard_map/ppermute | solution.py:296
  22.7 0.0 collective-permute-done.3.first
  22.7 0.0 copy-done
  22.7 1.5 %shard_map.42 = (f32[576,128]{1,0:T(8,128)}, f32[576,128]{1,0:T(8,128)}, f32[64,128]{1,0:T(8,128)}) custom-call(s32[1]{0:T(128)} %bitcast.flag, f32[108,128]{1,0:T(8,128)S(1)} %get-tuple-element.10.own.refs_1_, f32[108,128]{1,0:T(8,128)S(1)} %collective-permute-done.3.first, f32[108,128]{1,0:T(8,128)S(1)} %collective-permute-done.4.second, ...), custom_call_target="tpu_custom_call" | custom-call | tf_op jit(solution)/shard_map/pallas_call | solution.py:353
  24.2 7.6 %all-to-all-start = ((f32[64,1,128]{2,1,0:T(1,128)}), f32[64,1,128]{2,1,0:T(1,128)S(1)}, u32[]{:S(2)}, u32[]{:S(2)}) async-start(f32[64,1,128]{2,1,0:T(1,128)} %bitcast.7), calls=%async_computation | async-start | bytes 65536 | tf_op jit(solution)/shard_map/all_to_all | solution.py:358
  31.8 0.0 copy-start.1
  31.8 1.0 %copy-done.1 = f32[576,128]{1,0:T(8,128)S(1)} copy-done((f32[576,128]{1,0:T(8,128)S(1)}, f32[576,128]{1,0:T(8,128)}, u32[]{:S(2)}) %copy-start.1) | copy-done | bytes 294936
  32.7 0.0 copy-start.2
  32.7 1.0 %copy-done.2 = f32[576,128]{1,0:T(8,128)S(1)} copy-done((f32[576,128]{1,0:T(8,128)S(1)}, f32[576,128]{1,0:T(8,128)}, u32[]{:S(2)}) %copy-start.2) | copy-done | bytes 294936
  33.7 2.5 %shard_map.43.early = f32[2,6,64,128]{3,2,1,0:T(8,128)S(1)} custom-call(s32[1]{0:T(128)} %bitcast.flag, f32[6,384,128]{2,1,0:T(8,128)S(1)} %bitcast.14, f32[2,384,128]{2,1,0:T(8,128)} %collective-permute-done.5.first.h1, f32[2,384,128]{2,1,0:T(8,128)} %collective-permute-done.6.second.h2, f32[576,128]{1,0:T(8,128)S(1)} %copy-done.1, f32[576,128]{1,0:T(8,128)S(1)} %copy-done.2), custom_call_target="tpu_custom_call" | custom-call | flops 10000000000 | tf_op jit(solution)/shard_map/pallas_call | solution.py:359
  36.2 6.3 %collective-permute-done.8.h2 = f32[4,384,128]{2,1,0:T(8,128)S(1)} collective-permute-done((f32[4,384,128]{2,1,0:T(8,128)S(1)}, f32[4,384,128]{2,1,0:T(8,128)S(1)}, u32[]{:S(2)}, u32[]{:S(2)}) %collective-permute-start.8) | collective-permute-done | bytes 786464 | tf_op jit(solution)/shard_map/ppermute | solution.py:296
  42.4 0.0 collective-permute-done.7.h1
  42.4 3.2 %shard_map.45.late = f32[4,6,64,128]{3,2,1,0:T(8,128)S(1)} custom-call(s32[1]{0:T(128)} %bitcast.flag, f32[6,384,128]{2,1,0:T(8,128)S(1)} %bitcast.15, f32[4,384,128]{2,1,0:T(8,128)} %collective-permute-done.7.h1, f32[4,384,128]{2,1,0:T(8,128)S(1)} %collective-permute-done.8.h2, f32[576,128]{1,0:T(8,128)S(1)} %copy-done.1, f32[576,128]{1,0:T(8,128)S(1)} %copy-done.2), custom_call_target="tpu_custom_call" | custom-call | tf_op jit(solution)/shard_map/pallas_call | solution.py:372
  45.6 0.0 all-to-all-done
  45.6 1.3 %shard_map.46 = f32[6,6,64,128]{3,2,1,0:T(8,128)} custom-call(f32[64,128]{1,0:T(8,128)S(1)} %bitcast.19, f32[360,128]{1,0:T(8,128)S(1)} %get-tuple-element.11.fields, f32[2,6,64,128]{3,2,1,0:T(8,128)S(1)} %shard_map.43.early, f32[4,6,64,128]{3,2,1,0:T(8,128)S(1)} %shard_map.45.late), custom_call_target="tpu_custom_call" | custom-call | tf_op jit(solution)/shard_map/pallas_call | solution.py:383
  (3 shorter events, 0.0 us)
Async XLA Ops:
  0.0 11.1 %copy-start.3 = (f32[1,10,6,6,128]{4,0,3,2,1:T(1,128)S(1)}, f32[1,10,6,6,128]{4,0,3,2,1:T(1,128)}, u32[]{:S(2)}) copy-start(f32[1,10,6,6,128]{4,0,3,2,1:T(1,128)} %param.4) | copy-start | bytes 552964
  0.0 12.4 %collective-permute-start.1 = (f32[360,128]{1,0:T(8,128)}, f32[360,128]{1,0:T(8,128)S(1)}, u32[]{:S(2)}, u32[]{:S(2)}) collective-permute-start(f32[360,128]{1,0:T(8,128)} %bitcast.16), channel_id=1, source_target_pairs={{0,2},{1,3},{2,0},{3,1},{4,6},{5,7},{6,4},{7,5},{8,10},{9,11},{10,... | collective-permute-start | bytes 552968 | tf_op jit(solution)/shard_map/ppermute | solution.py:296
  3.1 17.4 %collective-permute-start.6 = (f32[2,384,128]{2,1,0:T(8,128)S(1)}, f32[2,384,128]{2,1,0:T(8,128)}, u32[]{:S(2)}, u32[]{:S(2)}) collective-permute-start(f32[2,384,128]{2,1,0:T(8,128)S(1)} %shard_map.40), channel_id=1, source_target_pairs={{0,252},{4,8},{8,4},{12,16},{16,12},{20,24},{24,20},{28,32},{32,28... | collective-permute-start | bytes 1179656 | tf_op jit(solution)/shard_map/ppermute | solution.py:296
  11.1 10.8 %collective-permute-start.5 = (f32[2,384,128]{2,1,0:T(8,128)S(1)}, f32[2,384,128]{2,1,0:T(8,128)}, u32[]{:S(2)}, u32[]{:S(2)}) collective-permute-start(f32[2,384,128]{2,1,0:T(8,128)S(1)} %shard_map.40), channel_id=1, source_target_pairs={{0,4},{4,0},{8,12},{12,8},{16,20},{20,16},{24,28},{28,24},{32,36},... | collective-permute-start | bytes 1179656 | tf_op jit(solution)/shard_map/ppermute | solution.py:296
  11.1 2.5 %collective-permute-start = (f32[360,128]{1,0:T(8,128)S(1)}, f32[360,128]{1,0:T(8,128)S(1)}, u32[]{:S(2)}, u32[]{:S(2)}) collective-permute-start(f32[360,128]{1,0:T(8,128)S(1)} %bitcast.17), channel_id=1, source_target_pairs={{0,1},{1,0},{2,3},{3,2},{4,5},{5,4},{6,7},{7,6},{8,9},{9,8},{10,11... | collective-permute-start | bytes 552968 | tf_op jit(solution)/shard_map/ppermute | solution.py:296
  12.4 1.6 %collective-permute-start.2 = (f32[360,128]{1,0:T(8,128)S(1)}, f32[360,128]{1,0:T(8,128)S(1)}, u32[]{:S(2)}, u32[]{:S(2)}) collective-permute-start(f32[360,128]{1,0:T(8,128)S(1)} %shard_map.38.far), channel_id=1, source_target_pairs={{0,1},{1,0},{2,3},{3,2},{4,5},{5,4},{6,7},{7,6},{8,9},{9,8},{10,11... | collective-permute-start | bytes 552968 | tf_op jit(solution)/shard_map/ppermute | solution.py:296
  14.2 8.5 %collective-permute-start.4 = (f32[108,128]{1,0:T(8,128)S(1)}, f32[108,128]{1,0:T(8,128)S(1)}, u32[]{:S(2)}, u32[]{:S(2)}) collective-permute-start(f32[108,128]{1,0:T(8,128)S(1)} %get-tuple-element.10.own.refs_1_), channel_id=1, source_target_pairs={{0,252},{4,8},{8,4},{12,16},{16,12},{20,24},{24,20},{28,32},{32,28... | collective-permute-start | bytes 165896 | tf_op jit(solution)/shard_map/ppermute | solution.py:296
  18.5 4.2 %collective-permute-start.3 = (f32[108,128]{1,0:T(8,128)S(1)}, f32[108,128]{1,0:T(8,128)S(1)}, u32[]{:S(2)}, u32[]{:S(2)}) collective-permute-start(f32[108,128]{1,0:T(8,128)S(1)} %get-tuple-element.10.own.refs_1_), channel_id=1, source_target_pairs={{0,4},{4,0},{8,12},{12,8},{16,20},{20,16},{24,28},{28,24},{32,36},... | collective-permute-start | bytes 165896 | tf_op jit(solution)/shard_map/ppermute | solution.py:296
  18.5 4.2 %copy-start = (f32[64,6,6,128]{3,0,2,1:T(8,128)S(1)}, f32[64,6,6,128]{3,0,2,1:T(8,128)}, u32[]{:S(2)}) copy-start(f32[64,6,6,128]{3,0,2,1:T(8,128)} %param.3) | copy-start | bytes 3538948
  18.5 23.9 %collective-permute-start.8 = (f32[4,384,128]{2,1,0:T(8,128)S(1)}, f32[4,384,128]{2,1,0:T(8,128)S(1)}, u32[]{:S(2)}, u32[]{:S(2)}) collective-permute-start(f32[4,384,128]{2,1,0:T(8,128)S(1)} %shard_map.44), channel_id=1, source_target_pairs={{0,252},{4,8},{8,4},{12,16},{16,12},{20,24},{24,20},{28,32},{32,28... | collective-permute-start | bytes 2359304 | tf_op jit(solution)/shard_map/ppermute | solution.py:296
  20.5 21.9 %collective-permute-start.7 = (f32[4,384,128]{2,1,0:T(8,128)S(1)}, f32[4,384,128]{2,1,0:T(8,128)}, u32[]{:S(2)}, u32[]{:S(2)}) collective-permute-start(f32[4,384,128]{2,1,0:T(8,128)S(1)} %shard_map.44), channel_id=1, source_target_pairs={{0,4},{4,0},{8,12},{12,8},{16,20},{20,16},{24,28},{28,24},{32,36},... | collective-permute-start | bytes 2359304 | tf_op jit(solution)/shard_map/ppermute | solution.py:296
  24.2 21.4 %all-to-all-start = ((f32[64,1,128]{2,1,0:T(1,128)}), f32[64,1,128]{2,1,0:T(1,128)S(1)}, u32[]{:S(2)}, u32[]{:S(2)}) async-start(f32[64,1,128]{2,1,0:T(1,128)} %bitcast.7), calls=%async_computation | async-start | bytes 65536 | tf_op jit(solution)/shard_map/all_to_all | solution.py:358
  31.8 1.0 %copy-start.1 = (f32[576,128]{1,0:T(8,128)S(1)}, f32[576,128]{1,0:T(8,128)}, u32[]{:S(2)}) copy-start(f32[576,128]{1,0:T(8,128)} %get-tuple-element.13.wx) | copy-start | bytes 884740
  32.7 1.0 %copy-start.2 = (f32[576,128]{1,0:T(8,128)S(1)}, f32[576,128]{1,0:T(8,128)}, u32[]{:S(2)}) copy-start(f32[576,128]{1,0:T(8,128)} %get-tuple-element.14.wy) | copy-start | bytes 884740

commit v7 on v6

--- a/solution.py
+++ b/solution.py
@@ -84,7 +84,8 @@
     core, chip = core_differs[0] == 0, chip_differs[0] == 0
     here = jnp.where(core, own[...], near[...])
     there = jnp.where(core, far[...], across[...])
-    fields[...] = jnp.where(chip, here, there)
+    fields[pl.ds(0, NF * ROWS), :] = jnp.where(chip, here, there)
+    message[pl.ds(3 * ROWS - 4, 8), :] = jnp.zeros((8, NY), F32)
     for x in range(CX):
         for f in range(2):
             message[pl.ds(f * ROWS + x * LEV, LEV), :] = fields[pl.ds(f * ROWS + x, LEV, stride=CX), :]
@@ -340,7 +341,7 @@
     across = other_core(far)
     differ = reader_table ^ mine.astype(jnp.int32)
     core_differs, chip_differs = differ & 1, differ >> 1
-    fields, message = call(merge_kernel, [SMEM] * 2 + [VMEM] * 4, [(NF * ROWS, NY), (3 * ROWS, NY)])(
+    fields, message = call(merge_kernel, [SMEM] * 2 + [VMEM] * 4, [(NF * ROWS + 16, NY), (3 * ROWS + 4, NY)])(
         core_differs, chip_differs, raw, near, far, across
     )
     c1 = swap(message, "cells", even_pairs)
@@ -353,7 +354,7 @@
     wx, wy, masses = call(
         weights_kernel,
         [SMEM, VMEM, VMEM, VMEM, VMEM, VMEM, ANY],
-        [pltpu.HBM((LEV * WIDE * 8, NY), F32), pltpu.HBM((LEV * WIDE * 8, NY), F32), (n, 2 * count)],
+        [pltpu.HBM((8 * WIDE * 8, NY), F32), pltpu.HBM((8 * WIDE * 8, NY), F32), (n, 2 * count)],
     )(odd, message, c1, c2, fields, state, token)
     received = lax.all_to_all(masses, "cells", 0, 0, tiled=True)
     third = call(

time: 47.2 us -> 47.2 us (level)
  no operation moved by 1% of the time
where the time goes in v7:
time: 47.2 us; the launch traced here: 47 us
  starting transfers between devices  24.7 us (52%)
  Pallas kernels  10.9 us (23%)
  waiting for transfers between devices  8.65 us (18%)
  local copies, waits for them, and re-layouts  1.99 us (4%)
  between operations  0.75 us (2%)
    ppermute x9, starting transfers between devices, swap(): return lax.ppermute(value, axis, [(i, partner(i, n)) for i in range(n)])  17.1 us
    ppermute x9, waiting for transfers between devices, swap(): return lax.ppermute(value, axis, [(i, partner(i, n)) for i in range(n)])  8.65 us
    all_to_all x1, starting transfers between devices, per_device(): received = lax.all_to_all(masses, 'cells', 0, 0, tiled=True)  7.58 us
    pallas_call x1, Pallas kernels, per_device(): call(functools.partial(late_kernel, early), [SMEM, VMEM, ANY, VMEM, VMEM,...  3.21 us
    pallas_call x1, Pallas kernels, per_device(): call(early_kernel, [SMEM, VMEM, ANY, ANY, VMEM, VMEM], [(early, CX, count...  2.48 us
    unnamed x8, local copies, waits for them, and re-layouts  1.99 us
    pallas_call x1, Pallas kernels, per_device(): call(weights_kernel, [SMEM, VMEM, VMEM, VMEM, VMEM, VMEM, ANY], [pltpu.HB...  1.5 us
    pallas_call x1, Pallas kernels, per_device(): call(mix_kernel, [VMEM] * 4, [(LEV, CX, count, NY)], [HBM], [pltpu.VMEM((...  1.31 us
  transfers between devices with their start and end apart: 10, of which 4 were waited for; matrix products, arithmetic and copies ran while one was open for 0% of the time, Pallas kernels for 20%

profile of v7, /device:TPU:16, one launch (start us, length us, event | category | flops | bytes accessed | tf_op | source)
XLA Modules:
  0.0 47.0 jit_solution(14681895214110021170)
XLA Ops:
  0.0 0.0 copy-start.3
  0.0 2.1 %collective-permute-start.1 = (f32[360,128]{1,0:T(8,128)}, f32[360,128]{1,0:T(8,128)S(1)}, u32[]{:S(2)}, u32[]{:S(2)}) collective-permute-start(f32[360,128]{1,0:T(8,128)} %bitcast.16), channel_id=1, source_target_pairs={{0,2},{1,3},{2,0},{3,1},{4,6},{5,7},{6,4},{7,5},{8,10},{9,11},{10,... | collective-permute-start | bytes 552968 | tf_op jit(solution)/shard_map/ppermute | solution.py:297
  2.1 1.0 %shard_map.40 = f32[2,384,128]{2,1,0:T(8,128)S(1)} custom-call(f32[6,384,128]{2,1,0:T(8,128)} %bitcast.11), custom_call_target="tpu_custom_call" | custom-call | tf_op jit(solution)/shard_map/pallas_call | solution.py:324
  3.1 8.0 %collective-permute-start.6 = (f32[2,384,128]{2,1,0:T(8,128)S(1)}, f32[2,384,128]{2,1,0:T(8,128)}, u32[]{:S(2)}, u32[]{:S(2)}) collective-permute-start(f32[2,384,128]{2,1,0:T(8,128)S(1)} %shard_map.40), channel_id=1, source_target_pairs={{0,252},{4,8},{8,4},{12,16},{16,12},{20,24},{24,20},{28,32},{32,28... | collective-permute-start | bytes 1179656 | tf_op jit(solution)/shard_map/ppermute | solution.py:297
  11.1 0.0 collective-permute-start.5
  11.1 0.0 copy-done.3
  11.1 0.0 collective-permute-start
  11.2 1.3 %shard_map.37.refs_1_.refs_0_ = f32[4,384,128]{2,1,0:T(8,128)S(1)} custom-call(f32[6,384,128]{2,1,0:T(8,128)} %bitcast.12), custom_call_target="tpu_custom_call" | custom-call | tf_op jit(solution)/shard_map/pallas_call | solution.py:333
  12.4 0.0 collective-permute-done.1.refs_0_
  12.4 0.6 %collective-permute-start.2 = (f32[360,128]{1,0:T(8,128)S(1)}, f32[360,128]{1,0:T(8,128)S(1)}, u32[]{:S(2)}, u32[]{:S(2)}) collective-permute-start(f32[360,128]{1,0:T(8,128)S(1)} %shard_map.38.far), channel_id=1, source_target_pairs={{0,1},{1,0},{2,3},{3,2},{4,5},{5,4},{6,7},{7,6},{8,9},{9,8},{10,11... | collective-permute-start | bytes 552968 | tf_op jit(solution)/shard_map/ppermute | solution.py:297
  13.7 0.0 collective-permute-done.near
  13.7 0.4 collective-permute-done.2.across
  14.1 0.1 shard_map.39
  14.2 4.3 %collective-permute-start.4 = (f32[112,128]{1,0:T(8,128)S(1)}, f32[112,128]{1,0:T(8,128)S(1)}, u32[]{:S(2)}, u32[]{:S(2)}) collective-permute-start(f32[112,128]{1,0:T(8,128)S(1)} %get-tuple-element.10.own.refs_1_), channel_id=1, source_target_pairs={{0,252},{4,8},{8,4},{12,16},{16,12},{20,24},{24,20},{28,32},{32,28... | collective-permute-start | bytes 172040 | tf_op jit(solution)/shard_map/ppermute | solution.py:297
  18.5 0.0 collective-permute-start.3
  18.5 0.0 copy-start
  18.5 2.0 %collective-permute-start.8 = (f32[4,384,128]{2,1,0:T(8,128)S(1)}, f32[4,384,128]{2,1,0:T(8,128)S(1)}, u32[]{:S(2)}, u32[]{:S(2)}) collective-permute-start(f32[4,384,128]{2,1,0:T(8,128)S(1)} %shard_map.44), channel_id=1, source_target_pairs={{0,252},{4,8},{8,4},{12,16},{16,12},{20,24},{24,20},{28,32},{32,28... | collective-permute-start | bytes 2359304 | tf_op jit(solution)/shard_map/ppermute | solution.py:297
  20.5 0.0 collective-permute-done.6.second.h2
  20.5 0.1 collective-permute-start.7
  20.6 1.4 %collective-permute-done.5.first.h1 = f32[2,384,128]{2,1,0:T(8,128)} collective-permute-done((f32[2,384,128]{2,1,0:T(8,128)S(1)}, f32[2,384,128]{2,1,0:T(8,128)}, u32[]{:S(2)}, u32[]{:S(2)}) %collective-permute-start.5) | collective-permute-done | bytes 393248 | tf_op jit(solution)/shard_map/ppermute | solution.py:297
  22.0 0.7 %collective-permute-done.4.second = f32[112,128]{1,0:T(8,128)S(1)} collective-permute-done((f32[112,128]{1,0:T(8,128)S(1)}, f32[112,128]{1,0:T(8,128)S(1)}, u32[]{:S(2)}, u32[]{:S(2)}) %collective-permute-start.4) | collective-permute-done | bytes 57376 | tf_op jit(solution)/shard_map/ppermute | solution.py:297
  22.7 0.0 collective-permute-done.3.first
  22.7 0.0 copy-done
  22.7 1.5 %shard_map.42 = (f32[768,128]{1,0:T(8,128)}, f32[768,128]{1,0:T(8,128)}, f32[64,128]{1,0:T(8,128)}) custom-call(s32[1]{0:T(128)} %bitcast.flag, f32[112,128]{1,0:T(8,128)S(1)} %get-tuple-element.10.own.refs_1_, f32[112,128]{1,0:T(8,128)S(1)} %collective-permute-done.3.first, f32[112,128]{1,0:T(8,128)S(1)} %collective-permute-done.4.second, ...), custom_call_target="tpu_custom_call" | custom-call | tf_op jit(solution)/shard_map/pallas_call | solution.py:354
  24.2 7.6 %all-to-all-start = ((f32[64,1,128]{2,1,0:T(1,128)}), f32[64,1,128]{2,1,0:T(1,128)S(1)}, u32[]{:S(2)}, u32[]{:S(2)}) async-start(f32[64,1,128]{2,1,0:T(1,128)} %bitcast.7), calls=%async_computation | async-start | bytes 65536 | tf_op jit(solution)/shard_map/all_to_all | solution.py:359
  31.8 0.0 copy-start.1
  31.8 1.0 %copy-done.1 = f32[768,128]{1,0:T(8,128)S(1)} copy-done((f32[768,128]{1,0:T(8,128)S(1)}, f32[768,128]{1,0:T(8,128)}, u32[]{:S(2)}) %copy-start.1) | copy-done | bytes 393240
  32.8 0.0 copy-start.2
  32.8 1.0 %copy-done.2 = f32[768,128]{1,0:T(8,128)S(1)} copy-done((f32[768,128]{1,0:T(8,128)S(1)}, f32[768,128]{1,0:T(8,128)}, u32[]{:S(2)}) %copy-start.2) | copy-done | bytes 393240
  33.8 2.5 %shard_map.43.early = f32[2,6,64,128]{3,2,1,0:T(8,128)S(1)} custom-call(s32[1]{0:T(128)} %bitcast.flag, f32[6,384,128]{2,1,0:T(8,128)S(1)} %bitcast.14, f32[2,384,128]{2,1,0:T(8,128)} %collective-permute-done.5.first.h1, f32[2,384,128]{2,1,0:T(8,128)} %collective-permute-done.6.second.h2, f32[768,128]{1,0:T(8,128)S(1)} %copy-done.1, f32[768,128]{1,0:T(8,128)S(1)} %copy-done.2), custom_call_target="tpu_custom_call" | custom-call | flops 10000000000 | tf_op jit(solution)/shard_map/pallas_call | solution.py:360
  36.3 6.2 %collective-permute-done.8.h2 = f32[4,384,128]{2,1,0:T(8,128)S(1)} collective-permute-done((f32[4,384,128]{2,1,0:T(8,128)S(1)}, f32[4,384,128]{2,1,0:T(8,128)S(1)}, u32[]{:S(2)}, u32[]{:S(2)}) %collective-permute-start.8) | collective-permute-done | bytes 786464 | tf_op jit(solution)/shard_map/ppermute | solution.py:297
  42.4 0.0 collective-permute-done.7.h1
  42.4 3.2 %shard_map.45.late = f32[4,6,64,128]{3,2,1,0:T(8,128)S(1)} custom-call(s32[1]{0:T(128)} %bitcast.flag, f32[6,384,128]{2,1,0:T(8,128)S(1)} %bitcast.15, f32[4,384,128]{2,1,0:T(8,128)} %collective-permute-done.7.h1, f32[4,384,128]{2,1,0:T(8,128)S(1)} %collective-permute-done.8.h2, f32[768,128]{1,0:T(8,128)S(1)} %copy-done.1, f32[768,128]{1,0:T(8,128)S(1)} %copy-done.2), custom_call_target="tpu_custom_call" | custom-call | tf_op jit(solution)/shard_map/pallas_call | solution.py:373
  45.7 0.0 all-to-all-done
  45.7 1.3 %shard_map.46 = f32[6,6,64,128]{3,2,1,0:T(8,128)} custom-call(f32[64,128]{1,0:T(8,128)S(1)} %bitcast.19, f32[376,128]{1,0:T(8,128)S(1)} %get-tuple-element.11.fields, f32[2,6,64,128]{3,2,1,0:T(8,128)S(1)} %shard_map.43.early, f32[4,6,64,128]{3,2,1,0:T(8,128)S(1)} %shard_map.45.late), custom_call_target="tpu_custom_call" | custom-call | tf_op jit(solution)/shard_map/pallas_call | solution.py:384
  (3 shorter events, 0.0 us)
Async XLA Ops:
  0.0 11.1 %copy-start.3 = (f32[1,10,6,6,128]{4,0,3,2,1:T(1,128)S(1)}, f32[1,10,6,6,128]{4,0,3,2,1:T(1,128)}, u32[]{:S(2)}) copy-start(f32[1,10,6,6,128]{4,0,3,2,1:T(1,128)} %param.4) | copy-start | bytes 552964
  0.0 12.4 %collective-permute-start.1 = (f32[360,128]{1,0:T(8,128)}, f32[360,128]{1,0:T(8,128)S(1)}, u32[]{:S(2)}, u32[]{:S(2)}) collective-permute-start(f32[360,128]{1,0:T(8,128)} %bitcast.16), channel_id=1, source_target_pairs={{0,2},{1,3},{2,0},{3,1},{4,6},{5,7},{6,4},{7,5},{8,10},{9,11},{10,... | collective-permute-start | bytes 552968 | tf_op jit(solution)/shard_map/ppermute | solution.py:297
  3.1 17.4 %collective-permute-start.6 = (f32[2,384,128]{2,1,0:T(8,128)S(1)}, f32[2,384,128]{2,1,0:T(8,128)}, u32[]{:S(2)}, u32[]{:S(2)}) collective-permute-start(f32[2,384,128]{2,1,0:T(8,128)S(1)} %shard_map.40), channel_id=1, source_target_pairs={{0,252},{4,8},{8,4},{12,16},{16,12},{20,24},{24,20},{28,32},{32,28... | collective-permute-start | bytes 1179656 | tf_op jit(solution)/shard_map/ppermute | solution.py:297
  11.1 10.8 %collective-permute-start.5 = (f32[2,384,128]{2,1,0:T(8,128)S(1)}, f32[2,384,128]{2,1,0:T(8,128)}, u32[]{:S(2)}, u32[]{:S(2)}) collective-permute-start(f32[2,384,128]{2,1,0:T(8,128)S(1)} %shard_map.40), channel_id=1, source_target_pairs={{0,4},{4,0},{8,12},{12,8},{16,20},{20,16},{24,28},{28,24},{32,36},... | collective-permute-start | bytes 1179656 | tf_op jit(solution)/shard_map/ppermute | solution.py:297
  11.1 2.5 %collective-permute-start = (f32[360,128]{1,0:T(8,128)S(1)}, f32[360,128]{1,0:T(8,128)S(1)}, u32[]{:S(2)}, u32[]{:S(2)}) collective-permute-start(f32[360,128]{1,0:T(8,128)S(1)} %bitcast.17), channel_id=1, source_target_pairs={{0,1},{1,0},{2,3},{3,2},{4,5},{5,4},{6,7},{7,6},{8,9},{9,8},{10,11... | collective-permute-start | bytes 552968 | tf_op jit(solution)/shard_map/ppermute | solution.py:297
  12.4 1.6 %collective-permute-start.2 = (f32[360,128]{1,0:T(8,128)S(1)}, f32[360,128]{1,0:T(8,128)S(1)}, u32[]{:S(2)}, u32[]{:S(2)}) collective-permute-start(f32[360,128]{1,0:T(8,128)S(1)} %shard_map.38.far), channel_id=1, source_target_pairs={{0,1},{1,0},{2,3},{3,2},{4,5},{5,4},{6,7},{7,6},{8,9},{9,8},{10,11... | collective-permute-start | bytes 552968 | tf_op jit(solution)/shard_map/ppermute | solution.py:297
  14.2 8.5 %collective-permute-start.4 = (f32[112,128]{1,0:T(8,128)S(1)}, f32[112,128]{1,0:T(8,128)S(1)}, u32[]{:S(2)}, u32[]{:S(2)}) collective-permute-start(f32[112,128]{1,0:T(8,128)S(1)} %get-tuple-element.10.own.refs_1_), channel_id=1, source_target_pairs={{0,252},{4,8},{8,4},{12,16},{16,12},{20,24},{24,20},{28,32},{32,28... | collective-permute-start | bytes 172040 | tf_op jit(solution)/shard_map/ppermute | solution.py:297
  18.5 4.2 %collective-permute-start.3 = (f32[112,128]{1,0:T(8,128)S(1)}, f32[112,128]{1,0:T(8,128)S(1)}, u32[]{:S(2)}, u32[]{:S(2)}) collective-permute-start(f32[112,128]{1,0:T(8,128)S(1)} %get-tuple-element.10.own.refs_1_), channel_id=1, source_target_pairs={{0,4},{4,0},{8,12},{12,8},{16,20},{20,16},{24,28},{28,24},{32,36},... | collective-permute-start | bytes 172040 | tf_op jit(solution)/shard_map/ppermute | solution.py:297
  18.5 4.2 %copy-start = (f32[64,6,6,128]{3,0,2,1:T(8,128)S(1)}, f32[64,6,6,128]{3,0,2,1:T(8,128)}, u32[]{:S(2)}) copy-start(f32[64,6,6,128]{3,0,2,1:T(8,128)} %param.3) | copy-start | bytes 3538948
  18.5 23.9 %collective-permute-start.8 = (f32[4,384,128]{2,1,0:T(8,128)S(1)}, f32[4,384,128]{2,1,0:T(8,128)S(1)}, u32[]{:S(2)}, u32[]{:S(2)}) collective-permute-start(f32[4,384,128]{2,1,0:T(8,128)S(1)} %shard_map.44), channel_id=1, source_target_pairs={{0,252},{4,8},{8,4},{12,16},{16,12},{20,24},{24,20},{28,32},{32,28... | collective-permute-start | bytes 2359304 | tf_op jit(solution)/shard_map/ppermute | solution.py:297
  20.5 21.9 %collective-permute-start.7 = (f32[4,384,128]{2,1,0:T(8,128)S(1)}, f32[4,384,128]{2,1,0:T(8,128)}, u32[]{:S(2)}, u32[]{:S(2)}) collective-permute-start(f32[4,384,128]{2,1,0:T(8,128)S(1)} %shard_map.44), channel_id=1, source_target_pairs={{0,4},{4,0},{8,12},{12,8},{16,20},{20,16},{24,28},{28,24},{32,36},... | collective-permute-start | bytes 2359304 | tf_op jit(solution)/shard_map/ppermute | solution.py:297
  24.2 21.5 %all-to-all-start = ((f32[64,1,128]{2,1,0:T(1,128)}), f32[64,1,128]{2,1,0:T(1,128)S(1)}, u32[]{:S(2)}, u32[]{:S(2)}) async-start(f32[64,1,128]{2,1,0:T(1,128)} %bitcast.7), calls=%async_computation | async-start | bytes 65536 | tf_op jit(solution)/shard_map/all_to_all | solution.py:359
  31.8 1.0 %copy-start.1 = (f32[768,128]{1,0:T(8,128)S(1)}, f32[768,128]{1,0:T(8,128)}, u32[]{:S(2)}) copy-start(f32[768,128]{1,0:T(8,128)} %get-tuple-element.13.wx) | copy-start | bytes 1179652
  32.8 1.0 %copy-start.2 = (f32[768,128]{1,0:T(8,128)S(1)}, f32[768,128]{1,0:T(8,128)}, u32[]{:S(2)}) copy-start(f32[768,128]{1,0:T(8,128)} %get-tuple-element.14.wy) | copy-start | bytes 1179652
